TPU v7x, 128 devices: a whole 4x4x4 slice. The times are simulated.
128 devices in a mesh: dp: 32 (over y, z, core), tensor: 4 (over x).
Axes of the slice: x: 4, y: 4, z: 4, core: 2. Of those that a mesh axis runs over, the one named last changes fastest.
Arguments:
- queries: bfloat16 [4096, 4096], P('dp', 'tensor'), may hold values from -5 to 5
- rotated_key_rows: bfloat16 [4096, 512], P('dp', 'tensor'), may hold values from -5 to 5
- value_matrix: bfloat16 [4096, 512], P('dp', 'tensor'), may hold values from -4 to 4
- residual: bfloat16 [4096, 4096], P('dp', 'tensor'), may hold values from -10.5 to 10.5
- lengths: int32 [64, 4], replicated, may hold values from 1 to 32, 64 in all within a row
- move_plan: int32 [64], replicated, may hold values from 0 to 31, as said below
- out_weight: bfloat16 [4096, 4096], P('tensor', 'dp'), may hold values from -0.09375 to 0.09375
- norm_gain: float32 [4096], P('tensor'), may hold values from 0.1 to 1.9
- routes: int32 [4096, 8], P('dp'), may hold values from 0 to 63, as said below
- bin_slots: int32 [4096, 8], P('dp'), may hold values from 0 to 15, as said below
- dropped: int32 [4096, 8], P('dp'), may hold values from 0 to 1, as said below
- route_weight: float32 [4096, 8], P('dp'), may hold values from 0.05 to 0.4
- gate_weight: bfloat16 [64, 4096, 1536], P('dp', None, 'tensor'), may hold values from -0.09375 to 0.09375
- up_weight: bfloat16 [64, 4096, 1536], P('dp', None, 'tensor'), may hold values from -0.09375 to 0.09375
- down_weight: bfloat16 [64, 1536, 4096], P('dp', 'tensor'), may hold values from -0.15625 to 0.15625
Outputs:
- stream: bfloat16 [4096, 4096], P('dp', 'tensor')
- expert_mix: bfloat16 [4096, 4096], P('dp', 'tensor')
Inputs may be any that keep to these rules, and one draw needn't show every extreme that they name: `lengths`: each row sums to 64; the largest entry of every row is exactly 32. Pack p goes to index move_plan[p] of dp. For each s, the packs with p % 2 = s go to different indices, and the 2 packs of one index go to different indices. `routes`: each row names 8 different experts. `bin_slots`: among the entries of the rows of one index of dp that are kept for one expert, the slots are different. 1 marks a dropped entry. The rows of one index of dp keep at most 16 entries for any expert; in every draw one expert keeps exactly 16 entries from every index, and on every index some expert is named by more than 16 entries.
All inputs are finite; a program needn't handle non-finite values.
Results may differ from a plain program's by a relative error of at most 0.03.
Values may be sent and summed in bfloat16 or wider, within the bound.
No kernel may reach another device: no remote copies, remote signals or barrier semaphores. Data moves between devices by JAX's collectives and lax.ppermute only.
A program may use at most 128 MiB of HBM per device.

v0:
```python
import jax
import jax.numpy as jnp
from jax import lax
from jax.experimental import pallas as pl
from jax.experimental.pallas import tpu as pltpu
from jax.sharding import Mesh, PartitionSpec as P

D = 4096
HEAD_WIDTH = 128
PACK_ROWS = 64
QUERY_PER_KEY = 8
DP = ("y", "z", "core")
ROWS = 128
CAP = 16
BINS = 32 * CAP
PART = 1024
F32 = jnp.float32
BF16 = jnp.bfloat16

RIGHT = [(i, (i + 1) % 4) for i in range(4)]
LEFT = [(i, (i - 1) % 4) for i in range(4)]


def iota(shape, dim):
    return lax.broadcasted_iota(jnp.int32, shape, dim)


def whole(memory_space=pltpu.VMEM):
    return pl.BlockSpec(memory_space=memory_space)


def params(megabytes):
    return pltpu.CompilerParams(vmem_limit_bytes=megabytes << 20)


def after(values, *done):
    count = len(values)
    return pl.pallas_call(
        lambda *refs: None,
        out_shape=[jax.ShapeDtypeStruct(v.shape, v.dtype) for v in values],
        in_specs=[whole(pl.ANY)] * (count + len(done)),
        out_specs=[whole(pl.ANY)] * count,
        input_output_aliases={i: i for i in range(count)},
        name="after",
    )(*values, *done)


def attend_kernel(
    index, lengths, queries_in, keys_in, values_in, residual_in, out, queries, keys, values, residual, sems
):
    pairs = ((queries_in, queries), (keys_in, keys), (values_in, values), (residual_in, residual))
    copies = [pltpu.make_async_copy(a, b, sems.at[i]) for i, (a, b) in enumerate(pairs)]
    for copy in copies:
        copy.start()
    first = 2 * index[0]
    position = iota((ROWS, ROWS), 0)
    other = iota((ROWS, ROWS), 1)

    def label(at):
        second = at >= PACK_ROWS
        inner = jnp.where(second, at - PACK_ROWS, at)
        found = jnp.where(second, 8, 0)
        ends = [jnp.int32(0), jnp.int32(0)]
        for doc in range(4):
            for s in range(2):
                ends[s] = ends[s] + lengths[doc, first + s]
            found = found + (inner >= jnp.where(second, ends[1], ends[0])).astype(jnp.int32)
        return found

    hidden = jnp.where((label(position) == label(other)) & (position >= other), 0.0, -1e30)
    for copy in copies:
        copy.wait()
    lanes = [slice(h * HEAD_WIDTH, (h + 1) * HEAD_WIDTH) for h in range(QUERY_PER_KEY)]
    stacked = jnp.concatenate([queries[:, part] for part in lanes], axis=0)
    scores = lax.dot_general(
        stacked, keys[...], (((1,), (1,)), ((), ())), preferred_element_type=F32
    ).reshape(QUERY_PER_KEY, ROWS, ROWS)
    masked = jnp.where(hidden[None] < 0.0, -1e30, scores * HEAD_WIDTH**-0.5)
    exps = jnp.exp(masked - jnp.max(masked, axis=2, keepdims=True))
    probs = (exps / jnp.sum(exps, axis=2, keepdims=True)).astype(BF16)
    heads = jnp.dot(
        probs.reshape(QUERY_PER_KEY * ROWS, ROWS), values[...], preferred_element_type=F32
    )
    attended = jnp.concatenate(
        [heads[h * ROWS : (h + 1) * ROWS] for h in range(QUERY_PER_KEY)], axis=1
    )
    rest = residual[...].astype(F32)

    def group(rows, at):
        low = rows[at * 8 : at * 8 + 8]
        high = rows[PACK_ROWS + at * 8 : PACK_ROWS + at * 8 + 8]
        return jnp.concatenate([low, high], axis=0).astype(BF16)

    for y in range(4):
        for core in range(2):
            mine = group(attended, y * 2 + core)
            plain = group(rest, y * 2 + core)
            for z in range(4):
                out[y, z, core, :, :PART] = mine
                out[y, z, core, :, PART:] = plain[:, z * 256 : z * 256 + 256]


def route_kernel(plan, base, own, one, two, out, placed):
    total = own[...] + one[...].astype(F32) + two[...].astype(F32)
    merged = (base[...].astype(F32) + total).astype(BF16).astype(F32)
    for source in range(32):
        for s in range(2):
            rows = merged[source * 16 + s * 8 : source * 16 + s * 8 + 8]
            placed[plan[source * 2 + s], s * 8 : s * 8 + 8, :] = rows
    out[...] = placed[...].astype(BF16)


def stream_kernel(landed, table, stream, bins):
    parts = []
    for z in range(4):
        tiles = [landed[y, z, core].astype(F32) for y in range(4) for core in range(2)]
        parts.append(
            jnp.concatenate([t[s * 8 : s * 8 + 8] for s in range(2) for t in tiles], axis=0)
        )
    rows = jnp.concatenate(parts, axis=1).astype(BF16)
    stream[...] = rows
    bins[...] = jnp.dot(table[...], rows, preferred_element_type=F32).astype(BF16)


def tables_kernel(
    routes_t, slots_t, dropped_t, routes, slots, dropped, weight, send0, send1, mix0, mix1
):
    def target(named, slot, drop):
        return jnp.where(drop == 0, (named // 2) * CAP + slot, -1), named % 2

    across, side = target(routes_t[...], slots_t[...], dropped_t[...])
    row = iota((BINS, ROWS), 0)
    for local, out in enumerate((send0, send1)):
        mine = jnp.where(side == local, across, -1)
        total = jnp.zeros((BINS, ROWS), F32)
        for k in range(8):
            total = total + jnp.where(mine[k : k + 1] == row, 1.0, 0.0)
        out[...] = total.astype(BF16)
    down, side = target(routes[...], slots[...], dropped[...])
    column = iota((ROWS, BINS), 1)
    for local, out in enumerate((mix0, mix1)):
        mine = jnp.where(side == local, down, -1)
        total = jnp.zeros((ROWS, BINS), F32)
        for k in range(8):
            total = total + jnp.where(mine[:, k : k + 1] == column, weight[:, k : k + 1], 0.0)
        out[...] = total.astype(BF16)


def expert_kernel(
    index, own, right, left, top, low, gain, gate_w, up_w, down_w,
    far_top, far_low, right_top, right_low, left_top, left_low, own_out,
    rows, gate, up, squares, hidden, sems,
):
    step = pl.program_id(0)
    half = BINS // 2
    copies = [
        pltpu.make_async_copy(own, rows.at[0], sems.at[0]),
        pltpu.make_async_copy(right, rows.at[1], sems.at[1]),
        pltpu.make_async_copy(left, rows.at[2], sems.at[2]),
        pltpu.make_async_copy(top, rows.at[3, pl.ds(0, half)], sems.at[3]),
        pltpu.make_async_copy(low, rows.at[3, pl.ds(half, half)], sems.at[4]),
    ]

    @pl.when(step == 0)
    def _():
        for copy in copies:
            copy.start()
        gate[...] = jnp.zeros_like(gate)
        up[...] = jnp.zeros_like(up)
        squares[...] = jnp.zeros_like(squares)
        copies[0].wait()

    @pl.when(step == 1)
    def _():
        copies[1].wait()

    @pl.when(step == 2)
    def _():
        copies[2].wait()

    @pl.when(step == 3)
    def _():
        copies[3].wait()
        copies[4].wait()

    @pl.when(step < 4)
    def _():
        wide = rows[step].astype(F32)
        squares[...] += jnp.sum(wide * wide, axis=1, keepdims=True)
        scaled = (wide * gain[...]).astype(BF16)
        gate[...] += jnp.dot(scaled, gate_w[...], preferred_element_type=F32)
        up[...] += jnp.dot(scaled, up_w[...], preferred_element_type=F32)

    @pl.when(step == 3)
    def _():
        norm = lax.rsqrt(squares[...] * (1.0 / D) + 1e-6)
        gated = gate[...] * norm
        hidden[...] = (gated / (1.0 + jnp.exp(-gated)) * (up[...] * norm)).astype(BF16)

    @pl.when(step >= 4)
    def _():
        product = jnp.dot(hidden[...], down_w[...], preferred_element_type=F32).astype(BF16)

        @pl.when(step == 4)
        def _():
            far_top[...] = product[:half]
            far_low[...] = product[half:]

        @pl.when(step == 5)
        def _():
            left_top[...] = product[:half]
            left_low[...] = product[half:]

        @pl.when(step == 6)
        def _():
            right_top[...] = product[:half]
            right_low[...] = product[half:]

        @pl.when(step == 7)
        def _():
            own_out[...] = product


def ring_distance(step):
    return step ^ (step >> 1)


def run_expert(x, local, blocks, gains, gate_weight, up_weight, down_weight):
    def up_place(i, at):
        return (local, (at[0] + ring_distance(jnp.minimum(i, 3))) % 4, 0)

    def down_place(i, at):
        return (local, 0, (at[0] + ring_distance(7 - jnp.maximum(i, 4))) % 4)

    half = jax.ShapeDtypeStruct((BINS // 2, PART), BF16)
    grid = pltpu.PrefetchScalarGridSpec(
        num_scalar_prefetch=1,
        grid=(8,),
        in_specs=[whole(pl.ANY)] * 5
        + [
            pl.BlockSpec((None, 1, PART), lambda i, at: (jnp.minimum(i, 3), 0, 0)),
            pl.BlockSpec((None, PART, 384), up_place),
            pl.BlockSpec((None, PART, 384), up_place),
            pl.BlockSpec((None, 384, PART), down_place),
        ],
        out_specs=[pl.BlockSpec((BINS // 2, PART), lambda i, at: (0, 0))] * 6
        + [pl.BlockSpec((BINS, PART), lambda i, at: (0, 0))],
        scratch_shapes=[
            pltpu.VMEM((4, BINS, PART), BF16),
            pltpu.VMEM((BINS, 384), F32),
            pltpu.VMEM((BINS, 384), F32),
            pltpu.VMEM((BINS, 1), F32),
            pltpu.VMEM((BINS, 384), BF16),
            pltpu.SemaphoreType.DMA((5,)),
        ],
    )
    return pl.pallas_call(
        expert_kernel,
        grid_spec=grid,
        out_shape=[half] * 6 + [jax.ShapeDtypeStruct((BINS, PART), BF16)],
        compiler_params=params(40),
        cost_estimate=pl.CostEstimate(
            flops=6 * BINS * 4096 * 384, bytes_accessed=18 << 20, transcendentals=BINS * 384
        ),
        name="expert",
    )(x, *blocks, gains, gate_weight, up_weight, down_weight)


def ring_gather(block):
    half = block.shape[0] // 2
    left = lax.ppermute(block, "tensor", RIGHT)
    right = lax.ppermute(block, "tensor", LEFT)
    return (
        right,
        left,
        lax.ppermute(left[:half], "tensor", RIGHT),
        lax.ppermute(right[half:], "tensor", LEFT),
    )


def ring_scatter(far_top, far_low, right_top, right_low, left_top, left_low, plain_done=(), sum_done=()):
    if plain_done:
        far_top, far_low = after((far_top, far_low), *plain_done)
        right_low, left_top = after((right_low, left_top), *sum_done)
    top = lax.ppermute(far_top, "tensor", RIGHT)
    low = lax.ppermute(far_low, "tensor", LEFT)
    from_left_low = lax.ppermute(right_low, "tensor", RIGHT)
    from_right_top = lax.ppermute(left_top, "tensor", LEFT)
    right_sum = (right_top.astype(F32) + top.astype(F32)).astype(BF16)
    left_sum = (left_low.astype(F32) + low.astype(F32)).astype(BF16)
    from_left_top = lax.ppermute(right_sum, "tensor", RIGHT)
    from_right_low = lax.ppermute(left_sum, "tensor", LEFT)
    return from_left_top, from_left_low, from_right_top, from_right_low


def per_device(
    queries,
    rotated_key_rows,
    value_matrix,
    residual,
    lengths,
    move_plan,
    out_weight,
    norm_gain,
    routes,
    bin_slots,
    dropped,
    route_weight,
    gate_weight,
    up_weight,
    down_weight,
):
    x = lax.axis_index("tensor")
    d = lax.axis_index(DP)
    x_ref = jnp.reshape(x, (1,)).astype(jnp.int32)

    weight = lax.all_gather(out_weight, ("y", "core"), axis=1, tiled=True)

    sent = pl.pallas_call(
        attend_kernel,
        out_shape=jax.ShapeDtypeStruct((4, 4, 2, 16, PART + 256), BF16),
        in_specs=[whole(pltpu.SMEM)] * 2 + [whole(pl.ANY)] * 4,
        out_specs=whole(),
        scratch_shapes=[
            pltpu.VMEM((ROWS, PART), BF16),
            pltpu.VMEM((ROWS, HEAD_WIDTH), BF16),
            pltpu.VMEM((ROWS, HEAD_WIDTH), BF16),
            pltpu.VMEM((ROWS, PART), BF16),
            pltpu.SemaphoreType.DMA((4,)),
        ],
        compiler_params=params(24),
        name="attend",
    )(jnp.reshape(d, (1,)).astype(jnp.int32), lengths.T, queries, rotated_key_rows, value_matrix, residual)
    spread = lax.all_to_all(sent.reshape(32, 16, PART + 256), DP, 0, 0, tiled=True)
    spread = spread.reshape(512, PART + 256)

    send0, send1, mix0, mix1 = pl.pallas_call(
        tables_kernel,
        out_shape=[jax.ShapeDtypeStruct((BINS, ROWS), BF16)] * 2
        + [jax.ShapeDtypeStruct((ROWS, BINS), BF16)] * 2,
        in_specs=[whole()] * 7,
        out_specs=[whole()] * 4,
        compiler_params=params(24),
        name="tables",
    )(routes.T, bin_slots.T, dropped.T, routes, bin_slots, dropped, route_weight)
    own_gain = norm_gain.reshape(8, 128)
    right_gain, left_gain, top_gain, low_gain = ring_gather(own_gain)
    far_gain = jnp.concatenate([top_gain, low_gain], axis=0)
    gains = jnp.stack([own_gain, right_gain, left_gain, far_gain], axis=0).reshape(4, 1, PART)

    tokens = spread[:, :PART]

    def project(distance):
        columns = lax.dynamic_slice_in_dim(weight, ((x + distance) % 4) * 256, 256, axis=1)
        return jnp.dot(tokens, columns, preferred_element_type=F32)

    far = project(2).astype(BF16)
    right = project(1).astype(BF16)
    left = project(3).astype(BF16)
    a, b, c, e = ring_scatter(far[:256], far[256:], right[:256], right[256:], left[:256], left[256:])
    onward = pl.pallas_call(
        route_kernel,
        out_shape=jax.ShapeDtypeStruct((32, 16, 256), BF16),
        in_specs=[whole(pltpu.SMEM)] + [whole()] * 4,
        out_specs=whole(),
        scratch_shapes=[pltpu.VMEM((32, 16, 256), F32)],
        compiler_params=params(24),
        name="route",
    )(
        move_plan,
        spread[:, PART:],
        project(0),
        jnp.concatenate([a, b], axis=0),
        jnp.concatenate([c, e], axis=0),
    )
    landed = lax.all_to_all(onward, DP, 0, 0, tiled=True)

    stream, bins0 = pl.pallas_call(
        stream_kernel,
        out_shape=[
            jax.ShapeDtypeStruct((ROWS, PART), BF16),
            jax.ShapeDtypeStruct((BINS, PART), BF16),
        ],
        in_specs=[whole()] * 2,
        out_specs=[whole()] * 2,
        compiler_params=params(24),
        name="stream",
    )(landed.reshape(4, 4, 2, 16, 256), send0)
    bins1 = jnp.dot(send1, stream, preferred_element_type=F32).astype(BF16)

    def exchange(rows):
        return lax.all_to_all(rows.reshape(32, CAP, PART), DP, 0, 0, tiled=True).reshape(BINS, PART)

    held0 = exchange(bins0)
    near0 = ring_gather(held0)
    (held1,) = after((exchange(bins1),), near0[0], near0[1])
    near1 = ring_gather(held1)
    weights = (gate_weight, up_weight, down_weight)
    products0 = run_expert(x_ref, 0, (held0, *near0), gains, *weights)
    sums0 = ring_scatter(*products0[:6])
    products1 = run_expert(x_ref, 1, (held1, *near1), gains, *weights)
    sums1 = ring_scatter(*products1[:6], (sums0[1], sums0[2]), (sums0[0], sums0[3]))

    def total(own, a, b, c, e):
        arrived = jnp.concatenate([a.astype(F32) + c.astype(F32), b.astype(F32) + e.astype(F32)], axis=0)
        return (own.astype(F32) + arrived).astype(BF16)

    back = [exchange(total(products0[6], *sums0)), exchange(total(products1[6], *sums1))]
    mix = jnp.dot(mix0, back[0], preferred_element_type=F32)
    mix = mix + jnp.dot(mix1, back[1], preferred_element_type=F32)
    return (stream, mix.astype(BF16))


def solution(mesh):
    fine = Mesh(mesh.devices.reshape(4, 4, 2, 4), ("y", "z", "core", "tensor"))
    return jax.shard_map(
        per_device,
        mesh=fine,
        in_specs=(
            P(DP, "tensor"),
            P(DP, "tensor"),
            P(DP, "tensor"),
            P(DP, "tensor"),
            P(),
            P(),
            P("tensor", DP),
            P("tensor"),
            P(DP, None),
            P(DP, None),
            P(DP, None),
            P(DP, None),
            P(DP, None, "tensor"),
            P(DP, None, "tensor"),
            P(DP, "tensor", None),
        ),
        out_specs=(P(DP, "tensor"), P(DP, "tensor")),
        check_vma=False,
    )
```

profile of v0, /device:TPU:1, one launch (start us, length us, event | category | flops | bytes accessed | tf_op | source)
XLA Modules:
  0.0 305.5 jit_solution(14280143106610085987)
XLA Ops:
  12.0 2.5 attend.1
  14.5 9.6 %all-to-all-start = ((bf16[32,16,1280]{2,1,0:T(8,128)(2,1)}), bf16[32,16,1280]{2,1,0:T(8,128)(2,1)S(1)}, u32[]{:S(2)}, u32[]{:S(2)}) async-start(bf16[32,16,1280]{2,1,0:T(8,128)(2,1)} %bitcast.2), calls=%async_computation | async-start | bytes 2621440 | tf_op jit(solution)/shard_map/all_to_all | solution.py:334
  24.2 26.0 %all-to-all-done = bf16[32,16,1280]{2,1,0:T(8,128)(2,1)S(1)} async-done(((bf16[32,16,1280]{2,1,0:T(8,128)(2,1)}), bf16[32,16,1280]{2,1,0:T(8,128)(2,1)S(1)}, u32[]{:S(2)}, u32[]{:S(2)}) %all-to-all-start) | async-done | bytes 1310752 | tf_op jit(solution)/shard_map/all_to_all | solution.py:334
  50.2 1.6 convolution_convert_fusion.3
  51.9 1.6 collective-permute-start.2
  54.0 1.3 collective-permute-start.4
  55.8 1.5 collective-permute-start.3
  57.3 1.3 collective-permute-done.4
  58.6 2.8 collective-permute-start.5
  63.8 3.6 %collective-permute-done.1 = bf16[256,256]{1,0:T(8,128)(2,1)S(1)} collective-permute-done((bf16[256,256]{1,0:T(8,128)(2,1)S(1)}, bf16[256,256]{1,0:T(8,128)(2,1)S(1)}, u32[]{:S(2)}, u32[]{:S(2)}) %collective-permute-start.1) | collective-permute-done | bytes 131104 | tf_op jit(solution)/shard_map/ppermute | solution.py:291
  67.5 1.5 route.1
  69.0 9.3 %all-to-all-start.1 = ((bf16[32,16,256]{2,1,0:T(8,128)(2,1)}), bf16[32,16,256]{2,1,0:T(8,128)(2,1)S(1)}, u32[]{:S(2)}, u32[]{:S(2)}) async-start(bf16[32,16,256]{2,1,0:T(8,128)(2,1)} %route.1), calls=%async_computation.1 | async-start | bytes 524288 | tf_op jit(solution)/shard_map/all_to_all | solution.py:376
  78.7 1.9 tables.1
  80.6 6.6 %all-to-all-done.1 = bf16[32,16,256]{2,1,0:T(8,128)(2,1)S(1)} async-done(((bf16[32,16,256]{2,1,0:T(8,128)(2,1)}), bf16[32,16,256]{2,1,0:T(8,128)(2,1)S(1)}, u32[]{:S(2)}, u32[]{:S(2)}) %all-to-all-start.1) | async-done | bytes 262176 | tf_op jit(solution)/shard_map/all_to_all | solution.py:376
  88.0 20.6 %all_to_all.30 = bf16[32,16,1024]{2,1,0:T(8,128)(2,1)} all-to-all(bf16[32,16,1024]{2,1,0:T(8,128)(2,1)S(1)} %bitcast.29), channel_id=1, replica_groups=mesh['y'=4,'z'=4,'core'=2,'tensor'=4] {'y','z','core'}, dimensions={0} | all-to-all | bytes 2097152 | tf_op jit(solution)/shard_map/all_to_all | solution.py:392
  108.6 2.7 collective-permute-start.6
  111.3 1.4 convolution_convert_fusion
  112.7 4.6 %all-to-all-start.4 = ((bf16[32,16,1024]{2,1,0:T(8,128)(2,1)}), bf16[32,16,1024]{2,1,0:T(8,128)(2,1)S(1)}, u32[]{:S(2)}, u32[]{:S(2)}) async-start(bf16[32,16,1024]{2,1,0:T(8,128)(2,1)} %bitcast.35), calls=%async_computation.4 | async-start | bytes 2097152 | tf_op jit(solution)/shard_map/all_to_all | solution.py:392
  117.3 17.3 %collective-permute-done.7.left.refs_2_ = bf16[512,1024]{1,0:T(8,128)(2,1)S(1)} collective-permute-done((bf16[512,1024]{1,0:T(8,128)(2,1)}, bf16[512,1024]{1,0:T(8,128)(2,1)S(1)}, u32[]{:S(2)}, u32[]{:S(2)}) %collective-permute-start.7) | collective-permute-done | bytes 1048608 | tf_op jit(solution)/shard_map/ppermute | solution.py:271
  136.5 2.7 collective-permute-start.9
  139.1 2.7 collective-permute-start.10
  141.8 7.8 %collective-permute-done.11 = f32[8,128]{1,0:T(8,128)S(1)} collective-permute-done((f32[8,128]{1,0:T(8,128)S(1)}, f32[8,128]{1,0:T(8,128)S(1)}, u32[]{:S(2)}, u32[]{:S(2)}) %collective-permute-start.11) | collective-permute-done | bytes 4128 | tf_op jit(solution)/shard_map/ppermute | solution.py:271
  149.7 3.3 %collective-permute-start.13 = (f32[4,128]{1,0:T(4,128)S(1)}, f32[4,128]{1,0:T(4,128)S(1)}, u32[]{:S(2)}, u32[]{:S(2)}) collective-permute-start(f32[4,128]{1,0:T(4,128)S(1)} %slice.53), channel_id=1, source_target_pairs={{0,3},{1,0},{2,1},{3,2},{4,7},{5,4},{6,5},{7,6},{8,11},{9,8},{10,9... | collective-permute-start | bytes 6152 | tf_op jit(solution)/shard_map/ppermute | solution.py:277
  154.6 2.9 collective-permute-start.20
  158.8 1.2 copy-done.5
  160.0 13.7 %expert.2 = (bf16[256,1024]{1,0:T(8,128)(2,1)S(1)}, bf16[256,1024]{1,0:T(8,128)(2,1)S(1)}, bf16[256,1024]{1,0:T(8,128)(2,1)S(1)}, bf16[256,1024]{1,0:T(8,128)(2,...) custom-call(s32[1]{0:T(128)} %bitcast.8.index, ...), custom_call_target="tpu_custom_call" | custom-call | flops 4831838208 | bytes 18874368 | tf_op jit(solution)/shard_map/expert/pallas_call | solution.py:257
  173.9 2.7 collective-permute-start.18
  176.5 1.4 collective-permute-done.21.left
  178.1 2.7 collective-permute-start.23
  180.9 8.3 %collective-permute-done.14 = bf16[256,1024]{1,0:T(8,128)(2,1)S(1)} collective-permute-done((bf16[256,1024]{1,0:T(8,128)(2,1)S(1)}, bf16[256,1024]{1,0:T(8,128)(2,1)S(1)}, u32[]{:S(2)}, u32[]{:S(2)}) %collective-permute-start.14) | collective-permute-done | bytes 524320 | tf_op jit(solution)/shard_map/ppermute | solution.py:285
  189.7 2.7 collective-permute-start.19
  192.5 7.9 %collective-permute-done.22.top = bf16[256,1024]{1,0:T(8,128)(2,1)S(1)} collective-permute-done((bf16[256,1024]{1,0:T(8,128)(2,1)S(1)}, bf16[256,1024]{1,0:T(8,128)(2,1)S(1)}, u32[]{:S(2)}, u32[]{:S(2)}) %collective-permute-start.22) | collective-permute-done | bytes 524320 | tf_op jit(solution)/shard_map/ppermute | solution.py:276
  200.4 11.9 %expert.3 = (bf16[256,1024]{1,0:T(8,128)(2,1)S(1)}, bf16[256,1024]{1,0:T(8,128)(2,1)S(1)}, bf16[256,1024]{1,0:T(8,128)(2,1)S(1)}, bf16[256,1024]{1,0:T(8,128)(2,...) custom-call(s32[1]{0:T(128)} %bitcast.8.index, ...), custom_call_target="tpu_custom_call" | custom-call | flops 4831838208 | bytes 18874368 | tf_op jit(solution)/shard_map/expert/pallas_call | solution.py:257
  215.5 2.7 collective-permute-start.26
  218.2 4.0 %collective-permute-done.16.refs_3_ = bf16[256,1024]{1,0:T(8,128)(2,1)} collective-permute-done((bf16[256,1024]{1,0:T(8,128)(2,1)}, bf16[256,1024]{1,0:T(8,128)(2,1)}, u32[]{:S(2)}, u32[]{:S(2)}) %collective-permute-start.16) | collective-permute-done | bytes 524320 | tf_op jit(solution)/shard_map/ppermute | solution.py:288
  223.6 2.2 collective-permute-start.28
  225.8 1.4 convert_add_fusion.2
  227.2 1.4 convert_add_fusion.3
  228.6 15.9 %collective-permute-done.24 = bf16[256,1024]{1,0:T(8,128)(2,1)S(1)} collective-permute-done((bf16[256,1024]{1,0:T(8,128)(2,1)}, bf16[256,1024]{1,0:T(8,128)(2,1)S(1)}, u32[]{:S(2)}, u32[]{:S(2)}) %collective-permute-start.24) | collective-permute-done | bytes 524320 | tf_op jit(solution)/shard_map/ppermute | solution.py:285
  246.5 2.7 collective-permute-start.29
  249.2 1.4 fusion
  250.6 9.2 %all-to-all-start.3 = ((bf16[32,16,1024]{2,1,0:T(8,128)(2,1)}), bf16[32,16,1024]{2,1,0:T(8,128)(2,1)S(1)}, u32[]{:S(2)}, u32[]{:S(2)}) async-start(bf16[32,16,1024]{2,1,0:T(8,128)(2,1)} %bitcast.16), calls=%async_computation.3 | async-start | bytes 2097152 | tf_op jit(solution)/shard_map/all_to_all | solution.py:392
  259.8 1.4 convert_add_fusion.1
  261.2 1.4 convert_add_fusion
  262.6 1.4 fusion.1
  264.0 12.8 %all-to-all-done.3 = bf16[32,16,1024]{2,1,0:T(8,128)(2,1)S(1)} async-done(((bf16[32,16,1024]{2,1,0:T(8,128)(2,1)}), bf16[32,16,1024]{2,1,0:T(8,128)(2,1)S(1)}, u32[]{:S(2)}, u32[]{:S(2)}) %all-to-all-start.3) | async-done | bytes 1048608 | tf_op jit(solution)/shard_map/all_to_all | solution.py:392
  276.7 4.0 %all-to-all-start.5 = ((bf16[32,16,1024]{2,1,0:T(8,128)(2,1)}), bf16[32,16,1024]{2,1,0:T(8,128)(2,1)S(1)}, u32[]{:S(2)}, u32[]{:S(2)}) async-start(bf16[32,16,1024]{2,1,0:T(8,128)(2,1)} %bitcast.38), calls=%async_computation.5 | async-start | bytes 2097152 | tf_op jit(solution)/shard_map/all_to_all | solution.py:392
  281.0 16.6 %all-to-all-done.5 = bf16[32,16,1024]{2,1,0:T(8,128)(2,1)S(1)} async-done(((bf16[32,16,1024]{2,1,0:T(8,128)(2,1)}), bf16[32,16,1024]{2,1,0:T(8,128)(2,1)S(1)}, u32[]{:S(2)}, u32[]{:S(2)}) %all-to-all-start.5) | async-done | bytes 1048608 | tf_op jit(solution)/shard_map/all_to_all | solution.py:392
  (118 shorter events, 22.8 us)
Async XLA Ops:
  7.2 43.1 %all-gather.2.cloned.1.call-start = ((), (), s32[]{:S(2)}) async-start(), calls=%async_computation.6 | async-start | bytes 2359296 | tf_op jit(solution)/shard_map/all_gather | solution.py:317
  14.5 35.6 %all-to-all-start = ((bf16[32,16,1280]{2,1,0:T(8,128)(2,1)}), bf16[32,16,1280]{2,1,0:T(8,128)(2,1)S(1)}, u32[]{:S(2)}, u32[]{:S(2)}) async-start(bf16[32,16,1280]{2,1,0:T(8,128)(2,1)} %bitcast.2), calls=%async_computation | async-start | bytes 2621440 | tf_op jit(solution)/shard_map/all_to_all | solution.py:334
  50.2 3.3 %copy-start.22 = (bf16[1024,1024]{1,0:T(8,128)(2,1)S(1)}, bf16[1024,1024]{1,0:T(8,128)(2,1)}, u32[]{:S(2)}) copy-start(bf16[1024,1024]{1,0:T(8,128)(2,1)} %all-gather.2.cloned.1.call-done) | copy-start | bytes 6291460
  51.9 11.9 %collective-permute-start.2 = (bf16[256,256]{1,0:T(8,128)(2,1)S(1)}, bf16[256,256]{1,0:T(8,128)(2,1)S(1)}, u32[]{:S(2)}, u32[]{:S(2)}) collective-permute-start(bf16[256,256]{1,0:T(8,128)(2,1)S(1)} %slice.60), channel_id=1, source_target_pairs={{0,1},{1,2},{2,3},{3,0},{4,5},{5,6},{6,7},{7,4},{8,9},{9,10},{10,1... | collective-permute-start | bytes 393224 | tf_op jit(solution)/shard_map/ppermute | solution.py:287
  54.0 4.6 %collective-permute-start.4 = (bf16[256,256]{1,0:T(8,128)(2,1)S(1)}, bf16[256,256]{1,0:T(8,128)(2,1)S(1)}, u32[]{:S(2)}, u32[]{:S(2)}) collective-permute-start(bf16[256,256]{1,0:T(8,128)(2,1)S(1)} %get-tuple-element.50), channel_id=1, source_target_pairs={{0,3},{1,0},{2,1},{3,2},{4,7},{5,4},{6,5},{7,6},{8,11},{9,8},{10,9... | collective-permute-start | bytes 393224 | tf_op jit(solution)/shard_map/ppermute | solution.py:286
  55.8 7.2 %collective-permute-start.3 = (bf16[256,256]{1,0:T(8,128)(2,1)S(1)}, bf16[256,256]{1,0:T(8,128)(2,1)S(1)}, u32[]{:S(2)}, u32[]{:S(2)}) collective-permute-start(bf16[256,256]{1,0:T(8,128)(2,1)S(1)} %slice.61), channel_id=1, source_target_pairs={{0,3},{1,0},{2,1},{3,2},{4,7},{5,4},{6,5},{7,6},{8,11},{9,8},{10,9... | collective-permute-start | bytes 393224 | tf_op jit(solution)/shard_map/ppermute | solution.py:288
  57.3 10.2 %copy-start.18 = (s32[64]{0:T(128)S(1)}, s32[64]{0:T(128)}, u32[]{:S(2)}) copy-start(s32[64]{0:T(128)} %plan.1) | copy-start | bytes 772
  57.3 5.0 %collective-permute-start = (bf16[256,256]{1,0:T(8,128)(2,1)S(1)}, bf16[256,256]{1,0:T(8,128)(2,1)S(1)}, u32[]{:S(2)}, u32[]{:S(2)}) collective-permute-start(bf16[256,256]{1,0:T(8,128)(2,1)S(1)} %get-tuple-element.51), channel_id=1, source_target_pairs={{0,1},{1,2},{2,3},{3,0},{4,5},{5,6},{6,7},{7,4},{8,9},{9,10},{10,1... | collective-permute-start | bytes 393224 | tf_op jit(solution)/shard_map/ppermute | solution.py:285
  58.6 5.2 %collective-permute-start.5 = (bf16[256,256]{1,0:T(8,128)(2,1)S(1)}, bf16[256,256]{1,0:T(8,128)(2,1)S(1)}, u32[]{:S(2)}, u32[]{:S(2)}) collective-permute-start(bf16[256,256]{1,0:T(8,128)(2,1)S(1)} %add_convert_fusion.4), channel_id=1, source_target_pairs={{0,3},{1,0},{2,1},{3,2},{4,7},{5,4},{6,5},{7,6},{8,11},{9,8},{10,9... | collective-permute-start | bytes 393224 | tf_op jit(solution)/shard_map/ppermute | solution.py:292
  62.4 5.1 %collective-permute-start.1 = (bf16[256,256]{1,0:T(8,128)(2,1)S(1)}, bf16[256,256]{1,0:T(8,128)(2,1)S(1)}, u32[]{:S(2)}, u32[]{:S(2)}) collective-permute-start(bf16[256,256]{1,0:T(8,128)(2,1)S(1)} %add_convert_fusion.5), channel_id=1, source_target_pairs={{0,1},{1,2},{2,3},{3,0},{4,5},{5,6},{6,7},{7,4},{8,9},{9,10},{10,1... | collective-permute-start | bytes 393224 | tf_op jit(solution)/shard_map/ppermute | solution.py:291
  62.9 15.3 %copy-start.20 = (f32[128,8]{0,1:T(8,128)S(1)}, f32[128,8]{0,1:T(8,128)}, u32[]{:S(2)}) copy-start(f32[128,8]{0,1:T(8,128)} %param.26) | copy-start | bytes 12292
  62.9 15.4 %copy-start.14 = (s32[128,8]{0,1:T(8,128)S(1)}, s32[128,8]{0,1:T(8,128)}, u32[]{:S(2)}) copy-start(s32[128,8]{0,1:T(8,128)} %param.23) | copy-start | bytes 12292
  62.9 15.5 %copy-start.15 = (s32[128,8]{0,1:T(8,128)S(1)}, s32[128,8]{0,1:T(8,128)}, u32[]{:S(2)}) copy-start(s32[128,8]{0,1:T(8,128)} %param.24) | copy-start | bytes 12292
  63.0 15.6 %copy-start.16 = (s32[128,8]{0,1:T(8,128)S(1)}, s32[128,8]{0,1:T(8,128)}, u32[]{:S(2)}) copy-start(s32[128,8]{0,1:T(8,128)} %param.25) | copy-start | bytes 12292
  69.0 18.3 %all-to-all-start.1 = ((bf16[32,16,256]{2,1,0:T(8,128)(2,1)}), bf16[32,16,256]{2,1,0:T(8,128)(2,1)S(1)}, u32[]{:S(2)}, u32[]{:S(2)}) async-start(bf16[32,16,256]{2,1,0:T(8,128)(2,1)} %route.1), calls=%async_computation.1 | async-start | bytes 524288 | tf_op jit(solution)/shard_map/all_to_all | solution.py:376
  88.0 23.3 %copy-start.19 = (bf16[128,1024]{1,0:T(8,128)(2,1)S(1)}, bf16[128,1024]{1,0:T(8,128)(2,1)}, u32[]{:S(2)}) copy-start(bf16[128,1024]{1,0:T(8,128)(2,1)} %get-tuple-element.24) | copy-start | bytes 786436
  108.6 26.0 %collective-permute-start.7 = (bf16[512,1024]{1,0:T(8,128)(2,1)}, bf16[512,1024]{1,0:T(8,128)(2,1)S(1)}, u32[]{:S(2)}, u32[]{:S(2)}) collective-permute-start(bf16[512,1024]{1,0:T(8,128)(2,1)} %bitcast.10.own), channel_id=1, source_target_pairs={{0,1},{1,2},{2,3},{3,0},{4,5},{5,6},{6,7},{7,4},{8,9},{9,10},{10,1... | collective-permute-start | bytes 3145736 | tf_op jit(solution)/shard_map/ppermute | solution.py:271
  108.6 26.9 %collective-permute-start.6 = (bf16[512,1024]{1,0:T(8,128)(2,1)}, bf16[512,1024]{1,0:T(8,128)(2,1)S(1)}, u32[]{:S(2)}, u32[]{:S(2)}) collective-permute-start(bf16[512,1024]{1,0:T(8,128)(2,1)} %bitcast.10.own), channel_id=1, source_target_pairs={{0,3},{1,0},{2,1},{3,2},{4,7},{5,4},{6,5},{7,6},{8,11},{9,8},{10,9... | collective-permute-start | bytes 3145736 | tf_op jit(solution)/shard_map/ppermute | solution.py:272
  112.7 26.4 %copy-start.21 = (f32[1024]{0:T(1024)S(1)}, f32[1024]{0:T(1024)}, u32[]{:S(2)}) copy-start(f32[1024]{0:T(1024)} %param.22) | copy-start | bytes 12292
  112.7 41.0 %all-to-all-start.4 = ((bf16[32,16,1024]{2,1,0:T(8,128)(2,1)}), bf16[32,16,1024]{2,1,0:T(8,128)(2,1)S(1)}, u32[]{:S(2)}, u32[]{:S(2)}) async-start(bf16[32,16,1024]{2,1,0:T(8,128)(2,1)} %bitcast.35), calls=%async_computation.4 | async-start | bytes 2097152 | tf_op jit(solution)/shard_map/all_to_all | solution.py:392
  134.7 19.0 %copy-start.2 = (bf16[512,1024]{1,0:T(8,128)(2,1)}, bf16[512,1024]{1,0:T(8,128)(2,1)S(1)}, u32[]{:S(2)}) copy-start(bf16[512,1024]{1,0:T(8,128)(2,1)S(1)} %collective-permute-done.7.left.refs_2_) | copy-start | bytes 3145732
  135.6 22.0 %collective-permute-start.8 = (bf16[256,1024]{1,0:T(8,128)(2,1)}, bf16[256,1024]{1,0:T(8,128)(2,1)}, u32[]{:S(2)}, u32[]{:S(2)}) collective-permute-start(bf16[256,1024]{1,0:T(8,128)(2,1)} %slice.64), channel_id=1, source_target_pairs={{0,1},{1,2},{2,3},{3,0},{4,5},{5,6},{6,7},{7,4},{8,9},{9,10},{10,1... | collective-permute-start | bytes 1572872 | tf_op jit(solution)/shard_map/ppermute | solution.py:276
  135.6 18.1 %copy-start.4 = (bf16[512,1024]{1,0:T(8,128)(2,1)}, bf16[512,1024]{1,0:T(8,128)(2,1)S(1)}, u32[]{:S(2)}) copy-start(bf16[512,1024]{1,0:T(8,128)(2,1)S(1)} %collective-permute-done.6.right.refs_1_) | copy-start | bytes 3145732
  136.5 21.1 %collective-permute-start.9 = (bf16[256,1024]{1,0:T(8,128)(2,1)}, bf16[256,1024]{1,0:T(8,128)(2,1)}, u32[]{:S(2)}, u32[]{:S(2)}) collective-permute-start(bf16[256,1024]{1,0:T(8,128)(2,1)} %slice.65), channel_id=1, source_target_pairs={{0,3},{1,0},{2,1},{3,2},{4,7},{5,4},{6,5},{7,6},{8,11},{9,8},{10,9... | collective-permute-start | bytes 1572872 | tf_op jit(solution)/shard_map/ppermute | solution.py:277
  139.1 10.5 %collective-permute-start.11 = (f32[8,128]{1,0:T(8,128)S(1)}, f32[8,128]{1,0:T(8,128)S(1)}, u32[]{:S(2)}, u32[]{:S(2)}) collective-permute-start(f32[8,128]{1,0:T(8,128)S(1)} %bitcast.47), channel_id=1, source_target_pairs={{0,1},{1,2},{2,3},{3,0},{4,5},{5,6},{6,7},{7,4},{8,9},{9,10},{10,1... | collective-permute-start | bytes 12296 | tf_op jit(solution)/shard_map/ppermute | solution.py:271
  139.1 10.5 %collective-permute-start.10 = (f32[8,128]{1,0:T(8,128)S(1)}, f32[8,128]{1,0:T(8,128)S(1)}, u32[]{:S(2)}, u32[]{:S(2)}) collective-permute-start(f32[8,128]{1,0:T(8,128)S(1)} %bitcast.48), channel_id=1, source_target_pairs={{0,3},{1,0},{2,1},{3,2},{4,7},{5,4},{6,5},{7,6},{8,11},{9,8},{10,9... | collective-permute-start | bytes 12296 | tf_op jit(solution)/shard_map/ppermute | solution.py:272
  149.6 3.6 %collective-permute-start.12 = (f32[4,128]{1,0:T(4,128)S(1)}, f32[4,128]{1,0:T(4,128)S(1)}, u32[]{:S(2)}, u32[]{:S(2)}) collective-permute-start(f32[4,128]{1,0:T(4,128)S(1)} %slice.52), channel_id=1, source_target_pairs={{0,1},{1,2},{2,3},{3,0},{4,5},{5,6},{6,7},{7,4},{8,9},{9,10},{10,1... | collective-permute-start | bytes 6152 | tf_op jit(solution)/shard_map/ppermute | solution.py:276
  149.7 4.0 %collective-permute-start.13 = (f32[4,128]{1,0:T(4,128)S(1)}, f32[4,128]{1,0:T(4,128)S(1)}, u32[]{:S(2)}, u32[]{:S(2)}) collective-permute-start(f32[4,128]{1,0:T(4,128)S(1)} %slice.53), channel_id=1, source_target_pairs={{0,3},{1,0},{2,1},{3,2},{4,7},{5,4},{6,5},{7,6},{8,11},{9,8},{10,9... | collective-permute-start | bytes 6152 | tf_op jit(solution)/shard_map/ppermute | solution.py:277
  154.6 23.3 %collective-permute-start.21 = (bf16[512,1024]{1,0:T(8,128)(2,1)}, bf16[512,1024]{1,0:T(8,128)(2,1)S(1)}, u32[]{:S(2)}, u32[]{:S(2)}) collective-permute-start(bf16[512,1024]{1,0:T(8,128)(2,1)} %after.3.own), channel_id=1, source_target_pairs={{0,1},{1,2},{2,3},{3,0},{4,5},{5,6},{6,7},{7,4},{8,9},{9,10},{10,1... | collective-permute-start | bytes 3145736 | tf_op jit(solution)/shard_map/ppermute | solution.py:271
  154.6 23.5 %collective-permute-start.20 = (bf16[512,1024]{1,0:T(8,128)(2,1)}, bf16[512,1024]{1,0:T(8,128)(2,1)S(1)}, u32[]{:S(2)}, u32[]{:S(2)}) collective-permute-start(bf16[512,1024]{1,0:T(8,128)(2,1)} %after.3.own), channel_id=1, source_target_pairs={{0,3},{1,0},{2,1},{3,2},{4,7},{5,4},{6,5},{7,6},{8,11},{9,8},{10,9... | collective-permute-start | bytes 3145736 | tf_op jit(solution)/shard_map/ppermute | solution.py:272
  157.6 1.2 copy-start.3
  173.8 15.4 %collective-permute-start.14 = (bf16[256,1024]{1,0:T(8,128)(2,1)S(1)}, bf16[256,1024]{1,0:T(8,128)(2,1)S(1)}, u32[]{:S(2)}, u32[]{:S(2)}) collective-permute-start(bf16[256,1024]{1,0:T(8,128)(2,1)S(1)} %get-tuple-element.32), channel_id=1, source_target_pairs={{0,1},{1,2},{2,3},{3,0},{4,5},{5,6},{6,7},{7,4},{8,9},{9,10},{10,1... | collective-permute-start | bytes 1572872 | tf_op jit(solution)/shard_map/ppermute | solution.py:285
  173.9 15.6 %collective-permute-start.18 = (bf16[256,1024]{1,0:T(8,128)(2,1)S(1)}, bf16[256,1024]{1,0:T(8,128)(2,1)S(1)}, u32[]{:S(2)}, u32[]{:S(2)}) collective-permute-start(bf16[256,1024]{1,0:T(8,128)(2,1)S(1)} %get-tuple-element.36), channel_id=1, source_target_pairs={{0,3},{1,0},{2,1},{3,2},{4,7},{5,4},{6,5},{7,6},{8,11},{9,8},{10,9... | collective-permute-start | bytes 1572872 | tf_op jit(solution)/shard_map/ppermute | solution.py:286
  178.0 22.4 %copy-start.1 = (bf16[512,1024]{1,0:T(8,128)(2,1)S(1)}, bf16[512,1024]{1,0:T(8,128)(2,1)}, u32[]{:S(2)}) copy-start(bf16[512,1024]{1,0:T(8,128)(2,1)} %after.3.own) | copy-start | bytes 3145732
  178.0 22.4 %collective-permute-start.22 = (bf16[256,1024]{1,0:T(8,128)(2,1)S(1)}, bf16[256,1024]{1,0:T(8,128)(2,1)S(1)}, u32[]{:S(2)}, u32[]{:S(2)}) collective-permute-start(bf16[256,1024]{1,0:T(8,128)(2,1)S(1)} %slice.66), channel_id=1, source_target_pairs={{0,1},{1,2},{2,3},{3,0},{4,5},{5,6},{6,7},{7,4},{8,9},{9,10},{10,1... | collective-permute-start | bytes 1572872 | tf_op jit(solution)/shard_map/ppermute | solution.py:276
  178.1 22.3 %collective-permute-start.23 = (bf16[256,1024]{1,0:T(8,128)(2,1)S(1)}, bf16[256,1024]{1,0:T(8,128)(2,1)S(1)}, u32[]{:S(2)}, u32[]{:S(2)}) collective-permute-start(bf16[256,1024]{1,0:T(8,128)(2,1)S(1)} %slice.67), channel_id=1, source_target_pairs={{0,3},{1,0},{2,1},{3,2},{4,7},{5,4},{6,5},{7,6},{8,11},{9,8},{10,9... | collective-permute-start | bytes 1572872 | tf_op jit(solution)/shard_map/ppermute | solution.py:277
  189.4 26.1 %collective-permute-start.15 = (bf16[256,1024]{1,0:T(8,128)(2,1)S(1)}, bf16[256,1024]{1,0:T(8,128)(2,1)}, u32[]{:S(2)}, u32[]{:S(2)}) collective-permute-start(bf16[256,1024]{1,0:T(8,128)(2,1)S(1)} %add_convert_fusion.3), channel_id=1, source_target_pairs={{0,1},{1,2},{2,3},{3,0},{4,5},{5,6},{6,7},{7,4},{8,9},{9,10},{10,1... | collective-permute-start | bytes 1572872 | tf_op jit(solution)/shard_map/ppermute | solution.py:291
  189.7 25.8 %collective-permute-start.19 = (bf16[256,1024]{1,0:T(8,128)(2,1)S(1)}, bf16[256,1024]{1,0:T(8,128)(2,1)}, u32[]{:S(2)}, u32[]{:S(2)}) collective-permute-start(bf16[256,1024]{1,0:T(8,128)(2,1)S(1)} %add_convert_fusion.2), channel_id=1, source_target_pairs={{0,3},{1,0},{2,1},{3,2},{4,7},{5,4},{6,5},{7,6},{8,11},{9,8},{10,9... | collective-permute-start | bytes 1572872 | tf_op jit(solution)/shard_map/ppermute | solution.py:292
  192.4 29.7 %collective-permute-start.16 = (bf16[256,1024]{1,0:T(8,128)(2,1)}, bf16[256,1024]{1,0:T(8,128)(2,1)}, u32[]{:S(2)}, u32[]{:S(2)}) collective-permute-start(bf16[256,1024]{1,0:T(8,128)(2,1)} %get-tuple-element.33), channel_id=1, source_target_pairs={{0,3},{1,0},{2,1},{3,2},{4,7},{5,4},{6,5},{7,6},{8,11},{9,8},{10,9... | collective-permute-start | bytes 1572872 | tf_op jit(solution)/shard_map/ppermute | solution.py:288
  200.4 22.6 %collective-permute-start.17 = (bf16[256,1024]{1,0:T(8,128)(2,1)}, bf16[256,1024]{1,0:T(8,128)(2,1)}, u32[]{:S(2)}, u32[]{:S(2)}) collective-permute-start(bf16[256,1024]{1,0:T(8,128)(2,1)} %get-tuple-element.34), channel_id=1, source_target_pairs={{0,1},{1,2},{2,3},{3,0},{4,5},{5,6},{6,7},{7,4},{8,9},{9,10},{10,1... | collective-permute-start | bytes 1572872 | tf_op jit(solution)/shard_map/ppermute | solution.py:287
  215.5 44.3 %collective-permute-start.26 = (bf16[256,1024]{1,0:T(8,128)(2,1)}, bf16[256,1024]{1,0:T(8,128)(2,1)}, u32[]{:S(2)}, u32[]{:S(2)}) collective-permute-start(bf16[256,1024]{1,0:T(8,128)(2,1)} %get-tuple-element.46), channel_id=1, source_target_pairs={{0,3},{1,0},{2,1},{3,2},{4,7},{5,4},{6,5},{7,6},{8,11},{9,8},{10,9... | collective-permute-start | bytes 1572872 | tf_op jit(solution)/shard_map/ppermute | solution.py:288
  218.2 43.0 %collective-permute-start.27 = (bf16[256,1024]{1,0:T(8,128)(2,1)}, bf16[256,1024]{1,0:T(8,128)(2,1)}, u32[]{:S(2)}, u32[]{:S(2)}) collective-permute-start(bf16[256,1024]{1,0:T(8,128)(2,1)} %get-tuple-element.47), channel_id=1, source_target_pairs={{0,1},{1,2},{2,3},{3,0},{4,5},{5,6},{6,7},{7,4},{8,9},{9,10},{10,1... | collective-permute-start | bytes 1572872 | tf_op jit(solution)/shard_map/ppermute | solution.py:287
  223.0 21.5 %collective-permute-start.24 = (bf16[256,1024]{1,0:T(8,128)(2,1)}, bf16[256,1024]{1,0:T(8,128)(2,1)S(1)}, u32[]{:S(2)}, u32[]{:S(2)}) collective-permute-start(bf16[256,1024]{1,0:T(8,128)(2,1)} %get-tuple-element.43), channel_id=1, source_target_pairs={{0,1},{1,2},{2,3},{3,0},{4,5},{5,6},{6,7},{7,4},{8,9},{9,10},{10,1... | collective-permute-start | bytes 1572872 | tf_op jit(solution)/shard_map/ppermute | solution.py:285
  223.6 21.9 %collective-permute-start.28 = (bf16[256,1024]{1,0:T(8,128)(2,1)}, bf16[256,1024]{1,0:T(8,128)(2,1)S(1)}, u32[]{:S(2)}, u32[]{:S(2)}) collective-permute-start(bf16[256,1024]{1,0:T(8,128)(2,1)} %get-tuple-element.49), channel_id=1, source_target_pairs={{0,3},{1,0},{2,1},{3,2},{4,7},{5,4},{6,5},{7,6},{8,11},{9,8},{10,9... | collective-permute-start | bytes 1572872 | tf_op jit(solution)/shard_map/ppermute | solution.py:286
  245.5 14.3 %collective-permute-start.25 = (bf16[256,1024]{1,0:T(8,128)(2,1)}, bf16[256,1024]{1,0:T(8,128)(2,1)}, u32[]{:S(2)}, u32[]{:S(2)}) collective-permute-start(bf16[256,1024]{1,0:T(8,128)(2,1)} %add_convert_fusion.1), channel_id=1, source_target_pairs={{0,1},{1,2},{2,3},{3,0},{4,5},{5,6},{6,7},{7,4},{8,9},{9,10},{10,1... | collective-permute-start | bytes 1572872 | tf_op jit(solution)/shard_map/ppermute | solution.py:291
  246.5 14.7 %collective-permute-start.29 = (bf16[256,1024]{1,0:T(8,128)(2,1)}, bf16[256,1024]{1,0:T(8,128)(2,1)}, u32[]{:S(2)}, u32[]{:S(2)}) collective-permute-start(bf16[256,1024]{1,0:T(8,128)(2,1)} %add_convert_fusion), channel_id=1, source_target_pairs={{0,3},{1,0},{2,1},{3,2},{4,7},{5,4},{6,5},{7,6},{8,11},{9,8},{10,9... | collective-permute-start | bytes 1572872 | tf_op jit(solution)/shard_map/ppermute | solution.py:292
  250.6 26.1 %all-to-all-start.3 = ((bf16[32,16,1024]{2,1,0:T(8,128)(2,1)}), bf16[32,16,1024]{2,1,0:T(8,128)(2,1)S(1)}, u32[]{:S(2)}, u32[]{:S(2)}) async-start(bf16[32,16,1024]{2,1,0:T(8,128)(2,1)} %bitcast.16), calls=%async_computation.3 | async-start | bytes 2097152 | tf_op jit(solution)/shard_map/all_to_all | solution.py:392
  276.7 20.9 %all-to-all-start.5 = ((bf16[32,16,1024]{2,1,0:T(8,128)(2,1)}), bf16[32,16,1024]{2,1,0:T(8,128)(2,1)S(1)}, u32[]{:S(2)}, u32[]{:S(2)}) async-start(bf16[32,16,1024]{2,1,0:T(8,128)(2,1)} %bitcast.38), calls=%async_computation.5 | async-start | bytes 2097152 | tf_op jit(solution)/shard_map/all_to_all | solution.py:392
  (11 other events, 9.5 us)
Sparse Core Ops, SparseCore 0:
  9.7 40.1 all-gather.1
where the time goes:
time: 307 us; the launch traced here: 305 us
  waiting for transfers between devices  134 us (44%)
  starting transfers between devices  74.9 us (24%)
  Pallas kernels  32.2 us (10%)
  blocking collectives  20.6 us (7%)
  between operations  14.6 us (5%)
  local copies, waits for them, and re-layouts  13 us (4%)
  other arithmetic  10.7 us (3%)
  matrix products  5.69 us (2%)
    all_to_all x3, waiting for transfers between devices, exchange(): lax.all_to_all(rows.reshape(32, CAP, PART), DP, 0, 0, tiled=True)  29.4 us
    ppermute x3, waiting for transfers between devices, ring_gather(): left = lax.ppermute(block, 'tensor', RIGHT)  26.6 us
    all_to_all x1, waiting for transfers between devices, per_device(): lax.all_to_all(sent.reshape(32, 16, PART + 256), DP, 0, 0, tiled=True)  26 us
    pallas_call x2, Pallas kernels, run_expert(): pl.pallas_call(expert_kernel, grid_spec=grid, out_shape=[half] * 6 + [jax...  25.6 us
    ppermute x3, waiting for transfers between devices, ring_scatter(): top = lax.ppermute(far_top, 'tensor', RIGHT)  25.1 us
    all_to_all x1, blocking collectives, exchange(): lax.all_to_all(rows.reshape(32, CAP, PART), DP, 0, 0, tiled=True)  20.6 us
    all_to_all x3, starting transfers between devices, exchange(): lax.all_to_all(rows.reshape(32, CAP, PART), DP, 0, 0, tiled=True)  17.8 us
    unnamed x50, local copies, waits for them, and re-layouts  11.1 us
  transfers between devices with their start and end apart: 36, of which 18 were waited for; matrix products, arithmetic and copies ran while one was open for 5% of the time, Pallas kernels for 10%

commit v1 on v0

v1 whole, which is shorter than its diff:
```python
import functools

import jax
import jax.numpy as jnp
from jax import lax
from jax.experimental import pallas as pl
from jax.experimental.pallas import tpu as pltpu
from jax.sharding import Mesh, PartitionSpec as P

D = 4096
HEAD_WIDTH = 128
PACK_ROWS = 64
QUERY_PER_KEY = 8
DP = ("y", "z", "core")
ROWS = 128
CAP = 16
BINS = 32 * CAP
PART = 1024
VMEM = 60
UNITS = 384
F32 = jnp.float32
BF16 = jnp.bfloat16

RIGHT = [(i, (i + 1) % 4) for i in range(4)]
LEFT = [(i, (i - 1) % 4) for i in range(4)]


NO_COST = pl.CostEstimate(flops=0, bytes_accessed=0, transcendentals=0)


def iota(shape, dim):
    return lax.broadcasted_iota(jnp.int32, shape, dim)


def whole(memory_space=pltpu.VMEM):
    return pl.BlockSpec(memory_space=memory_space)


def params(megabytes):
    return pltpu.CompilerParams(vmem_limit_bytes=megabytes << 20)


def after(values, *done):
    count = len(values)
    return pl.pallas_call(
        lambda *refs: None,
        out_shape=[jax.ShapeDtypeStruct(v.shape, v.dtype) for v in values],
        in_specs=[whole(pltpu.HBM)] * (count + len(done)),
        out_specs=[whole(pltpu.HBM)] * count,
        input_output_aliases={i: i for i in range(count)},
        name="after",
    )(*values, *done)


def attend_kernel(
    index, lengths, queries_in, keys_in, values_in, residual_in, out, queries, keys, values, residual, sems
):
    pairs = ((queries_in, queries), (keys_in, keys), (values_in, values), (residual_in, residual))
    copies = [pltpu.make_async_copy(a, b, sems.at[i]) for i, (a, b) in enumerate(pairs)]
    for copy in copies:
        copy.start()
    first = 2 * index[0]
    position = iota((ROWS, ROWS), 0)
    other = iota((ROWS, ROWS), 1)

    def label(at):
        second = at >= PACK_ROWS
        inner = jnp.where(second, at - PACK_ROWS, at)
        found = jnp.where(second, 8, 0)
        ends = [jnp.int32(0), jnp.int32(0)]
        for doc in range(4):
            for s in range(2):
                ends[s] = ends[s] + lengths[doc, first + s]
            found = found + (inner >= jnp.where(second, ends[1], ends[0])).astype(jnp.int32)
        return found

    hidden = jnp.where((label(position) == label(other)) & (position >= other), 0.0, -1e30)
    for copy in copies:
        copy.wait()
    lanes = [slice(h * HEAD_WIDTH, (h + 1) * HEAD_WIDTH) for h in range(QUERY_PER_KEY)]
    stacked = jnp.concatenate([queries[:, part] for part in lanes], axis=0)
    scores = lax.dot_general(
        stacked, keys[...], (((1,), (1,)), ((), ())), preferred_element_type=F32
    ).reshape(QUERY_PER_KEY, ROWS, ROWS)
    masked = jnp.where(hidden[None] < 0.0, -1e30, scores * HEAD_WIDTH**-0.5)
    exps = jnp.exp(masked - jnp.max(masked, axis=2, keepdims=True))
    probs = (exps / jnp.sum(exps, axis=2, keepdims=True)).astype(BF16)
    heads = jnp.dot(
        probs.reshape(QUERY_PER_KEY * ROWS, ROWS), values[...], preferred_element_type=F32
    )
    attended = jnp.concatenate(
        [heads[h * ROWS : (h + 1) * ROWS] for h in range(QUERY_PER_KEY)], axis=1
    )
    rest = residual[...].astype(F32)

    def group(rows, at):
        low = rows[at * 8 : at * 8 + 8]
        high = rows[PACK_ROWS + at * 8 : PACK_ROWS + at * 8 + 8]
        return jnp.concatenate([low, high], axis=0).astype(BF16)

    for y in range(4):
        for core in range(2):
            mine = group(attended, y * 2 + core)
            plain = group(rest, y * 2 + core)
            for z in range(4):
                out[y, z, core, :, :PART] = mine
                out[y, z, core, :, PART:] = plain[:, z * 256 : z * 256 + 256]


def columns_kernel(distances, count, index, weight, gain, *rest):
    outs, sems = rest[-1 - len(distances) : -1], rest[-1]
    copies = []
    for n, (distance, first) in enumerate(distances):
        start = pl.multiple_of(((index[0] + distance) % 4) * PART, PART)
        for i in range(count):
            copies.append(
                pltpu.make_async_copy(
                    weight.at[first + i, :, pl.ds(start, PART)],
                    outs[n].at[pl.ds(i * UNITS, UNITS)],
                    sems.at[n * count + i],
                )
            )
    for copy in copies:
        copy.start()
    left = jnp.broadcast_to(gain[...], (16, PART))
    row = iota((16, PART), 0)
    terms = jnp.zeros((16, PART), F32)
    for k in range(3):
        term = left.astype(BF16).astype(F32)
        terms = jnp.where(row == k, term, terms)
        left = left - term
    for out in outs:
        out[pl.ds(count * UNITS, 16), :] = terms.astype(BF16)
    for copy in copies:
        copy.wait()


def run_columns(x, weight, gain, distances, count, *done):
    rows = count * UNITS + 16
    return pl.pallas_call(
        functools.partial(columns_kernel, distances, count),
        out_shape=[jax.ShapeDtypeStruct((rows, PART), BF16)] * len(distances),
        in_specs=[whole(pltpu.SMEM), whole(pltpu.HBM), whole()] + [whole(pltpu.HBM)] * len(done),
        out_specs=[whole()] * len(distances),
        scratch_shapes=[pltpu.SemaphoreType.DMA((len(distances) * count,))],
        compiler_params=params(VMEM),
        cost_estimate=NO_COST,
        name="columns",
    )(x, weight, gain, *done)


def project_kernel(
    index, rows, weight, far_top, far_low, right_top, right_low, left_top, left_low, mine
):
    def product(distance):
        start = pl.multiple_of(((index[0] + distance) % 4) * 256, 256)
        return jnp.dot(rows[:, :PART], weight[:, pl.ds(start, 256)], preferred_element_type=F32)

    for distance, upper, lower in ((2, far_top, far_low), (1, right_top, right_low), (3, left_top, left_low)):
        result = product(distance).astype(BF16)
        upper[...] = result[:256]
        lower[...] = result[256:]
    mine[...] = product(0) + rows[:, PART:].astype(F32)


def route_kernel(plan, own, one_top, one_low, two_top, two_low, out, placed):
    top = own[:256] + (one_top[...].astype(F32) + two_top[...].astype(F32))
    low = own[256:] + (one_low[...].astype(F32) + two_low[...].astype(F32))
    for source in range(32):
        at = source * 16
        half = top[at : at + 16] if at < 256 else low[at - 256 : at - 240]
        merged = half.astype(BF16).astype(F32)
        for s in range(2):
            placed[plan[source * 2 + s], s * 8 : s * 8 + 8, :] = merged[s * 8 : s * 8 + 8]
    out[...] = placed[...].astype(BF16)


def stream_kernel(landed, table, stream, bins):
    parts = []
    for z in range(4):
        tiles = [landed[y, z, core].astype(F32) for y in range(4) for core in range(2)]
        parts.append(
            jnp.concatenate([t[s * 8 : s * 8 + 8] for s in range(2) for t in tiles], axis=0)
        )
    rows = jnp.concatenate(parts, axis=1).astype(BF16)
    stream[...] = rows
    bins[...] = jnp.dot(table[...], rows, preferred_element_type=F32).astype(BF16)


def tables_kernel(
    routes_t, slots_t, dropped_t, routes, slots, dropped, weight, send0, send1, mix
):
    across = jnp.where(dropped_t[...] == 0, (routes_t[...] // 2) * CAP + slots_t[...], -1)
    row = iota((BINS, ROWS), 0)
    for local, out in enumerate((send0, send1)):
        mine = jnp.where(routes_t[...] % 2 == local, across, -1)
        total = jnp.zeros((BINS, ROWS), F32)
        for k in range(8):
            total = total + jnp.where(mine[k : k + 1] == row, 1.0, 0.0)
        out[...] = total.astype(BF16)
    down = jnp.where(dropped[...] == 0, routes[...] * CAP + slots[...], -1)
    column = iota((ROWS, 2 * BINS), 1)
    total = jnp.zeros((ROWS, 2 * BINS), F32)
    for k in range(8):
        total = total + jnp.where(down[:, k : k + 1] == column, weight[:, k : k + 1], 0.0)
    mix[...] = total.astype(BF16)


def near_kernel(index, own, right, left, gain, gate_w, up_w, total, squares, rows, sems):
    step = pl.program_id(0)
    copies = [
        pltpu.make_async_copy(source, rows.at[i], sems.at[i])
        for i, source in enumerate((own, right, left))
    ]

    @pl.when(step == 0)
    def _():
        for copy in copies:
            copy.start()
        total[...] = jnp.zeros_like(total)
        squares[...] = jnp.zeros_like(squares)
        copies[0].wait()

    @pl.when(step == 1)
    def _():
        copies[1].wait()

    @pl.when(step == 2)
    def _():
        copies[2].wait()

    wide = rows[step].astype(F32)
    squares[...] += jnp.sum(wide * wide, axis=1, keepdims=True)
    scaled = (wide * gain[...]).astype(BF16)
    both = jnp.concatenate([gate_w[...], up_w[...]], axis=1)
    total[...] += jnp.dot(scaled, both, preferred_element_type=F32)


def far_kernel(index, top, low, total, squares, gain, gate_w, up_w, hidden):
    wide = jnp.concatenate([top[...], low[...]], axis=0).astype(F32)
    mean = (squares[...] + jnp.sum(wide * wide, axis=1, keepdims=True)) * (1.0 / D)
    norm = lax.rsqrt(mean + 1e-6)
    scaled = (wide * gain[...]).astype(BF16)
    both = jnp.concatenate([gate_w[...], up_w[...]], axis=1)
    values = (total[...] + jnp.dot(scaled, both, preferred_element_type=F32)) * norm
    gate = values[:, :UNITS]
    hidden[...] = (gate / (1.0 + jnp.exp(-gate)) * values[:, UNITS:]).astype(BF16)


def flat(shape):
    return pl.BlockSpec(shape, lambda i, at: (0, 0))


def gain_at(slot):
    return pl.BlockSpec((None, 1, PART), lambda i, at: (slot(i), 0, 0))


def weights_at(local, place):
    return [pl.BlockSpec((None, PART, UNITS), lambda i, at: (local, place(i, at), 0))] * 2


def run_near(x, local, blocks, gains, gate_weight, up_weight):
    return pl.pallas_call(
        near_kernel,
        grid_spec=pltpu.PrefetchScalarGridSpec(
            num_scalar_prefetch=1,
            grid=(3,),
            in_specs=[whole(pltpu.HBM)] * 3
            + [gain_at(lambda i: i)]
            + weights_at(local, lambda i, at: (at[0] + (i ^ (i >> 1))) % 4),
            out_specs=[flat((BINS, 2 * UNITS)), flat((BINS, 1))],
            scratch_shapes=[pltpu.VMEM((3, BINS, PART), BF16), pltpu.SemaphoreType.DMA((3,))],
        ),
        out_shape=[
            jax.ShapeDtypeStruct((BINS, 2 * UNITS), F32),
            jax.ShapeDtypeStruct((BINS, 1), F32),
        ],
        compiler_params=params(VMEM),
        cost_estimate=NO_COST,
        name="near",
    )(x, *blocks, gains, gate_weight, up_weight)


def run_far(x, local, blocks, near, gains, gate_weight, up_weight):
    return pl.pallas_call(
        far_kernel,
        grid_spec=pltpu.PrefetchScalarGridSpec(
            num_scalar_prefetch=1,
            grid=(1,),
            in_specs=[flat(v.shape) for v in (*blocks, *near)]
            + [gain_at(lambda i: 3)]
            + weights_at(local, lambda i, at: (at[0] + 2) % 4),
            out_specs=flat((BINS, UNITS)),
        ),
        out_shape=jax.ShapeDtypeStruct((BINS, UNITS), BF16),
        compiler_params=params(VMEM),
        cost_estimate=NO_COST,
        name="far",
    )(x, *blocks, *near, gains, gate_weight, up_weight)


def down_kernel(
    local, index, own, right, left, top, low, own_w, right_w, left_w, far_w, *rest
):
    out, units, weights, product, sems = rest[-5:]
    half = BINS // 2
    column = pl.multiple_of(index[0] * PART, PART)
    rows = pl.ds(local * UNITS, UNITS)
    pairs = (
        (own, units.at[0]),
        (own_w.at[local, :, pl.ds(column, PART)], weights.at[0]),
        (right, units.at[1]),
        (right_w.at[rows], weights.at[1]),
        (left, units.at[2]),
        (left_w.at[rows], weights.at[2]),
        (top, units.at[3, pl.ds(0, half)]),
        (low, units.at[3, pl.ds(half, half)]),
        (far_w.at[pl.ds(0, UNITS)], weights.at[3]),
    )
    copies = [pltpu.make_async_copy(a, b, sems.at[i]) for i, (a, b) in enumerate(pairs)]
    for copy in copies:
        copy.start()
    total = 0.0
    for block in range(4):
        for copy in copies[2 * block : 2 * block + (3 if block == 3 else 2)]:
            copy.wait()
        total = total + jnp.dot(units[block], weights[block], preferred_element_type=F32)
    product[...] = total.astype(BF16).reshape(32, CAP, PART)
    result = pltpu.make_async_copy(product, out.at[:, local], sems.at[9])
    result.start()
    result.wait()


def run_down(x, local, blocks, down_weight, right_w, left_w, far_w, *more, into=None):
    given = (*blocks, down_weight, right_w, left_w, far_w, *more) + (() if into is None else (into,))
    return pl.pallas_call(
        functools.partial(down_kernel, local),
        out_shape=jax.ShapeDtypeStruct((32, 2, CAP, PART), BF16),
        in_specs=[whole(pltpu.SMEM)] + [whole(pl.ANY)] * len(given),
        out_specs=whole(pltpu.HBM),
        input_output_aliases={} if into is None else {len(given): 0},
        scratch_shapes=[
            pltpu.VMEM((4, BINS, UNITS), BF16),
            pltpu.VMEM((4, UNITS, PART), BF16),
            pltpu.VMEM((32, CAP, PART), BF16),
            pltpu.SemaphoreType.DMA((10,)),
        ],
        compiler_params=params(VMEM),
        cost_estimate=NO_COST,
        name="down",
    )(x, *given)


def ring_gather(block, axis="tensor", done=()):
    half = block.shape[0] // 2
    left = lax.ppermute(block, axis, RIGHT)
    right = lax.ppermute(block, axis, LEFT)
    upper, lower = left[:half], right[half:]
    if done:
        upper, lower = after((upper, lower), *done)
    return right, left, lax.ppermute(upper, axis, RIGHT), lax.ppermute(lower, axis, LEFT)


def ring_scatter(far_top, far_low, right_top, right_low, left_top, left_low):
    top = lax.ppermute(far_top, "tensor", RIGHT)
    low = lax.ppermute(far_low, "tensor", LEFT)
    from_left_low = lax.ppermute(right_low, "tensor", RIGHT)
    from_right_top = lax.ppermute(left_top, "tensor", LEFT)
    right_sum = (right_top.astype(F32) + top.astype(F32)).astype(BF16)
    left_sum = (left_low.astype(F32) + low.astype(F32)).astype(BF16)
    from_left_top = lax.ppermute(right_sum, "tensor", RIGHT)
    from_right_low = lax.ppermute(left_sum, "tensor", LEFT)
    return from_left_top, from_left_low, from_right_top, from_right_low


def per_device(
    queries,
    rotated_key_rows,
    value_matrix,
    residual,
    lengths,
    move_plan,
    out_weight,
    norm_gain,
    routes,
    bin_slots,
    dropped,
    route_weight,
    gate_weight,
    up_weight,
    down_weight,
):
    x = lax.axis_index("tensor")
    d = lax.axis_index(DP)
    x_ref = jnp.reshape(x, (1,)).astype(jnp.int32)

    weight = lax.all_gather(out_weight, ("y", "core"), axis=1, tiled=True)

    sent = pl.pallas_call(
        attend_kernel,
        out_shape=jax.ShapeDtypeStruct((4, 4, 2, 16, PART + 256), BF16),
        in_specs=[whole(pltpu.SMEM)] * 2 + [whole(pl.ANY)] * 4,
        out_specs=whole(),
        scratch_shapes=[
            pltpu.VMEM((ROWS, PART), BF16),
            pltpu.VMEM((ROWS, HEAD_WIDTH), BF16),
            pltpu.VMEM((ROWS, HEAD_WIDTH), BF16),
            pltpu.VMEM((ROWS, PART), BF16),
            pltpu.SemaphoreType.DMA((4,)),
        ],
        compiler_params=params(VMEM),
        cost_estimate=NO_COST,
        name="attend",
    )(jnp.reshape(d, (1,)).astype(jnp.int32), lengths.T, queries, rotated_key_rows, value_matrix, residual)
    spread = lax.all_to_all(sent.reshape(32, 16, PART + 256), DP, 0, 0, tiled=True)
    spread = spread.reshape(512, PART + 256)

    send0, send1, mix = pl.pallas_call(
        tables_kernel,
        out_shape=[jax.ShapeDtypeStruct((BINS, ROWS), BF16)] * 2
        + [jax.ShapeDtypeStruct((ROWS, 2 * BINS), BF16)],
        in_specs=[whole()] * 7,
        out_specs=[whole()] * 3,
        compiler_params=params(VMEM),
        cost_estimate=NO_COST,
        name="tables",
    )(routes.T, bin_slots.T, dropped.T, routes, bin_slots, dropped, route_weight)
    own_gain = norm_gain.reshape(1, PART)
    for_right, for_left = run_columns(x_ref, down_weight, own_gain, ((1, 0), (3, 0)), 2)
    left_w = lax.ppermute(for_right, "tensor", RIGHT)
    right_w = lax.ppermute(for_left, "tensor", LEFT)
    far0, far1 = run_columns(x_ref, down_weight, own_gain, ((2, 0), (2, 1)), 1, sent)
    (weight,) = after((weight,), left_w, right_w, far0, far1, send0)

    half = jax.ShapeDtypeStruct((256, 256), BF16)
    *partial, mine = pl.pallas_call(
        project_kernel,
        out_shape=[half] * 6 + [jax.ShapeDtypeStruct((512, 256), F32)],
        in_specs=[whole(pltpu.SMEM)] + [whole()] * 2,
        out_specs=[whole()] * 7,
        compiler_params=params(VMEM),
        cost_estimate=NO_COST,
        name="project",
    )(x_ref, spread, weight)
    sums = ring_scatter(*partial)
    onward = pl.pallas_call(
        route_kernel,
        out_shape=jax.ShapeDtypeStruct((32, 16, 256), BF16),
        in_specs=[whole(pltpu.SMEM)] + [whole()] * 5,
        out_specs=whole(),
        scratch_shapes=[pltpu.VMEM((32, 16, 256), F32)],
        compiler_params=params(VMEM),
        cost_estimate=NO_COST,
        name="route",
    )(move_plan, mine, *sums)
    landed = lax.all_to_all(onward, DP, 0, 0, tiled=True)
    far0, far1 = after((far0, far1), onward)
    far_w0 = lax.ppermute(far0, "tensor", RIGHT)
    far_w1 = lax.ppermute(far1, "tensor", LEFT)
    far_w0 = lax.ppermute(far_w0, "tensor", RIGHT)
    far_w1 = lax.ppermute(far_w1, "tensor", LEFT)

    stream, bins0 = pl.pallas_call(
        stream_kernel,
        out_shape=[
            jax.ShapeDtypeStruct((ROWS, PART), BF16),
            jax.ShapeDtypeStruct((BINS, PART), BF16),
        ],
        in_specs=[whole()] * 2,
        out_specs=[whole()] * 2,
        compiler_params=params(VMEM),
        cost_estimate=NO_COST,
        name="stream",
    )(landed.reshape(4, 4, 2, 16, 256), send0)
    bins1 = jnp.dot(send1, stream, preferred_element_type=F32).astype(BF16)

    def exchange(rows):
        return lax.all_to_all(rows.reshape(32, CAP, PART), DP, 0, 0, tiled=True).reshape(BINS, PART)

    held0 = exchange(bins0)
    (bins1,) = after((bins1,), far_w0, far_w1)

    def whole_gain(rows):
        return jnp.sum(rows[-16:].astype(F32), axis=0, keepdims=True)

    gains = jnp.stack([own_gain, whole_gain(right_w), whole_gain(left_w), whole_gain(far_w0)], axis=0)
    weights = (gate_weight, up_weight)
    right0, left0, top0, low0 = ring_gather(held0)
    partial0 = run_near(x_ref, 0, (held0, right0, left0), gains, *weights)
    (held1,) = after((exchange(bins1),), top0, low0, partial0[1])
    hidden0 = run_far(x_ref, 0, (top0, low0), partial0, gains, *weights)
    units0 = ring_gather(hidden0)
    right1, left1, top1, low1 = ring_gather(held1, done=units0[:2])
    partial1 = run_near(x_ref, 1, (held1, right1, left1), gains, *weights)
    hidden1 = run_far(x_ref, 1, (top1, low1), partial1, gains, *weights)
    units1 = ring_gather(hidden1)
    back = run_down(x_ref, 0, (hidden0, *units0), down_weight, right_w, left_w, far_w0, hidden1)
    back = run_down(x_ref, 1, (hidden1, *units1), down_weight, right_w, left_w, far_w1, into=back)
    back = lax.all_to_all(back.reshape(32, 2 * CAP, PART), DP, 0, 0, tiled=True)
    result = jnp.dot(mix, back.reshape(2 * BINS, PART), preferred_element_type=F32)
    return (stream, result.astype(BF16))


def solution(mesh):
    fine = Mesh(mesh.devices.reshape(4, 4, 2, 4), ("y", "z", "core", "tensor"))
    return jax.shard_map(
        per_device,
        mesh=fine,
        in_specs=(
            P(DP, "tensor"),
            P(DP, "tensor"),
            P(DP, "tensor"),
            P(DP, "tensor"),
            P(),
            P(),
            P("tensor", DP),
            P("tensor"),
            P(DP, None),
            P(DP, None),
            P(DP, None),
            P(DP, None),
            P(DP, None, "tensor"),
            P(DP, None, "tensor"),
            P(DP, "tensor", None),
        ),
        out_specs=(P(DP, "tensor"), P(DP, "tensor")),
        check_vma=False,
    )
```

time: 307 us -> 296 us (0.964)
  waiting for transfers between devices: 134 us -> 82.5 us
  Pallas kernels: 32.2 us -> 56.9 us
  blocking collectives: 20.6 us -> 43.9 us
  other arithmetic: 10.7 us -> 4.82 us
  local copies, waits for them, and re-layouts: 13 us -> 17.8 us
  matrix products: 5.69 us -> 2.54 us
    ppermute x12 -> x22, waiting for transfers between devices: 35.3 us -> 61.3 us  [the longest x4 23.1 us: ring_gather(): right = lax.ppermute(block, axis, LEFT)]
    all_to_all x1, waiting for transfers between devices: 26 us -> 1.35 us  [per_device(): lax.all_to_all(sent.reshape(32, 16, PART + 256), DP, 0, 0, tiled=True)]
    ppermute x3 -> x1, waiting for transfers between devices: 25.1 us -> 1.53 us  [ring_scatter(): top = lax.ppermute(far_top, 'tensor', RIGHT)]
    all_to_all x1, blocking collectives: 20.6 us -> 43.9 us  [per_device(): back = lax.all_to_all(back.reshape(32, 2 * CAP, PART), DP, 0, 0, tiled=True)]
    all_to_all x3 -> x2, waiting for transfers between devices: 29.4 us -> 8.09 us  [exchange(): lax.all_to_all(rows.reshape(32, CAP, PART), DP, 0, 0, tiled=True)]
    pallas_call x2 -> x9, Pallas kernels: 25.6 us -> 45.3 us  [the longest x2 15 us: run_near(): pl.pallas_call(near_kernel, grid_spec=pltpu.PrefetchScalarGridSpec(num_sc...]
    ppermute x12 -> x22, starting transfers between devices: 17 us -> 32 us  [the longest x4 11.9 us: ring_gather(): lax.ppermute(lower, axis, LEFT)]
    ppermute x3 -> x1, starting transfers between devices: 8.23 us -> 2.55 us  [ring_scatter(): from_right_low = lax.ppermute(left_sum, 'tensor', LEFT)]
  transfers between devices with their start and end apart: 36 -> 33, of which waited for: 18 -> 17; matrix products, arithmetic and copies ran while one was open for 5% -> 4% of each run, Pallas kernels for 10% -> 14%
where the time goes in v1:
time: 296 us; the launch traced here: 295 us
  waiting for transfers between devices  82.5 us (28%)
  starting transfers between devices  72 us (24%)
  Pallas kernels  56.9 us (19%)
  blocking collectives  43.9 us (15%)
  local copies, waits for them, and re-layouts  17.8 us (6%)
  between operations  14.5 us (5%)
  other arithmetic  4.82 us (2%)
    all_to_all x1, blocking collectives, per_device(): back = lax.all_to_all(back.reshape(32, 2 * CAP, PART), DP, 0, 0, tiled=True)  43.9 us
    ppermute x4, waiting for transfers between devices, ring_gather(): right = lax.ppermute(block, axis, LEFT)  23.1 us
    pallas_call x2, Pallas kernels, run_near(): pl.pallas_call(near_kernel, grid_spec=pltpu.PrefetchScalarGridSpec(num_sc...  15 us
    all_to_all x2, starting transfers between devices, exchange(): lax.all_to_all(rows.reshape(32, CAP, PART), DP, 0, 0, tiled=True)  13.9 us
    unnamed x74, local copies, waits for them, and re-layouts  13.8 us
    ppermute x4, waiting for transfers between devices, ring_gather(): left = lax.ppermute(block, axis, RIGHT)  11.9 us
    ppermute x4, starting transfers between devices, ring_gather(): lax.ppermute(lower, axis, LEFT)  11.9 us
    ppermute x1, waiting for transfers between devices, per_device(): left_w = lax.ppermute(for_right, 'tensor', RIGHT)  11.7 us
  transfers between devices with their start and end apart: 33, of which 17 were waited for; matrix products, arithmetic and copies ran while one was open for 4% of the time, Pallas kernels for 14%

profile of v1, /device:TPU:1, one launch (start us, length us, event | category | flops | bytes accessed | tf_op | source)
XLA Modules:
  0.0 294.9 jit_solution(6464516911324755450)
XLA Ops:
  7.9 4.3 %columns.2 = (bf16[784,1024]{1,0:T(8,128)(2,1)}, bf16[784,1024]{1,0:T(8,128)(2,1)}) custom-call(s32[1]{0:T(128)} %bitcast.index, bf16[2,384,4096]{2,1,0:T(8,128)(2,1)} %own_w.3, f32[1,1024]{1,0:T(1,128)} %bitcast.34), custom_call_target="tpu_custom_call" | custom-call | tf_op jit(solution)/shard_map/columns/pallas_call | solution.py:140
  12.2 2.1 collective-permute-start
  14.3 1.3 collective-permute-start.1
  15.6 3.6 %attend.1.rest_0_ = bf16[4,4,2,16,1280]{4,3,2,1,0:T(8,128)(2,1)} custom-call(s32[1]{0:T(128)} %bitcast.1.index, s32[4,64]{1,0:T(4,128)} %bitcast.43, bf16[128,1024]{1,0:T(8,128)(2,1)} %queries_in.1, bf16[128,128]{1,0:T(8,128)(2,1)} %keys_in.1, bf16[128,128]{1,0:T(8,128)(2,1)} %values_in.1, bf16[128,1024]{1,0:T(8,128)(2,1)} %residual_in.1), custom_call_target="tpu_custom_call" | custom-call | tf_op jit(solution)/shard_map/attend/pallas_call | solution.py:399
  19.2 9.5 %all-to-all-start = ((bf16[32,16,1280]{2,1,0:T(8,128)(2,1)}), bf16[32,16,1280]{2,1,0:T(8,128)(2,1)}, u32[]{:S(2)}, u32[]{:S(2)}) async-start(bf16[32,16,1280]{2,1,0:T(8,128)(2,1)} %bitcast.25), calls=%async_computation | async-start | bytes 2621440 | tf_op jit(solution)/shard_map/all_to_all | solution.py:415
  28.8 3.4 %columns.3 = (bf16[400,1024]{1,0:T(8,128)(2,1)}, bf16[400,1024]{1,0:T(8,128)(2,1)}) custom-call(s32[1]{0:T(128)} %bitcast.index, bf16[2,384,4096]{2,1,0:T(8,128)(2,1)} %own_w.3, f32[1,1024]{1,0:T(1,128)} %bitcast.35, bf16[4,4,2,16,1280]{4,3,2,1,0:T(8,128)(2,1)} %attend.1.rest_0_), custom_call_target="tpu_custom_call" | custom-call | tf_op jit(solution)/shard_map/columns/pallas_call | solution.py:140
  35.1 3.4 %tables.1 = (bf16[512,128]{1,0:T(8,128)(2,1)}, bf16[512,128]{1,0:T(8,128)(2,1)}, bf16[128,1024]{1,0:T(8,128)(2,1)}) custom-call(s32[8,128]{1,0:T(8,128)} %bitcast.37, s32[8,128]{1,0:T(8,128)} %bitcast.38, s32[8,128]{1,0:T(8,128)} %bitcast.39, s32[128,8]{1,0:T(8,128)} %copy.25.routes, s32[128,8]{1,0:T(8,128)} %copy.26.slots, s32[128,8]{1,0:T(8,128)} %copy.27.dropped, ...), custom_call_target="tpu_custom_call" | custom-call | tf_op jit(solution)/shard_map/tables/pallas_call | solution.py:418
  38.5 11.7 %collective-permute-done.refs_1_.left_w = bf16[784,1024]{1,0:T(8,128)(2,1)S(1)} collective-permute-done((bf16[784,1024]{1,0:T(8,128)(2,1)}, bf16[784,1024]{1,0:T(8,128)(2,1)S(1)}, u32[]{:S(2)}, u32[]{:S(2)}) %collective-permute-start) | collective-permute-done | bytes 1605664 | tf_op jit(solution)/shard_map/ppermute | solution.py:430
  51.9 1.3 all-to-all-done
  53.3 4.1 %project.1 = (bf16[256,256]{1,0:T(8,128)(2,1)}, bf16[256,256]{1,0:T(8,128)(2,1)}, bf16[256,256]{1,0:T(8,128)(2,1)}, bf16[256,256]{1,0:T(8,128)(2,1)}, bf16[256,2...) custom-call(s32[1]{0:T(128)} %bitcast.index, bf16[512,1280]{1,0:T(8,128)(2,1)} %bitcast.4.rows, ...), custom_call_target="tpu_custom_call" | custom-call | tf_op jit(solution)/shard_map/project/pallas_call | solution.py:436
  59.4 1.5 collective-permute-start.5
  61.6 1.5 collective-permute-done.2
  64.1 2.2 collective-permute-done.6
  67.2 2.5 collective-permute-start.7
  69.8 1.9 collective-permute-done.7.two_low
  72.4 2.1 route.1.refs_2_
  74.5 9.8 %all-to-all-start.1 = ((bf16[32,16,256]{2,1,0:T(8,128)(2,1)}), bf16[32,16,256]{2,1,0:T(8,128)(2,1)S(1)}, u32[]{:S(2)}, u32[]{:S(2)}) async-start(bf16[32,16,256]{2,1,0:T(8,128)(2,1)} %route.1.refs_2_), calls=%async_computation.1 | async-start | bytes 524288 | tf_op jit(solution)/shard_map/all_to_all | solution.py:456
  85.0 2.9 collective-permute-start.10
  87.8 5.4 %all-to-all-done.1 = bf16[32,16,256]{2,1,0:T(8,128)(2,1)S(1)} async-done(((bf16[32,16,256]{2,1,0:T(8,128)(2,1)}), bf16[32,16,256]{2,1,0:T(8,128)(2,1)S(1)}, u32[]{:S(2)}, u32[]{:S(2)}) %all-to-all-start.1) | async-done | bytes 262176 | tf_op jit(solution)/shard_map/all_to_all | solution.py:456
  94.0 2.4 stream.1
  96.4 3.9 %all-to-all-start.3 = ((bf16[32,16,1024]{2,1,0:T(8,128)(2,1)}), bf16[32,16,1024]{2,1,0:T(8,128)(2,1)S(1)}, u32[]{:S(2)}, u32[]{:S(2)}) async-start(bf16[32,16,1024]{2,1,0:T(8,128)(2,1)} %bitcast.32), calls=%async_computation.3 | async-start | bytes 2097152 | tf_op jit(solution)/shard_map/all_to_all | solution.py:478
  100.3 6.2 %collective-permute-done.8 = bf16[400,1024]{1,0:T(8,128)(2,1)} collective-permute-done((bf16[400,1024]{1,0:T(8,128)(2,1)}, bf16[400,1024]{1,0:T(8,128)(2,1)}, u32[]{:S(2)}, u32[]{:S(2)}) %collective-permute-start.8) | collective-permute-done | bytes 819232 | tf_op jit(solution)/shard_map/ppermute | solution.py:458
  106.5 2.7 collective-permute-start.11
  109.2 8.1 %all-to-all-done.3 = bf16[32,16,1024]{2,1,0:T(8,128)(2,1)S(1)} async-done(((bf16[32,16,1024]{2,1,0:T(8,128)(2,1)}), bf16[32,16,1024]{2,1,0:T(8,128)(2,1)S(1)}, u32[]{:S(2)}, u32[]{:S(2)}) %all-to-all-start.3) | async-done | bytes 1048608 | tf_op jit(solution)/shard_map/all_to_all | solution.py:478
  117.3 3.4 %collective-permute-start.14 = (bf16[512,1024]{1,0:T(8,128)(2,1)S(1)}, bf16[512,1024]{1,0:T(8,128)(2,1)}, u32[]{:S(2)}, u32[]{:S(2)}) collective-permute-start(bf16[512,1024]{1,0:T(8,128)(2,1)S(1)} %bitcast.29), channel_id=1, source_target_pairs={{0,3},{1,0},{2,1},{3,2},{4,7},{5,4},{6,5},{7,6},{8,11},{9,8},{10,9... | collective-permute-start | bytes 3145736 | tf_op jit(solution)/shard_map/ppermute | solution.py:357
  120.7 1.4 convolution_convert_fusion.refs_0_
  122.1 4.9 %collective-permute-done.9.refs_1_.far_w = bf16[400,1024]{1,0:T(8,128)(2,1)S(1)} collective-permute-done((bf16[400,1024]{1,0:T(8,128)(2,1)}, bf16[400,1024]{1,0:T(8,128)(2,1)S(1)}, u32[]{:S(2)}, u32[]{:S(2)}) %collective-permute-start.9) | collective-permute-done | bytes 819232 | tf_op jit(solution)/shard_map/ppermute | solution.py:460
  128.8 10.0 %all-to-all-start.2 = ((bf16[32,16,1024]{2,1,0:T(8,128)(2,1)}), bf16[32,16,1024]{2,1,0:T(8,128)(2,1)S(1)}, u32[]{:S(2)}, u32[]{:S(2)}) async-start(bf16[32,16,1024]{2,1,0:T(8,128)(2,1)} %bitcast.26), calls=%async_computation.2 | async-start | bytes 2097152 | tf_op jit(solution)/shard_map/all_to_all | solution.py:478
  138.8 9.6 %collective-permute-done.14.right = bf16[512,1024]{1,0:T(8,128)(2,1)} collective-permute-done((bf16[512,1024]{1,0:T(8,128)(2,1)S(1)}, bf16[512,1024]{1,0:T(8,128)(2,1)}, u32[]{:S(2)}, u32[]{:S(2)}) %collective-permute-start.14) | collective-permute-done | bytes 1048608 | tf_op jit(solution)/shard_map/ppermute | solution.py:357
  149.5 3.6 %collective-permute-start.15 = (bf16[256,1024]{1,0:T(8,128)(2,1)S(1)}, bf16[256,1024]{1,0:T(8,128)(2,1)S(1)}, u32[]{:S(2)}, u32[]{:S(2)}) collective-permute-start(bf16[256,1024]{1,0:T(8,128)(2,1)S(1)} %slice.45), channel_id=1, source_target_pairs={{0,3},{1,0},{2,1},{3,2},{4,7},{5,4},{6,5},{7,6},{8,11},{9,8},{10,9... | collective-permute-start | bytes 1572872 | tf_op jit(solution)/shard_map/ppermute | solution.py:361
  157.2 7.5 %near.2 = (f32[512,768]{1,0:T(8,128)}, f32[512,1]{1,0:T(8,128)}) custom-call(s32[1]{0:T(128)} %bitcast.index, bf16[512,1024]{1,0:T(8,128)(2,1)} %bitcast.31, bf16[512,1024]{1,0:T(8,128)(2,1)} %collective-permute-done.14.right, bf16[512,1024]{1,0:T(8,128)(2,1)} %collective-permute-done.12.left, f32[4,1,1024]{2,1,0:T(1,128)} %pad_maximum_fusion.gain, ...), custom_call_target="tpu_custom_call" | custom-call | tf_op jit(solution)/shard_map/near/pallas_call | solution.py:263
  164.7 1.9 collective-permute-done.13.refs_1_.top
  167.4 1.3 collective-permute-start.17
  168.9 4.1 %far.2.own = bf16[512,384]{1,0:T(8,128)(2,1)} custom-call(s32[1]{0:T(128)} %bitcast.index, bf16[256,1024]{1,0:T(8,128)(2,1)} %copy-done.13, bf16[256,1024]{1,0:T(8,128)(2,1)} %copy-done.12, f32[512,768]{1,0:T(8,128)} %get-tuple-element.45.total, f32[512,1]{1,0:T(8,128)} %get-tuple-element.44.refs_3_.squares, f32[4,1,1024]{2,1,0:T(1,128)} %pad_maximum_fusion.gain, ...), custom_call_target="tpu_custom_call" | custom-call | tf_op jit(solution)/shard_map/far/pallas_call | solution.py:285
  173.0 2.7 collective-permute-start.18
  175.7 13.5 %collective-permute-done.17.right = bf16[512,1024]{1,0:T(8,128)(2,1)S(1)} collective-permute-done((bf16[512,1024]{1,0:T(8,128)(2,1)}, bf16[512,1024]{1,0:T(8,128)(2,1)S(1)}, u32[]{:S(2)}, u32[]{:S(2)}) %collective-permute-start.17) | collective-permute-done | bytes 1048608 | tf_op jit(solution)/shard_map/ppermute | solution.py:357
  190.1 1.9 collective-permute-done.16.left
  192.9 7.5 %collective-permute-done.19.refs_3_.left = bf16[512,384]{1,0:T(8,128)(2,1)S(1)} collective-permute-done((bf16[512,384]{1,0:T(8,128)(2,1)}, bf16[512,384]{1,0:T(8,128)(2,1)S(1)}, u32[]{:S(2)}, u32[]{:S(2)}) %collective-permute-start.19) | collective-permute-done | bytes 393248 | tf_op jit(solution)/shard_map/ppermute | solution.py:356
  202.0 2.7 collective-permute-start.21
  204.6 7.5 %near.3 = (f32[512,768]{1,0:T(8,128)}, f32[512,1]{1,0:T(8,128)}) custom-call(s32[1]{0:T(128)} %bitcast.index, bf16[512,1024]{1,0:T(8,128)(2,1)} %after.8.own, bf16[512,1024]{1,0:T(8,128)(2,1)} %copy-done.10, bf16[512,1024]{1,0:T(8,128)(2,1)} %copy-done.11, f32[4,1,1024]{2,1,0:T(1,128)} %pad_maximum_fusion.gain, bf16[2,4096,384]{2,1,0:T(8,128)(2,1)} %gate_w.7, ...), custom_call_target="tpu_custom_call" | custom-call | tf_op jit(solution)/shard_map/near/pallas_call | solution.py:263
  214.1 4.2 %far.3.rest_0_.own = bf16[512,384]{1,0:T(8,128)(2,1)} custom-call(s32[1]{0:T(128)} %bitcast.index, bf16[256,1024]{1,0:T(8,128)(2,1)} %copy-done.17, bf16[256,1024]{1,0:T(8,128)(2,1)} %copy-done.18, f32[512,768]{1,0:T(8,128)} %get-tuple-element.48.total, f32[512,1]{1,0:T(8,128)} %get-tuple-element.49.squares, f32[4,1,1024]{2,1,0:T(1,128)} %pad_maximum_fusion.gain, ...), custom_call_target="tpu_custom_call" | custom-call | tf_op jit(solution)/shard_map/far/pallas_call | solution.py:285
  218.2 2.7 collective-permute-start.22
  221.1 2.7 collective-permute-start.27
  223.8 2.5 collective-permute-done.23.left
  226.5 2.9 collective-permute-start.25
  231.2 5.2 %down.2.rest_0_ = bf16[32,2,16,1024]{3,2,1,0:T(8,128)(2,1)} custom-call(s32[1]{0:T(128)} %bitcast.index, bf16[512,384]{1,0:T(8,128)(2,1)} %far.2.own, bf16[512,384]{1,0:T(8,128)(2,1)} %copy-done.8, bf16[512,384]{1,0:T(8,128)(2,1)} %copy-done.6, bf16[256,384]{1,0:T(8,128)(2,1)} %copy-done.22, bf16[256,384]{1,0:T(8,128)(2,1)} %copy-done.24, ...), custom_call_target="tpu_custom_call" | custom-call | tf_op jit(solution)/shard_map/down/pallas_call | solution.py:336
  237.8 5.1 %down.3 = bf16[32,2,16,1024]{3,2,1,0:T(8,128)(2,1)} custom-call(s32[1]{0:T(128)} %bitcast.index, bf16[512,384]{1,0:T(8,128)(2,1)} %far.3.rest_0_.own, bf16[512,384]{1,0:T(8,128)(2,1)} %copy-done.16, bf16[512,384]{1,0:T(8,128)(2,1)} %copy-done.15, bf16[256,384]{1,0:T(8,128)(2,1)} %copy-done.21, ...), custom_call_target="tpu_custom_call", output_to_operand_aliasing={{}: (10, {})} | custom-call | tf_op jit(solution)/shard_map/down/pallas_call | solution.py:336
  242.9 43.9 %all_to_all.25 = bf16[32,32,1024]{2,1,0:T(8,128)(2,1)S(1)} all-to-all(bf16[32,32,1024]{2,1,0:T(8,128)(2,1)} %bitcast.24), channel_id=1, replica_groups=mesh['y'=4,'z'=4,'core'=2,'tensor'=4] {'y','z','core'}, dimensions={0} | all-to-all | bytes 4194304 | tf_op jit(solution)/shard_map/all_to_all | solution.py:499
  (128 shorter events, 29.9 us)
Async XLA Ops:
  7.2 43.1 %all-gather.2.cloned.1.call-start = ((), (), s32[]{:S(2)}) async-start(), calls=%async_computation.5 | async-start | bytes 2359296 | tf_op jit(solution)/shard_map/all_gather | solution.py:397
  12.2 38.1 %collective-permute-start = (bf16[784,1024]{1,0:T(8,128)(2,1)}, bf16[784,1024]{1,0:T(8,128)(2,1)S(1)}, u32[]{:S(2)}, u32[]{:S(2)}) collective-permute-start(bf16[784,1024]{1,0:T(8,128)(2,1)} %get-tuple-element.26), channel_id=1, source_target_pairs={{0,1},{1,2},{2,3},{3,0},{4,5},{5,6},{6,7},{7,4},{8,9},{9,10},{10,1... | collective-permute-start | bytes 4816904 | tf_op jit(solution)/shard_map/ppermute | solution.py:430
  14.3 36.0 %collective-permute-start.1 = (bf16[784,1024]{1,0:T(8,128)(2,1)}, bf16[784,1024]{1,0:T(8,128)(2,1)S(1)}, u32[]{:S(2)}, u32[]{:S(2)}) collective-permute-start(bf16[784,1024]{1,0:T(8,128)(2,1)} %get-tuple-element.27), channel_id=1, source_target_pairs={{0,3},{1,0},{2,1},{3,2},{4,7},{5,4},{6,5},{7,6},{8,11},{9,8},{10,9... | collective-permute-start | bytes 4816904 | tf_op jit(solution)/shard_map/ppermute | solution.py:431
  19.2 34.0 %all-to-all-start = ((bf16[32,16,1280]{2,1,0:T(8,128)(2,1)}), bf16[32,16,1280]{2,1,0:T(8,128)(2,1)}, u32[]{:S(2)}, u32[]{:S(2)}) async-start(bf16[32,16,1280]{2,1,0:T(8,128)(2,1)} %bitcast.25), calls=%async_computation | async-start | bytes 2621440 | tf_op jit(solution)/shard_map/all_to_all | solution.py:415
  28.8 3.5 %copy-start.34 = (f32[128,8]{0,1:T(8,128)S(1)}, f32[128,8]{0,1:T(8,128)}, u32[]{:S(2)}) copy-start(f32[128,8]{0,1:T(8,128)} %param.26) | copy-start | bytes 12292
  28.8 4.2 %copy-start.31 = (s32[128,8]{0,1:T(8,128)S(1)}, s32[128,8]{0,1:T(8,128)}, u32[]{:S(2)}) copy-start(s32[128,8]{0,1:T(8,128)} %param.23) | copy-start | bytes 12292
  28.8 4.9 %copy-start.32 = (s32[128,8]{0,1:T(8,128)S(1)}, s32[128,8]{0,1:T(8,128)}, u32[]{:S(2)}) copy-start(s32[128,8]{0,1:T(8,128)} %param.24) | copy-start | bytes 12292
  28.8 5.6 %copy-start.33 = (s32[128,8]{0,1:T(8,128)S(1)}, s32[128,8]{0,1:T(8,128)}, u32[]{:S(2)}) copy-start(s32[128,8]{0,1:T(8,128)} %param.25) | copy-start | bytes 12292
  57.4 5.7 %collective-permute-start.2 = (bf16[256,256]{1,0:T(8,128)(2,1)}, bf16[256,256]{1,0:T(8,128)(2,1)S(1)}, u32[]{:S(2)}, u32[]{:S(2)}) collective-permute-start(bf16[256,256]{1,0:T(8,128)(2,1)} %get-tuple-element.33), channel_id=1, source_target_pairs={{0,1},{1,2},{2,3},{3,0},{4,5},{5,6},{6,7},{7,4},{8,9},{9,10},{10,1... | collective-permute-start | bytes 393224 | tf_op jit(solution)/shard_map/ppermute | solution.py:365
  58.2 11.6 %collective-permute-start.4 = (bf16[256,256]{1,0:T(8,128)(2,1)}, bf16[256,256]{1,0:T(8,128)(2,1)S(1)}, u32[]{:S(2)}, u32[]{:S(2)}) collective-permute-start(bf16[256,256]{1,0:T(8,128)(2,1)} %get-tuple-element.34), channel_id=1, source_target_pairs={{0,1},{1,2},{2,3},{3,0},{4,5},{5,6},{6,7},{7,4},{8,9},{9,10},{10,1... | collective-permute-start | bytes 393224 | tf_op jit(solution)/shard_map/ppermute | solution.py:367
  59.4 10.4 %collective-permute-start.5 = (bf16[256,256]{1,0:T(8,128)(2,1)}, bf16[256,256]{1,0:T(8,128)(2,1)S(1)}, u32[]{:S(2)}, u32[]{:S(2)}) collective-permute-start(bf16[256,256]{1,0:T(8,128)(2,1)} %get-tuple-element.35), channel_id=1, source_target_pairs={{0,3},{1,0},{2,1},{3,2},{4,7},{5,4},{6,5},{7,6},{8,11},{9,8},{10,9... | collective-permute-start | bytes 393224 | tf_op jit(solution)/shard_map/ppermute | solution.py:368
  60.8 5.4 %collective-permute-start.6 = (bf16[256,256]{1,0:T(8,128)(2,1)}, bf16[256,256]{1,0:T(8,128)(2,1)S(1)}, u32[]{:S(2)}, u32[]{:S(2)}) collective-permute-start(bf16[256,256]{1,0:T(8,128)(2,1)} %get-tuple-element.37), channel_id=1, source_target_pairs={{0,3},{1,0},{2,1},{3,2},{4,7},{5,4},{6,5},{7,6},{8,11},{9,8},{10,9... | collective-permute-start | bytes 393224 | tf_op jit(solution)/shard_map/ppermute | solution.py:366
  64.0 5.8 %collective-permute-start.3 = (bf16[256,256]{1,0:T(8,128)(2,1)S(1)}, bf16[256,256]{1,0:T(8,128)(2,1)S(1)}, u32[]{:S(2)}, u32[]{:S(2)}) collective-permute-start(bf16[256,256]{1,0:T(8,128)(2,1)S(1)} %add_convert_fusion.1), channel_id=1, source_target_pairs={{0,1},{1,2},{2,3},{3,0},{4,5},{5,6},{6,7},{7,4},{8,9},{9,10},{10,1... | collective-permute-start | bytes 393224 | tf_op jit(solution)/shard_map/ppermute | solution.py:371
  67.2 4.5 %collective-permute-start.7 = (bf16[256,256]{1,0:T(8,128)(2,1)S(1)}, bf16[256,256]{1,0:T(8,128)(2,1)S(1)}, u32[]{:S(2)}, u32[]{:S(2)}) collective-permute-start(bf16[256,256]{1,0:T(8,128)(2,1)S(1)} %add_convert_fusion), channel_id=1, source_target_pairs={{0,3},{1,0},{2,1},{3,2},{4,7},{5,4},{6,5},{7,6},{8,11},{9,8},{10,9... | collective-permute-start | bytes 393224 | tf_op jit(solution)/shard_map/ppermute | solution.py:372
  74.5 18.8 %all-to-all-start.1 = ((bf16[32,16,256]{2,1,0:T(8,128)(2,1)}), bf16[32,16,256]{2,1,0:T(8,128)(2,1)S(1)}, u32[]{:S(2)}, u32[]{:S(2)}) async-start(bf16[32,16,256]{2,1,0:T(8,128)(2,1)} %route.1.refs_2_), calls=%async_computation.1 | async-start | bytes 524288 | tf_op jit(solution)/shard_map/all_to_all | solution.py:456
  84.3 36.4 %copy-start.29 = (bf16[512,128]{1,0:T(8,128)(2,1)S(1)}, bf16[512,128]{1,0:T(8,128)(2,1)}, u32[]{:S(2)}) copy-start(bf16[512,128]{1,0:T(8,128)(2,1)} %get-tuple-element.40) | copy-start | bytes 393220
  84.3 22.2 %collective-permute-start.8 = (bf16[400,1024]{1,0:T(8,128)(2,1)}, bf16[400,1024]{1,0:T(8,128)(2,1)}, u32[]{:S(2)}, u32[]{:S(2)}) collective-permute-start(bf16[400,1024]{1,0:T(8,128)(2,1)} %get-tuple-element.41), channel_id=1, source_target_pairs={{0,1},{1,2},{2,3},{3,0},{4,5},{5,6},{6,7},{7,4},{8,9},{9,10},{10,1... | collective-permute-start | bytes 2457608 | tf_op jit(solution)/shard_map/ppermute | solution.py:458
  85.0 21.6 %collective-permute-start.10 = (bf16[400,1024]{1,0:T(8,128)(2,1)}, bf16[400,1024]{1,0:T(8,128)(2,1)}, u32[]{:S(2)}, u32[]{:S(2)}) collective-permute-start(bf16[400,1024]{1,0:T(8,128)(2,1)} %get-tuple-element.42), channel_id=1, source_target_pairs={{0,3},{1,0},{2,1},{3,2},{4,7},{5,4},{6,5},{7,6},{8,11},{9,8},{10,9... | collective-permute-start | bytes 2457608 | tf_op jit(solution)/shard_map/ppermute | solution.py:459
  96.4 24.3 %copy-start.20 = (bf16[128,1024]{1,0:T(8,128)(2,1)S(1)}, bf16[128,1024]{1,0:T(8,128)(2,1)}, u32[]{:S(2)}) copy-start(bf16[128,1024]{1,0:T(8,128)(2,1)} %get-tuple-element.24) | copy-start | bytes 786436
  96.4 20.9 %all-to-all-start.3 = ((bf16[32,16,1024]{2,1,0:T(8,128)(2,1)}), bf16[32,16,1024]{2,1,0:T(8,128)(2,1)S(1)}, u32[]{:S(2)}, u32[]{:S(2)}) async-start(bf16[32,16,1024]{2,1,0:T(8,128)(2,1)} %bitcast.32), calls=%async_computation.3 | async-start | bytes 2097152 | tf_op jit(solution)/shard_map/all_to_all | solution.py:478
  106.5 20.5 %collective-permute-start.9 = (bf16[400,1024]{1,0:T(8,128)(2,1)}, bf16[400,1024]{1,0:T(8,128)(2,1)S(1)}, u32[]{:S(2)}, u32[]{:S(2)}) collective-permute-start(bf16[400,1024]{1,0:T(8,128)(2,1)} %collective-permute-done.8), channel_id=1, source_target_pairs={{0,1},{1,2},{2,3},{3,0},{4,5},{5,6},{6,7},{7,4},{8,9},{9,10},{10,1... | collective-permute-start | bytes 2457608 | tf_op jit(solution)/shard_map/ppermute | solution.py:460
  106.5 20.5 %collective-permute-start.11 = (bf16[400,1024]{1,0:T(8,128)(2,1)}, bf16[400,1024]{1,0:T(8,128)(2,1)S(1)}, u32[]{:S(2)}, u32[]{:S(2)}) collective-permute-start(bf16[400,1024]{1,0:T(8,128)(2,1)} %collective-permute-done.10), channel_id=1, source_target_pairs={{0,3},{1,0},{2,1},{3,2},{4,7},{5,4},{6,5},{7,6},{8,11},{9,8},{10,9... | collective-permute-start | bytes 2457608 | tf_op jit(solution)/shard_map/ppermute | solution.py:461
  117.3 11.5 %copy-start.3 = (bf16[32,16,1024]{2,1,0:T(8,128)(2,1)}, bf16[32,16,1024]{2,1,0:T(8,128)(2,1)S(1)}, u32[]{:S(2)}) copy-start(bf16[32,16,1024]{2,1,0:T(8,128)(2,1)S(1)} %all-to-all-done.3) | copy-start | bytes 3145732
  117.3 31.1 %collective-permute-start.14 = (bf16[512,1024]{1,0:T(8,128)(2,1)S(1)}, bf16[512,1024]{1,0:T(8,128)(2,1)}, u32[]{:S(2)}, u32[]{:S(2)}) collective-permute-start(bf16[512,1024]{1,0:T(8,128)(2,1)S(1)} %bitcast.29), channel_id=1, source_target_pairs={{0,3},{1,0},{2,1},{3,2},{4,7},{5,4},{6,5},{7,6},{8,11},{9,8},{10,9... | collective-permute-start | bytes 3145736 | tf_op jit(solution)/shard_map/ppermute | solution.py:357
  120.7 32.4 %collective-permute-start.12 = (bf16[512,1024]{1,0:T(8,128)(2,1)S(1)}, bf16[512,1024]{1,0:T(8,128)(2,1)}, u32[]{:S(2)}, u32[]{:S(2)}) collective-permute-start(bf16[512,1024]{1,0:T(8,128)(2,1)S(1)} %bitcast.30), channel_id=1, source_target_pairs={{0,1},{1,2},{2,3},{3,0},{4,5},{5,6},{6,7},{7,4},{8,9},{9,10},{10,1... | collective-permute-start | bytes 3145736 | tf_op jit(solution)/shard_map/ppermute | solution.py:356
  128.8 27.8 %copy-start.30 = (f32[1024]{0:T(1024)S(1)}, f32[1024]{0:T(1024)}, u32[]{:S(2)}) copy-start(f32[1024]{0:T(1024)} %param.22) | copy-start | bytes 12292
  128.8 35.9 %all-to-all-start.2 = ((bf16[32,16,1024]{2,1,0:T(8,128)(2,1)}), bf16[32,16,1024]{2,1,0:T(8,128)(2,1)S(1)}, u32[]{:S(2)}, u32[]{:S(2)}) async-start(bf16[32,16,1024]{2,1,0:T(8,128)(2,1)} %bitcast.26), calls=%async_computation.2 | async-start | bytes 2097152 | tf_op jit(solution)/shard_map/all_to_all | solution.py:478
  149.5 15.2 %collective-permute-start.15 = (bf16[256,1024]{1,0:T(8,128)(2,1)S(1)}, bf16[256,1024]{1,0:T(8,128)(2,1)S(1)}, u32[]{:S(2)}, u32[]{:S(2)}) collective-permute-start(bf16[256,1024]{1,0:T(8,128)(2,1)S(1)} %slice.45), channel_id=1, source_target_pairs={{0,3},{1,0},{2,1},{3,2},{4,7},{5,4},{6,5},{7,6},{8,11},{9,8},{10,9... | collective-permute-start | bytes 1572872 | tf_op jit(solution)/shard_map/ppermute | solution.py:361
  154.2 12.5 %collective-permute-start.13 = (bf16[256,1024]{1,0:T(8,128)(2,1)S(1)}, bf16[256,1024]{1,0:T(8,128)(2,1)S(1)}, u32[]{:S(2)}, u32[]{:S(2)}) collective-permute-start(bf16[256,1024]{1,0:T(8,128)(2,1)S(1)} %slice.44), channel_id=1, source_target_pairs={{0,1},{1,2},{2,3},{3,0},{4,5},{5,6},{6,7},{7,4},{8,9},{9,10},{10,1... | collective-permute-start | bytes 1572872 | tf_op jit(solution)/shard_map/ppermute | solution.py:361
  167.4 21.7 %collective-permute-start.17 = (bf16[512,1024]{1,0:T(8,128)(2,1)}, bf16[512,1024]{1,0:T(8,128)(2,1)S(1)}, u32[]{:S(2)}, u32[]{:S(2)}) collective-permute-start(bf16[512,1024]{1,0:T(8,128)(2,1)} %after.8.own), channel_id=1, source_target_pairs={{0,3},{1,0},{2,1},{3,2},{4,7},{5,4},{6,5},{7,6},{8,11},{9,8},{10,9... | collective-permute-start | bytes 3145736 | tf_op jit(solution)/shard_map/ppermute | solution.py:357
  168.7 23.3 %collective-permute-start.16 = (bf16[512,1024]{1,0:T(8,128)(2,1)}, bf16[512,1024]{1,0:T(8,128)(2,1)S(1)}, u32[]{:S(2)}, u32[]{:S(2)}) collective-permute-start(bf16[512,1024]{1,0:T(8,128)(2,1)} %after.8.own), channel_id=1, source_target_pairs={{0,1},{1,2},{2,3},{3,0},{4,5},{5,6},{6,7},{7,4},{8,9},{9,10},{10,1... | collective-permute-start | bytes 3145736 | tf_op jit(solution)/shard_map/ppermute | solution.py:356
  173.0 27.4 %collective-permute-start.19 = (bf16[512,384]{1,0:T(8,128)(2,1)}, bf16[512,384]{1,0:T(8,128)(2,1)S(1)}, u32[]{:S(2)}, u32[]{:S(2)}) collective-permute-start(bf16[512,384]{1,0:T(8,128)(2,1)} %far.2.own), channel_id=1, source_target_pairs={{0,1},{1,2},{2,3},{3,0},{4,5},{5,6},{6,7},{7,4},{8,9},{9,10},{10,1... | collective-permute-start | bytes 1179656 | tf_op jit(solution)/shard_map/ppermute | solution.py:356
  173.0 27.4 %collective-permute-start.18 = (bf16[512,384]{1,0:T(8,128)(2,1)}, bf16[512,384]{1,0:T(8,128)(2,1)S(1)}, u32[]{:S(2)}, u32[]{:S(2)}) collective-permute-start(bf16[512,384]{1,0:T(8,128)(2,1)} %far.2.own), channel_id=1, source_target_pairs={{0,3},{1,0},{2,1},{3,2},{4,7},{5,4},{6,5},{7,6},{8,11},{9,8},{10,9... | collective-permute-start | bytes 1179656 | tf_op jit(solution)/shard_map/ppermute | solution.py:357
  189.2 15.5 %copy-start.10 = (bf16[512,1024]{1,0:T(8,128)(2,1)}, bf16[512,1024]{1,0:T(8,128)(2,1)S(1)}, u32[]{:S(2)}) copy-start(bf16[512,1024]{1,0:T(8,128)(2,1)S(1)} %collective-permute-done.17.right) | copy-start | bytes 3145732
  192.0 12.6 %copy-start.11 = (bf16[512,1024]{1,0:T(8,128)(2,1)}, bf16[512,1024]{1,0:T(8,128)(2,1)S(1)}, u32[]{:S(2)}) copy-start(bf16[512,1024]{1,0:T(8,128)(2,1)S(1)} %collective-permute-done.16.left) | copy-start | bytes 3145732
  202.0 11.1 %collective-permute-start.20 = (bf16[256,1024]{1,0:T(8,128)(2,1)}, bf16[256,1024]{1,0:T(8,128)(2,1)S(1)}, u32[]{:S(2)}, u32[]{:S(2)}) collective-permute-start(bf16[256,1024]{1,0:T(8,128)(2,1)} %get-tuple-element.46), channel_id=1, source_target_pairs={{0,1},{1,2},{2,3},{3,0},{4,5},{5,6},{6,7},{7,4},{8,9},{9,10},{10,1... | collective-permute-start | bytes 1572872 | tf_op jit(solution)/shard_map/ppermute | solution.py:361
  202.0 11.1 %collective-permute-start.21 = (bf16[256,1024]{1,0:T(8,128)(2,1)}, bf16[256,1024]{1,0:T(8,128)(2,1)S(1)}, u32[]{:S(2)}, u32[]{:S(2)}) collective-permute-start(bf16[256,1024]{1,0:T(8,128)(2,1)} %get-tuple-element.47), channel_id=1, source_target_pairs={{0,3},{1,0},{2,1},{3,2},{4,7},{5,4},{6,5},{7,6},{8,11},{9,8},{10,9... | collective-permute-start | bytes 1572872 | tf_op jit(solution)/shard_map/ppermute | solution.py:361
  214.1 6.8 %copy-start.7 = (bf16[512,384]{1,0:T(8,128)(2,1)S(1)}, bf16[512,384]{1,0:T(8,128)(2,1)}, u32[]{:S(2)}) copy-start(bf16[512,384]{1,0:T(8,128)(2,1)} %copy-done.6) | copy-start | bytes 1179652
  214.1 6.9 %copy-start.9 = (bf16[512,384]{1,0:T(8,128)(2,1)S(1)}, bf16[512,384]{1,0:T(8,128)(2,1)}, u32[]{:S(2)}) copy-start(bf16[512,384]{1,0:T(8,128)(2,1)} %copy-done.8) | copy-start | bytes 1179652
  218.2 8.0 %collective-permute-start.23 = (bf16[512,384]{1,0:T(8,128)(2,1)}, bf16[512,384]{1,0:T(8,128)(2,1)S(1)}, u32[]{:S(2)}, u32[]{:S(2)}) collective-permute-start(bf16[512,384]{1,0:T(8,128)(2,1)} %far.3.rest_0_.own), channel_id=1, source_target_pairs={{0,1},{1,2},{2,3},{3,0},{4,5},{5,6},{6,7},{7,4},{8,9},{9,10},{10,1... | collective-permute-start | bytes 1179656 | tf_op jit(solution)/shard_map/ppermute | solution.py:356
  218.2 8.2 %collective-permute-start.22 = (bf16[512,384]{1,0:T(8,128)(2,1)}, bf16[512,384]{1,0:T(8,128)(2,1)S(1)}, u32[]{:S(2)}, u32[]{:S(2)}) collective-permute-start(bf16[512,384]{1,0:T(8,128)(2,1)} %far.3.rest_0_.own), channel_id=1, source_target_pairs={{0,3},{1,0},{2,1},{3,2},{4,7},{5,4},{6,5},{7,6},{8,11},{9,8},{10,9... | collective-permute-start | bytes 1179656 | tf_op jit(solution)/shard_map/ppermute | solution.py:357
  220.9 8.9 %collective-permute-start.26 = (bf16[256,384]{1,0:T(8,128)(2,1)S(1)}, bf16[256,384]{1,0:T(8,128)(2,1)S(1)}, u32[]{:S(2)}, u32[]{:S(2)}) collective-permute-start(bf16[256,384]{1,0:T(8,128)(2,1)S(1)} %slice.53), channel_id=1, source_target_pairs={{0,1},{1,2},{2,3},{3,0},{4,5},{5,6},{6,7},{7,4},{8,9},{9,10},{10,1... | collective-permute-start | bytes 589832 | tf_op jit(solution)/shard_map/ppermute | solution.py:361
  221.1 8.8 %collective-permute-start.27 = (bf16[256,384]{1,0:T(8,128)(2,1)S(1)}, bf16[256,384]{1,0:T(8,128)(2,1)S(1)}, u32[]{:S(2)}, u32[]{:S(2)}) collective-permute-start(bf16[256,384]{1,0:T(8,128)(2,1)S(1)} %slice.54), channel_id=1, source_target_pairs={{0,3},{1,0},{2,1},{3,2},{4,7},{5,4},{6,5},{7,6},{8,11},{9,8},{10,9... | collective-permute-start | bytes 589832 | tf_op jit(solution)/shard_map/ppermute | solution.py:361
  226.3 10.1 %copy-start.15 = (bf16[512,384]{1,0:T(8,128)(2,1)}, bf16[512,384]{1,0:T(8,128)(2,1)S(1)}, u32[]{:S(2)}) copy-start(bf16[512,384]{1,0:T(8,128)(2,1)S(1)} %collective-permute-done.23.left) | copy-start | bytes 1179652
  226.3 10.1 %collective-permute-start.24 = (bf16[256,384]{1,0:T(8,128)(2,1)S(1)}, bf16[256,384]{1,0:T(8,128)(2,1)S(1)}, u32[]{:S(2)}, u32[]{:S(2)}) collective-permute-start(bf16[256,384]{1,0:T(8,128)(2,1)S(1)} %slice.51), channel_id=1, source_target_pairs={{0,1},{1,2},{2,3},{3,0},{4,5},{5,6},{6,7},{7,4},{8,9},{9,10},{10,1... | collective-permute-start | bytes 589832 | tf_op jit(solution)/shard_map/ppermute | solution.py:361
  226.4 10.0 %copy-start.16 = (bf16[512,384]{1,0:T(8,128)(2,1)}, bf16[512,384]{1,0:T(8,128)(2,1)S(1)}, u32[]{:S(2)}) copy-start(bf16[512,384]{1,0:T(8,128)(2,1)S(1)} %collective-permute-done.22.right) | copy-start | bytes 1179652
  226.5 10.0 %collective-permute-start.25 = (bf16[256,384]{1,0:T(8,128)(2,1)S(1)}, bf16[256,384]{1,0:T(8,128)(2,1)S(1)}, u32[]{:S(2)}, u32[]{:S(2)}) collective-permute-start(bf16[256,384]{1,0:T(8,128)(2,1)S(1)} %slice.52), channel_id=1, source_target_pairs={{0,3},{1,0},{2,1},{3,2},{4,7},{5,4},{6,5},{7,6},{8,11},{9,8},{10,9... | collective-permute-start | bytes 589832 | tf_op jit(solution)/shard_map/ppermute | solution.py:361
  242.9 43.9 %copy-start.19 = (bf16[128,1024]{1,0:T(8,128)(2,1)S(1)}, bf16[128,1024]{1,0:T(8,128)(2,1)}, u32[]{:S(2)}) copy-start(bf16[128,1024]{1,0:T(8,128)(2,1)} %get-tuple-element.39) | copy-start | bytes 786436
  (20 other events, 22.5 us)
Sparse Core Ops, SparseCore 0:
  9.7 40.1 all-gather.1

commit v2 on v1

--- a/solution.py
+++ b/solution.py
@@ -153,8 +153,9 @@
     index, rows, weight, far_top, far_low, right_top, right_low, left_top, left_low, mine
 ):
     def product(distance):
-        start = pl.multiple_of(((index[0] + distance) % 4) * 256, 256)
-        return jnp.dot(rows[:, :PART], weight[:, pl.ds(start, 256)], preferred_element_type=F32)
+        first = ((index[0] + distance) % 4) * 2
+        columns = jnp.concatenate([weight[first], weight[first + 1]], axis=1)
+        return jnp.dot(rows[:, :PART], columns, preferred_element_type=F32)
 
     for distance, upper, lower in ((2, far_top, far_low), (1, right_top, right_low), (3, left_top, left_low)):
         result = product(distance).astype(BF16)
@@ -394,7 +395,7 @@
     d = lax.axis_index(DP)
     x_ref = jnp.reshape(x, (1,)).astype(jnp.int32)
 
-    weight = lax.all_gather(out_weight, ("y", "core"), axis=1, tiled=True)
+    weight = lax.all_gather(out_weight, ("y", "core"), axis=0, tiled=False)
 
     sent = pl.pallas_call(
         attend_kernel,
@@ -426,11 +427,11 @@
         name="tables",
     )(routes.T, bin_slots.T, dropped.T, routes, bin_slots, dropped, route_weight)
     own_gain = norm_gain.reshape(1, PART)
-    for_right, for_left = run_columns(x_ref, down_weight, own_gain, ((1, 0), (3, 0)), 2)
-    left_w = lax.ppermute(for_right, "tensor", RIGHT)
-    right_w = lax.ppermute(for_left, "tensor", LEFT)
-    far0, far1 = run_columns(x_ref, down_weight, own_gain, ((2, 0), (2, 1)), 1, sent)
-    (weight,) = after((weight,), left_w, right_w, far0, far1, send0)
+    far0, far1 = run_columns(x_ref, down_weight, own_gain, ((2, 0), (2, 1)), 1)
+    far_w0 = lax.ppermute(lax.ppermute(far0, "tensor", RIGHT), "tensor", RIGHT)
+    far_w1 = lax.ppermute(lax.ppermute(far1, "tensor", LEFT), "tensor", LEFT)
+    for_right, for_left = run_columns(x_ref, down_weight, own_gain, ((1, 0), (3, 0)), 2, sent)
+    (weight,) = after((weight,), far_w0, far_w1, for_right, for_left, send0)
 
     half = jax.ShapeDtypeStruct((256, 256), BF16)
     *partial, mine = pl.pallas_call(
@@ -454,11 +455,9 @@
         name="route",
     )(move_plan, mine, *sums)
     landed = lax.all_to_all(onward, DP, 0, 0, tiled=True)
-    far0, far1 = after((far0, far1), onward)
-    far_w0 = lax.ppermute(far0, "tensor", RIGHT)
-    far_w1 = lax.ppermute(far1, "tensor", LEFT)
-    far_w0 = lax.ppermute(far_w0, "tensor", RIGHT)
-    far_w1 = lax.ppermute(far_w1, "tensor", LEFT)
+    for_right, for_left = after((for_right, for_left), onward)
+    left_w = lax.ppermute(for_right, "tensor", RIGHT)
+    right_w = lax.ppermute(for_left, "tensor", LEFT)
 
     stream, bins0 = pl.pallas_call(
         stream_kernel,
@@ -477,8 +476,7 @@
     def exchange(rows):
         return lax.all_to_all(rows.reshape(32, CAP, PART), DP, 0, 0, tiled=True).reshape(BINS, PART)
 
-    held0 = exchange(bins0)
-    (bins1,) = after((bins1,), far_w0, far_w1)
+    (held0,) = after((exchange(bins0),), left_w, right_w)
 
     def whole_gain(rows):
         return jnp.sum(rows[-16:].astype(F32), axis=0, keepdims=True)
@@ -489,12 +487,13 @@
     partial0 = run_near(x_ref, 0, (held0, right0, left0), gains, *weights)
     (held1,) = after((exchange(bins1),), top0, low0, partial0[1])
     hidden0 = run_far(x_ref, 0, (top0, low0), partial0, gains, *weights)
+    right1, left1, top1, low1 = ring_gather(held1, done=(hidden0,))
+    partial1 = run_near(x_ref, 1, (held1, right1, left1), gains, *weights)
+    (hidden0,) = after((hidden0,), partial1[1])
     units0 = ring_gather(hidden0)
-    right1, left1, top1, low1 = ring_gather(held1, done=units0[:2])
-    partial1 = run_near(x_ref, 1, (held1, right1, left1), gains, *weights)
     hidden1 = run_far(x_ref, 1, (top1, low1), partial1, gains, *weights)
     units1 = ring_gather(hidden1)
-    back = run_down(x_ref, 0, (hidden0, *units0), down_weight, right_w, left_w, far_w0, hidden1)
+    back = run_down(x_ref, 0, (hidden0, *units0), down_weight, right_w, left_w, far_w0)
     back = run_down(x_ref, 1, (hidden1, *units1), down_weight, right_w, left_w, far_w1, into=back)
     back = lax.all_to_all(back.reshape(32, 2 * CAP, PART), DP, 0, 0, tiled=True)
     result = jnp.dot(mix, back.reshape(2 * BINS, PART), preferred_element_type=F32)

time: 296 us -> 288 us (0.973)
  blocking collectives: 43.9 us -> 82.1 us
  starting transfers between devices: 72 us -> 49.5 us
  waiting for transfers between devices: 82.5 us -> 60.6 us
  local copies, waits for them, and re-layouts: 17.8 us -> 14.8 us
    all_to_all x0 -> x2, blocking collectives: none -> 44.8 us  [the longest x1 23.3 us: per_device(): landed = lax.all_to_all(onward, DP, 0, 0, tiled=True)]
    ppermute x1, waiting for transfers between devices: 11.7 us -> 0.01 us  [per_device(): left_w = lax.ppermute(for_right, 'tensor', RIGHT)]
    ppermute x4, waiting for transfers between devices: 23.1 us -> 33.6 us  [ring_gather(): right = lax.ppermute(block, axis, LEFT)]
    all_to_all x1 -> x0, starting transfers between devices: 9.77 us -> none  [per_device(): landed = lax.all_to_all(onward, DP, 0, 0, tiled=True)]
    all_to_all x2 -> x1, starting transfers between devices: 13.9 us -> 4.42 us  [exchange(): lax.all_to_all(rows.reshape(32, CAP, PART), DP, 0, 0, tiled=True)]
    all_to_all x2 -> x1, waiting for transfers between devices: 8.09 us -> 0.01 us  [exchange(): lax.all_to_all(rows.reshape(32, CAP, PART), DP, 0, 0, tiled=True)]
    all_to_all x1, blocking collectives: 43.9 us -> 37.4 us  [per_device(): back = lax.all_to_all(back.reshape(32, 2 * CAP, PART), DP, 0, 0, tiled=True)]
    all_to_all x1 -> x0, waiting for transfers between devices: 5.44 us -> none  [per_device(): landed = lax.all_to_all(onward, DP, 0, 0, tiled=True)]
  transfers between devices with their start and end apart: 33 -> 31, of which waited for: 17 -> 13; matrix products, arithmetic and copies ran while one was open for 4% -> 4% of each run, Pallas kernels for 14% -> 16%
where the time goes in v2:
time: 288 us; the launch traced here: 286 us
  blocking collectives  82.1 us (29%)
  waiting for transfers between devices  60.6 us (21%)
  Pallas kernels  56.5 us (20%)
  starting transfers between devices  49.5 us (17%)
  local copies, waits for them, and re-layouts  14.8 us (5%)
  between operations  14.4 us (5%)
  other arithmetic  4.82 us (2%)
  matrix products  3.47 us (1%)
    all_to_all x1, blocking collectives, per_device(): back = lax.all_to_all(back.reshape(32, 2 * CAP, PART), DP, 0, 0, tiled=True)  37.4 us
    ppermute x4, waiting for transfers between devices, ring_gather(): right = lax.ppermute(block, axis, LEFT)  33.6 us
    all_to_all x1, blocking collectives, per_device(): landed = lax.all_to_all(onward, DP, 0, 0, tiled=True)  23.3 us
    all_to_all x1, blocking collectives, exchange(): lax.all_to_all(rows.reshape(32, CAP, PART), DP, 0, 0, tiled=True)  21.5 us
    pallas_call x2, Pallas kernels, run_near(): pl.pallas_call(near_kernel, grid_spec=pltpu.PrefetchScalarGridSpec(num_sc...  15 us
    ppermute x4, starting transfers between devices, ring_gather(): lax.ppermute(lower, axis, LEFT)  11.2 us
    unnamed x68, local copies, waits for them, and re-layouts  11.1 us
    ppermute x2, waiting for transfers between devices, per_device(): far_w0 = lax.ppermute(lax.ppermute(far0, 'tensor', RIGHT), 'tensor', RIGHT)  10.9 us
  transfers between devices with their start and end apart: 31, of which 13 were waited for; matrix products, arithmetic and copies ran while one was open for 4% of the time, Pallas kernels for 16%

profile of v2, /device:TPU:1, one launch (start us, length us, event | category | flops | bytes accessed | tf_op | source)
XLA Modules:
  0.0 286.3 jit_solution(2424006778407171842)
XLA Ops:
  7.9 3.3 %columns.2 = (bf16[400,1024]{1,0:T(8,128)(2,1)}, bf16[400,1024]{1,0:T(8,128)(2,1)}) custom-call(s32[1]{0:T(128)} %bitcast.index, bf16[2,384,4096]{2,1,0:T(8,128)(2,1)} %own_w.3, f32[1,1024]{1,0:T(1,128)} %bitcast.34), custom_call_target="tpu_custom_call" | custom-call | tf_op jit(solution)/shard_map/columns/pallas_call | solution.py:140
  11.2 2.1 collective-permute-start
  13.3 1.4 collective-permute-start.2
  14.6 3.5 %attend.1.rest_0_ = bf16[4,4,2,16,1280]{4,3,2,1,0:T(8,128)(2,1)} custom-call(s32[1]{0:T(128)} %bitcast.1.index, s32[4,64]{1,0:T(4,128)} %bitcast.43, bf16[128,1024]{1,0:T(8,128)(2,1)} %queries_in.1, bf16[128,128]{1,0:T(8,128)(2,1)} %keys_in.1, bf16[128,128]{1,0:T(8,128)(2,1)} %values_in.1, bf16[128,1024]{1,0:T(8,128)(2,1)} %residual_in.1), custom_call_target="tpu_custom_call" | custom-call | tf_op jit(solution)/shard_map/attend/pallas_call | solution.py:400
  18.2 9.5 %all-to-all-start = ((bf16[32,16,1280]{2,1,0:T(8,128)(2,1)}), bf16[32,16,1280]{2,1,0:T(8,128)(2,1)S(1)}, u32[]{:S(2)}, u32[]{:S(2)}) async-start(bf16[32,16,1280]{2,1,0:T(8,128)(2,1)} %bitcast.26), calls=%async_computation | async-start | bytes 2621440 | tf_op jit(solution)/shard_map/all_to_all | solution.py:416
  27.7 4.7 %collective-permute-done = bf16[400,1024]{1,0:T(8,128)(2,1)} collective-permute-done((bf16[400,1024]{1,0:T(8,128)(2,1)}, bf16[400,1024]{1,0:T(8,128)(2,1)}, u32[]{:S(2)}, u32[]{:S(2)}) %collective-permute-start) | collective-permute-done | bytes 819232 | tf_op jit(solution)/shard_map/ppermute | solution.py:431
  32.7 2.4 collective-permute-start.3
  35.1 4.3 %columns.3 = (bf16[784,1024]{1,0:T(8,128)(2,1)}, bf16[784,1024]{1,0:T(8,128)(2,1)}) custom-call(s32[1]{0:T(128)} %bitcast.index, bf16[2,384,4096]{2,1,0:T(8,128)(2,1)} %own_w.3, f32[1,1024]{1,0:T(1,128)} %bitcast.35, bf16[4,4,2,16,1280]{4,3,2,1,0:T(8,128)(2,1)} %attend.1.rest_0_), custom_call_target="tpu_custom_call" | custom-call | tf_op jit(solution)/shard_map/columns/pallas_call | solution.py:140
  42.3 3.4 %tables.1 = (bf16[512,128]{1,0:T(8,128)(2,1)}, bf16[512,128]{1,0:T(8,128)(2,1)}, bf16[128,1024]{1,0:T(8,128)(2,1)}) custom-call(s32[8,128]{1,0:T(8,128)} %bitcast.37, s32[8,128]{1,0:T(8,128)} %bitcast.38, s32[8,128]{1,0:T(8,128)} %bitcast.39, s32[128,8]{1,0:T(8,128)} %copy.26.routes, s32[128,8]{1,0:T(8,128)} %copy.27.slots, s32[128,8]{1,0:T(8,128)} %copy.28.dropped, ...), custom_call_target="tpu_custom_call" | custom-call | tf_op jit(solution)/shard_map/tables/pallas_call | solution.py:419
  45.7 6.2 %collective-permute-done.1.refs_1_.far_w = bf16[400,1024]{1,0:T(8,128)(2,1)S(1)} collective-permute-done((bf16[400,1024]{1,0:T(8,128)(2,1)}, bf16[400,1024]{1,0:T(8,128)(2,1)S(1)}, u32[]{:S(2)}, u32[]{:S(2)}) %collective-permute-start.1) | collective-permute-done | bytes 819232 | tf_op jit(solution)/shard_map/ppermute | solution.py:431
  53.0 1.1 copy-done.3
  54.1 4.1 %project.1 = (bf16[256,256]{1,0:T(8,128)(2,1)}, bf16[256,256]{1,0:T(8,128)(2,1)}, bf16[256,256]{1,0:T(8,128)(2,1)}, bf16[256,256]{1,0:T(8,128)(2,1)}, bf16[256,2...) custom-call(s32[1]{0:T(128)} %bitcast.index, bf16[512,1280]{1,0:T(8,128)(2,1)} %bitcast.31, ...), custom_call_target="tpu_custom_call" | custom-call | tf_op jit(solution)/shard_map/project/pallas_call | solution.py:437
  59.0 1.9 collective-permute-start.7
  60.9 1.4 collective-permute-start.8
  62.3 1.1 collective-permute-done.4
  64.4 1.0 collective-permute-done.8
  66.4 2.2 collective-permute-start.9
  69.4 1.1 collective-permute-done.9.two_low
  71.2 2.1 route.1.refs_2_
  73.3 1.7 collective-permute-start.10
  75.0 1.5 collective-permute-start.11
  76.4 23.3 %all_to_all.25 = bf16[32,16,256]{2,1,0:T(8,128)(2,1)} all-to-all(bf16[32,16,256]{2,1,0:T(8,128)(2,1)S(1)} %copy-done.6), channel_id=1, replica_groups=mesh['y'=4,'z'=4,'core'=2,'tensor'=4] {'y','z','core'}, dimensions={0} | all-to-all | bytes 524288 | tf_op jit(solution)/shard_map/all_to_all | solution.py:457
  99.7 2.4 stream.1
  102.2 21.5 %all_to_all.26 = bf16[32,16,1024]{2,1,0:T(8,128)(2,1)} all-to-all(bf16[32,16,1024]{2,1,0:T(8,128)(2,1)} %bitcast.32), channel_id=1, replica_groups=mesh['y'=4,'z'=4,'core'=2,'tensor'=4] {'y','z','core'}, dimensions={0} | all-to-all | bytes 2097152 | tf_op jit(solution)/shard_map/all_to_all | solution.py:477
  123.6 1.2 copy-done
  125.3 1.7 collective-permute-start.14
  127.0 2.3 convolution_convert_fusion
  129.3 4.4 %all-to-all-start.2 = ((bf16[32,16,1024]{2,1,0:T(8,128)(2,1)}), bf16[32,16,1024]{2,1,0:T(8,128)(2,1)S(1)}, u32[]{:S(2)}, u32[]{:S(2)}) async-start(bf16[32,16,1024]{2,1,0:T(8,128)(2,1)} %bitcast.11), calls=%async_computation.2 | async-start | bytes 2097152 | tf_op jit(solution)/shard_map/all_to_all | solution.py:477
  133.8 16.4 %collective-permute-done.14.right = bf16[512,1024]{1,0:T(8,128)(2,1)S(1)} collective-permute-done((bf16[512,1024]{1,0:T(8,128)(2,1)}, bf16[512,1024]{1,0:T(8,128)(2,1)S(1)}, u32[]{:S(2)}, u32[]{:S(2)}) %collective-permute-start.14) | collective-permute-done | bytes 1048608 | tf_op jit(solution)/shard_map/ppermute | solution.py:358
  151.1 2.9 %collective-permute-start.15 = (bf16[256,1024]{1,0:T(8,128)(2,1)}, bf16[256,1024]{1,0:T(8,128)(2,1)}, u32[]{:S(2)}, u32[]{:S(2)}) collective-permute-start(bf16[256,1024]{1,0:T(8,128)(2,1)} %slice.45), channel_id=1, source_target_pairs={{0,3},{1,0},{2,1},{3,2},{4,7},{5,4},{6,5},{7,6},{8,11},{9,8},{10,9... | collective-permute-start | bytes 1572872 | tf_op jit(solution)/shard_map/ppermute | solution.py:362
  157.9 7.5 %near.2 = (f32[512,768]{1,0:T(8,128)}, f32[512,1]{1,0:T(8,128)}) custom-call(s32[1]{0:T(128)} %bitcast.index, bf16[512,1024]{1,0:T(8,128)(2,1)} %after.8.own, bf16[512,1024]{1,0:T(8,128)(2,1)} %copy-done.7, bf16[512,1024]{1,0:T(8,128)(2,1)} %copy-done.8, f32[4,1,1024]{2,1,0:T(1,128)} %pad_maximum_fusion.gain, bf16[2,4096,384]{2,1,0:T(8,128)(2,1)} %gate_w.7, ...), custom_call_target="tpu_custom_call" | custom-call | tf_op jit(solution)/shard_map/near/pallas_call | solution.py:264
  165.4 3.2 %collective-permute-done.13.refs_1_.top = bf16[256,1024]{1,0:T(8,128)(2,1)} collective-permute-done((bf16[256,1024]{1,0:T(8,128)(2,1)}, bf16[256,1024]{1,0:T(8,128)(2,1)}, u32[]{:S(2)}, u32[]{:S(2)}) %collective-permute-start.13) | collective-permute-done | bytes 524320 | tf_op jit(solution)/shard_map/ppermute | solution.py:362
  170.1 4.1 %far.2.refs_2_.refs_0_ = bf16[512,384]{1,0:T(8,128)(2,1)} custom-call(s32[1]{0:T(128)} %bitcast.index, bf16[256,1024]{1,0:T(8,128)(2,1)} %collective-permute-done.13.refs_1_.top, bf16[256,1024]{1,0:T(8,128)(2,1)} %collective-permute-done.15.refs_2_.low, f32[512,768]{1,0:T(8,128)} %get-tuple-element.45.total, f32[512,1]{1,0:T(8,128)} %get-tuple-element.44.refs_3_.squares, ...), custom_call_target="tpu_custom_call" | custom-call | tf_op jit(solution)/shard_map/far/pallas_call | solution.py:286
  174.1 17.2 %collective-permute-done.17.right = bf16[512,1024]{1,0:T(8,128)(2,1)S(1)} collective-permute-done((bf16[512,1024]{1,0:T(8,128)(2,1)}, bf16[512,1024]{1,0:T(8,128)(2,1)S(1)}, u32[]{:S(2)}, u32[]{:S(2)}) %collective-permute-start.17) | collective-permute-done | bytes 1048608 | tf_op jit(solution)/shard_map/ppermute | solution.py:358
  192.2 1.2 collective-permute-done.16.left
  194.2 2.7 collective-permute-start.19
  196.9 7.5 %near.3 = (f32[512,768]{1,0:T(8,128)}, f32[512,1]{1,0:T(8,128)}) custom-call(s32[1]{0:T(128)} %bitcast.index, bf16[512,1024]{1,0:T(8,128)(2,1)} %after.9.own, bf16[512,1024]{1,0:T(8,128)(2,1)} %copy-done.9, bf16[512,1024]{1,0:T(8,128)(2,1)} %copy-done.10, f32[4,1,1024]{2,1,0:T(1,128)} %pad_maximum_fusion.gain, bf16[2,4096,384]{2,1,0:T(8,128)(2,1)} %gate_w.7, ...), custom_call_target="tpu_custom_call" | custom-call | tf_op jit(solution)/shard_map/near/pallas_call | solution.py:264
  204.5 2.7 collective-permute-start.24
  208.2 4.1 %far.3.own = bf16[512,384]{1,0:T(8,128)(2,1)} custom-call(s32[1]{0:T(128)} %bitcast.index, bf16[256,1024]{1,0:T(8,128)(2,1)} %copy-done.15, bf16[256,1024]{1,0:T(8,128)(2,1)} %copy-done.16, f32[512,768]{1,0:T(8,128)} %get-tuple-element.48.total, f32[512,1]{1,0:T(8,128)} %get-tuple-element.49.squares.refs_1_, f32[4,1,1024]{2,1,0:T(1,128)} %pad_maximum_fusion.gain, ...), custom_call_target="tpu_custom_call" | custom-call | tf_op jit(solution)/shard_map/far/pallas_call | solution.py:286
  212.3 2.7 collective-permute-start.20
  215.4 2.7 collective-permute-start.27
  218.1 5.6 %collective-permute-done.21.left = bf16[512,384]{1,0:T(8,128)(2,1)S(1)} collective-permute-done((bf16[512,384]{1,0:T(8,128)(2,1)}, bf16[512,384]{1,0:T(8,128)(2,1)S(1)}, u32[]{:S(2)}, u32[]{:S(2)}) %collective-permute-start.21) | collective-permute-done | bytes 393248 | tf_op jit(solution)/shard_map/ppermute | solution.py:357
  223.9 2.9 %collective-permute-start.23 = (bf16[256,384]{1,0:T(8,128)(2,1)S(1)}, bf16[256,384]{1,0:T(8,128)(2,1)S(1)}, u32[]{:S(2)}, u32[]{:S(2)}) collective-permute-start(bf16[256,384]{1,0:T(8,128)(2,1)S(1)} %slice.52), channel_id=1, source_target_pairs={{0,3},{1,0},{2,1},{3,2},{4,7},{5,4},{6,5},{7,6},{8,11},{9,8},{10,9... | collective-permute-start | bytes 589832 | tf_op jit(solution)/shard_map/ppermute | solution.py:362
  226.8 1.1 collective-permute-done.26.top
  229.3 5.1 %down.2.rest_0_ = bf16[32,2,16,1024]{3,2,1,0:T(8,128)(2,1)} custom-call(s32[1]{0:T(128)} %bitcast.index, bf16[512,384]{1,0:T(8,128)(2,1)} %after.11.own, bf16[512,384]{1,0:T(8,128)(2,1)} %copy-done.12, bf16[512,384]{1,0:T(8,128)(2,1)} %copy-done.11, bf16[256,384]{1,0:T(8,128)(2,1)} %copy-done.21, bf16[256,384]{1,0:T(8,128)(2,1)} %copy-done.22, ...), custom_call_target="tpu_custom_call" | custom-call | tf_op jit(solution)/shard_map/down/pallas_call | solution.py:337
  235.8 5.1 %down.3 = bf16[32,2,16,1024]{3,2,1,0:T(8,128)(2,1)} custom-call(s32[1]{0:T(128)} %bitcast.index, bf16[512,384]{1,0:T(8,128)(2,1)} %far.3.own, bf16[512,384]{1,0:T(8,128)(2,1)} %copy-done.14, bf16[512,384]{1,0:T(8,128)(2,1)} %copy-done.13, bf16[256,384]{1,0:T(8,128)(2,1)} %copy-done.19, bf16[256,384]{1,0:T(8,128)(2,1)} %copy-done.20, ...), custom_call_target="tpu_custom_call", output_to_operand_aliasing={{}: (10, {})} | custom-call | tf_op jit(solution)/shard_map/down/pallas_call | solution.py:337
  241.0 37.4 %all_to_all.27 = bf16[32,32,1024]{2,1,0:T(8,128)(2,1)S(1)} all-to-all(bf16[32,32,1024]{2,1,0:T(8,128)(2,1)} %bitcast.25), channel_id=1, replica_groups=mesh['y'=4,'z'=4,'core'=2,'tensor'=4] {'y','z','core'}, dimensions={0} | all-to-all | bytes 4194304 | tf_op jit(solution)/shard_map/all_to_all | solution.py:498
  278.3 1.1 convolution_convert_fusion.1
  (121 shorter events, 22.3 us)
Async XLA Ops:
  7.2 44.7 %all-gather.3.cloned.1.call-start = ((), (), s32[]{:S(2)}) async-start(), calls=%async_computation.5 | async-start | bytes 2359296 | tf_op jit(solution)/shard_map/all_gather | solution.py:398
  11.2 21.2 %collective-permute-start = (bf16[400,1024]{1,0:T(8,128)(2,1)}, bf16[400,1024]{1,0:T(8,128)(2,1)}, u32[]{:S(2)}, u32[]{:S(2)}) collective-permute-start(bf16[400,1024]{1,0:T(8,128)(2,1)} %get-tuple-element.26), channel_id=1, source_target_pairs={{0,1},{1,2},{2,3},{3,0},{4,5},{5,6},{6,7},{7,4},{8,9},{9,10},{10,1... | collective-permute-start | bytes 2457608 | tf_op jit(solution)/shard_map/ppermute | solution.py:431
  13.3 19.4 %collective-permute-start.2 = (bf16[400,1024]{1,0:T(8,128)(2,1)}, bf16[400,1024]{1,0:T(8,128)(2,1)}, u32[]{:S(2)}, u32[]{:S(2)}) collective-permute-start(bf16[400,1024]{1,0:T(8,128)(2,1)} %get-tuple-element.27), channel_id=1, source_target_pairs={{0,3},{1,0},{2,1},{3,2},{4,7},{5,4},{6,5},{7,6},{8,11},{9,8},{10,9... | collective-permute-start | bytes 2457608 | tf_op jit(solution)/shard_map/ppermute | solution.py:432
  18.2 34.9 %all-to-all-start = ((bf16[32,16,1280]{2,1,0:T(8,128)(2,1)}), bf16[32,16,1280]{2,1,0:T(8,128)(2,1)S(1)}, u32[]{:S(2)}, u32[]{:S(2)}) async-start(bf16[32,16,1280]{2,1,0:T(8,128)(2,1)} %bitcast.26), calls=%async_computation | async-start | bytes 2621440 | tf_op jit(solution)/shard_map/all_to_all | solution.py:416
  27.6 11.7 %copy-start.31 = (f32[128,8]{0,1:T(8,128)S(1)}, f32[128,8]{0,1:T(8,128)}, u32[]{:S(2)}) copy-start(f32[128,8]{0,1:T(8,128)} %param.26) | copy-start | bytes 12292
  27.6 12.5 %copy-start.28 = (s32[128,8]{0,1:T(8,128)S(1)}, s32[128,8]{0,1:T(8,128)}, u32[]{:S(2)}) copy-start(s32[128,8]{0,1:T(8,128)} %param.23) | copy-start | bytes 12292
  27.6 13.2 %copy-start.29 = (s32[128,8]{0,1:T(8,128)S(1)}, s32[128,8]{0,1:T(8,128)}, u32[]{:S(2)}) copy-start(s32[128,8]{0,1:T(8,128)} %param.24) | copy-start | bytes 12292
  27.7 13.9 %copy-start.30 = (s32[128,8]{0,1:T(8,128)S(1)}, s32[128,8]{0,1:T(8,128)}, u32[]{:S(2)}) copy-start(s32[128,8]{0,1:T(8,128)} %param.25) | copy-start | bytes 12292
  32.4 19.5 %collective-permute-start.1 = (bf16[400,1024]{1,0:T(8,128)(2,1)}, bf16[400,1024]{1,0:T(8,128)(2,1)S(1)}, u32[]{:S(2)}, u32[]{:S(2)}) collective-permute-start(bf16[400,1024]{1,0:T(8,128)(2,1)} %collective-permute-done), channel_id=1, source_target_pairs={{0,1},{1,2},{2,3},{3,0},{4,5},{5,6},{6,7},{7,4},{8,9},{9,10},{10,1... | collective-permute-start | bytes 2457608 | tf_op jit(solution)/shard_map/ppermute | solution.py:431
  32.7 19.2 %collective-permute-start.3 = (bf16[400,1024]{1,0:T(8,128)(2,1)}, bf16[400,1024]{1,0:T(8,128)(2,1)S(1)}, u32[]{:S(2)}, u32[]{:S(2)}) collective-permute-start(bf16[400,1024]{1,0:T(8,128)(2,1)} %collective-permute-done.2), channel_id=1, source_target_pairs={{0,3},{1,0},{2,1},{3,2},{4,7},{5,4},{6,5},{7,6},{8,11},{9,8},{10,9... | collective-permute-start | bytes 2457608 | tf_op jit(solution)/shard_map/ppermute | solution.py:432
  58.2 5.2 %collective-permute-start.4 = (bf16[256,256]{1,0:T(8,128)(2,1)}, bf16[256,256]{1,0:T(8,128)(2,1)S(1)}, u32[]{:S(2)}, u32[]{:S(2)}) collective-permute-start(bf16[256,256]{1,0:T(8,128)(2,1)} %get-tuple-element.33), channel_id=1, source_target_pairs={{0,1},{1,2},{2,3},{3,0},{4,5},{5,6},{6,7},{7,4},{8,9},{9,10},{10,1... | collective-permute-start | bytes 393224 | tf_op jit(solution)/shard_map/ppermute | solution.py:366
  58.2 10.4 %collective-permute-start.6 = (bf16[256,256]{1,0:T(8,128)(2,1)}, bf16[256,256]{1,0:T(8,128)(2,1)S(1)}, u32[]{:S(2)}, u32[]{:S(2)}) collective-permute-start(bf16[256,256]{1,0:T(8,128)(2,1)} %get-tuple-element.34), channel_id=1, source_target_pairs={{0,1},{1,2},{2,3},{3,0},{4,5},{5,6},{6,7},{7,4},{8,9},{9,10},{10,1... | collective-permute-start | bytes 393224 | tf_op jit(solution)/shard_map/ppermute | solution.py:368
  59.0 9.6 %collective-permute-start.7 = (bf16[256,256]{1,0:T(8,128)(2,1)}, bf16[256,256]{1,0:T(8,128)(2,1)S(1)}, u32[]{:S(2)}, u32[]{:S(2)}) collective-permute-start(bf16[256,256]{1,0:T(8,128)(2,1)} %get-tuple-element.35), channel_id=1, source_target_pairs={{0,3},{1,0},{2,1},{3,2},{4,7},{5,4},{6,5},{7,6},{8,11},{9,8},{10,9... | collective-permute-start | bytes 393224 | tf_op jit(solution)/shard_map/ppermute | solution.py:369
  60.9 4.6 %collective-permute-start.8 = (bf16[256,256]{1,0:T(8,128)(2,1)}, bf16[256,256]{1,0:T(8,128)(2,1)S(1)}, u32[]{:S(2)}, u32[]{:S(2)}) collective-permute-start(bf16[256,256]{1,0:T(8,128)(2,1)} %get-tuple-element.37), channel_id=1, source_target_pairs={{0,3},{1,0},{2,1},{3,2},{4,7},{5,4},{6,5},{7,6},{8,11},{9,8},{10,9... | collective-permute-start | bytes 393224 | tf_op jit(solution)/shard_map/ppermute | solution.py:367
  64.3 5.1 %collective-permute-start.5 = (bf16[256,256]{1,0:T(8,128)(2,1)S(1)}, bf16[256,256]{1,0:T(8,128)(2,1)S(1)}, u32[]{:S(2)}, u32[]{:S(2)}) collective-permute-start(bf16[256,256]{1,0:T(8,128)(2,1)S(1)} %add_convert_fusion.1), channel_id=1, source_target_pairs={{0,1},{1,2},{2,3},{3,0},{4,5},{5,6},{6,7},{7,4},{8,9},{9,10},{10,1... | collective-permute-start | bytes 393224 | tf_op jit(solution)/shard_map/ppermute | solution.py:372
  66.4 4.1 %collective-permute-start.9 = (bf16[256,256]{1,0:T(8,128)(2,1)S(1)}, bf16[256,256]{1,0:T(8,128)(2,1)S(1)}, u32[]{:S(2)}, u32[]{:S(2)}) collective-permute-start(bf16[256,256]{1,0:T(8,128)(2,1)S(1)} %add_convert_fusion), channel_id=1, source_target_pairs={{0,3},{1,0},{2,1},{3,2},{4,7},{5,4},{6,5},{7,6},{8,11},{9,8},{10,9... | collective-permute-start | bytes 393224 | tf_op jit(solution)/shard_map/ppermute | solution.py:373
  68.6 1.9 copy-start.23
  73.3 3.2 %copy-start.6 = (bf16[32,16,256]{2,1,0:T(8,128)(2,1)S(1)}, bf16[32,16,256]{2,1,0:T(8,128)(2,1)}, u32[]{:S(2)}) copy-start(bf16[32,16,256]{2,1,0:T(8,128)(2,1)} %route.1.refs_2_) | copy-start | bytes 786436
  73.3 50.4 %collective-permute-start.10 = (bf16[784,1024]{1,0:T(8,128)(2,1)}, bf16[784,1024]{1,0:T(8,128)(2,1)S(1)}, u32[]{:S(2)}, u32[]{:S(2)}) collective-permute-start(bf16[784,1024]{1,0:T(8,128)(2,1)} %get-tuple-element.42), channel_id=1, source_target_pairs={{0,1},{1,2},{2,3},{3,0},{4,5},{5,6},{6,7},{7,4},{8,9},{9,10},{10,1... | collective-permute-start | bytes 4816904 | tf_op jit(solution)/shard_map/ppermute | solution.py:459
  75.0 48.7 %collective-permute-start.11 = (bf16[784,1024]{1,0:T(8,128)(2,1)}, bf16[784,1024]{1,0:T(8,128)(2,1)S(1)}, u32[]{:S(2)}, u32[]{:S(2)}) collective-permute-start(bf16[784,1024]{1,0:T(8,128)(2,1)} %get-tuple-element.43), channel_id=1, source_target_pairs={{0,3},{1,0},{2,1},{3,2},{4,7},{5,4},{6,5},{7,6},{8,11},{9,8},{10,9... | collective-permute-start | bytes 4816904 | tf_op jit(solution)/shard_map/ppermute | solution.py:460
  125.3 24.8 %collective-permute-start.14 = (bf16[512,1024]{1,0:T(8,128)(2,1)}, bf16[512,1024]{1,0:T(8,128)(2,1)S(1)}, u32[]{:S(2)}, u32[]{:S(2)}) collective-permute-start(bf16[512,1024]{1,0:T(8,128)(2,1)} %after.8.own), channel_id=1, source_target_pairs={{0,3},{1,0},{2,1},{3,2},{4,7},{5,4},{6,5},{7,6},{8,11},{9,8},{10,9... | collective-permute-start | bytes 3145736 | tf_op jit(solution)/shard_map/ppermute | solution.py:358
  127.0 26.9 %collective-permute-start.12 = (bf16[512,1024]{1,0:T(8,128)(2,1)}, bf16[512,1024]{1,0:T(8,128)(2,1)S(1)}, u32[]{:S(2)}, u32[]{:S(2)}) collective-permute-start(bf16[512,1024]{1,0:T(8,128)(2,1)} %after.8.own), channel_id=1, source_target_pairs={{0,1},{1,2},{2,3},{3,0},{4,5},{5,6},{6,7},{7,4},{8,9},{9,10},{10,1... | collective-permute-start | bytes 3145736 | tf_op jit(solution)/shard_map/ppermute | solution.py:357
  129.3 27.9 %copy-start.27 = (f32[1024]{0:T(1024)S(1)}, f32[1024]{0:T(1024)}, u32[]{:S(2)}) copy-start(f32[1024]{0:T(1024)} %param.22) | copy-start | bytes 12292
  129.3 36.0 %all-to-all-start.2 = ((bf16[32,16,1024]{2,1,0:T(8,128)(2,1)}), bf16[32,16,1024]{2,1,0:T(8,128)(2,1)S(1)}, u32[]{:S(2)}, u32[]{:S(2)}) async-start(bf16[32,16,1024]{2,1,0:T(8,128)(2,1)} %bitcast.11), calls=%async_computation.2 | async-start | bytes 2097152 | tf_op jit(solution)/shard_map/all_to_all | solution.py:477
  150.2 7.7 %copy-start.7 = (bf16[512,1024]{1,0:T(8,128)(2,1)}, bf16[512,1024]{1,0:T(8,128)(2,1)S(1)}, u32[]{:S(2)}) copy-start(bf16[512,1024]{1,0:T(8,128)(2,1)S(1)} %collective-permute-done.14.right) | copy-start | bytes 3145732
  151.1 14.3 %collective-permute-start.15 = (bf16[256,1024]{1,0:T(8,128)(2,1)}, bf16[256,1024]{1,0:T(8,128)(2,1)}, u32[]{:S(2)}, u32[]{:S(2)}) collective-permute-start(bf16[256,1024]{1,0:T(8,128)(2,1)} %slice.45), channel_id=1, source_target_pairs={{0,3},{1,0},{2,1},{3,2},{4,7},{5,4},{6,5},{7,6},{8,11},{9,8},{10,9... | collective-permute-start | bytes 1572872 | tf_op jit(solution)/shard_map/ppermute | solution.py:362
  153.9 3.9 %copy-start.8 = (bf16[512,1024]{1,0:T(8,128)(2,1)}, bf16[512,1024]{1,0:T(8,128)(2,1)S(1)}, u32[]{:S(2)}) copy-start(bf16[512,1024]{1,0:T(8,128)(2,1)S(1)} %collective-permute-done.12.left) | copy-start | bytes 3145732
  154.9 13.7 %collective-permute-start.13 = (bf16[256,1024]{1,0:T(8,128)(2,1)}, bf16[256,1024]{1,0:T(8,128)(2,1)}, u32[]{:S(2)}, u32[]{:S(2)}) collective-permute-start(bf16[256,1024]{1,0:T(8,128)(2,1)} %slice.44), channel_id=1, source_target_pairs={{0,1},{1,2},{2,3},{3,0},{4,5},{5,6},{6,7},{7,4},{8,9},{9,10},{10,1... | collective-permute-start | bytes 1572872 | tf_op jit(solution)/shard_map/ppermute | solution.py:362
  165.4 3.2 %copy-start.2 = (bf16[32,16,1024]{2,1,0:T(8,128)(2,1)}, bf16[32,16,1024]{2,1,0:T(8,128)(2,1)S(1)}, u32[]{:S(2)}) copy-start(bf16[32,16,1024]{2,1,0:T(8,128)(2,1)S(1)} %all-to-all-done.2) | copy-start | bytes 3145732
  168.6 22.7 %collective-permute-start.17 = (bf16[512,1024]{1,0:T(8,128)(2,1)}, bf16[512,1024]{1,0:T(8,128)(2,1)S(1)}, u32[]{:S(2)}, u32[]{:S(2)}) collective-permute-start(bf16[512,1024]{1,0:T(8,128)(2,1)} %after.9.own), channel_id=1, source_target_pairs={{0,3},{1,0},{2,1},{3,2},{4,7},{5,4},{6,5},{7,6},{8,11},{9,8},{10,9... | collective-permute-start | bytes 3145736 | tf_op jit(solution)/shard_map/ppermute | solution.py:358
  169.1 24.3 %collective-permute-start.16 = (bf16[512,1024]{1,0:T(8,128)(2,1)}, bf16[512,1024]{1,0:T(8,128)(2,1)S(1)}, u32[]{:S(2)}, u32[]{:S(2)}) collective-permute-start(bf16[512,1024]{1,0:T(8,128)(2,1)} %after.9.own), channel_id=1, source_target_pairs={{0,1},{1,2},{2,3},{3,0},{4,5},{5,6},{6,7},{7,4},{8,9},{9,10},{10,1... | collective-permute-start | bytes 3145736 | tf_op jit(solution)/shard_map/ppermute | solution.py:357
  191.3 5.6 %copy-start.9 = (bf16[512,1024]{1,0:T(8,128)(2,1)}, bf16[512,1024]{1,0:T(8,128)(2,1)S(1)}, u32[]{:S(2)}) copy-start(bf16[512,1024]{1,0:T(8,128)(2,1)S(1)} %collective-permute-done.17.right) | copy-start | bytes 3145732
  193.4 3.6 %copy-start.10 = (bf16[512,1024]{1,0:T(8,128)(2,1)}, bf16[512,1024]{1,0:T(8,128)(2,1)S(1)}, u32[]{:S(2)}) copy-start(bf16[512,1024]{1,0:T(8,128)(2,1)S(1)} %collective-permute-done.16.left) | copy-start | bytes 3145732
  194.2 12.9 %collective-permute-start.18 = (bf16[256,1024]{1,0:T(8,128)(2,1)}, bf16[256,1024]{1,0:T(8,128)(2,1)S(1)}, u32[]{:S(2)}, u32[]{:S(2)}) collective-permute-start(bf16[256,1024]{1,0:T(8,128)(2,1)} %get-tuple-element.46), channel_id=1, source_target_pairs={{0,1},{1,2},{2,3},{3,0},{4,5},{5,6},{6,7},{7,4},{8,9},{9,10},{10,1... | collective-permute-start | bytes 1572872 | tf_op jit(solution)/shard_map/ppermute | solution.py:362
  194.2 12.9 %collective-permute-start.19 = (bf16[256,1024]{1,0:T(8,128)(2,1)}, bf16[256,1024]{1,0:T(8,128)(2,1)S(1)}, u32[]{:S(2)}, u32[]{:S(2)}) collective-permute-start(bf16[256,1024]{1,0:T(8,128)(2,1)} %get-tuple-element.47), channel_id=1, source_target_pairs={{0,3},{1,0},{2,1},{3,2},{4,7},{5,4},{6,5},{7,6},{8,11},{9,8},{10,9... | collective-permute-start | bytes 1572872 | tf_op jit(solution)/shard_map/ppermute | solution.py:362
  204.4 10.8 %collective-permute-start.25 = (bf16[512,384]{1,0:T(8,128)(2,1)}, bf16[512,384]{1,0:T(8,128)(2,1)S(1)}, u32[]{:S(2)}, u32[]{:S(2)}) collective-permute-start(bf16[512,384]{1,0:T(8,128)(2,1)} %after.11.own), channel_id=1, source_target_pairs={{0,1},{1,2},{2,3},{3,0},{4,5},{5,6},{6,7},{7,4},{8,9},{9,10},{10,1... | collective-permute-start | bytes 1179656 | tf_op jit(solution)/shard_map/ppermute | solution.py:357
  204.5 10.8 %collective-permute-start.24 = (bf16[512,384]{1,0:T(8,128)(2,1)}, bf16[512,384]{1,0:T(8,128)(2,1)S(1)}, u32[]{:S(2)}, u32[]{:S(2)}) collective-permute-start(bf16[512,384]{1,0:T(8,128)(2,1)} %after.11.own), channel_id=1, source_target_pairs={{0,3},{1,0},{2,1},{3,2},{4,7},{5,4},{6,5},{7,6},{8,11},{9,8},{10,9... | collective-permute-start | bytes 1179656 | tf_op jit(solution)/shard_map/ppermute | solution.py:358
  212.3 11.4 %collective-permute-start.21 = (bf16[512,384]{1,0:T(8,128)(2,1)}, bf16[512,384]{1,0:T(8,128)(2,1)S(1)}, u32[]{:S(2)}, u32[]{:S(2)}) collective-permute-start(bf16[512,384]{1,0:T(8,128)(2,1)} %far.3.own), channel_id=1, source_target_pairs={{0,1},{1,2},{2,3},{3,0},{4,5},{5,6},{6,7},{7,4},{8,9},{9,10},{10,1... | collective-permute-start | bytes 1179656 | tf_op jit(solution)/shard_map/ppermute | solution.py:357
  212.3 11.5 %collective-permute-start.20 = (bf16[512,384]{1,0:T(8,128)(2,1)}, bf16[512,384]{1,0:T(8,128)(2,1)S(1)}, u32[]{:S(2)}, u32[]{:S(2)}) collective-permute-start(bf16[512,384]{1,0:T(8,128)(2,1)} %far.3.own), channel_id=1, source_target_pairs={{0,3},{1,0},{2,1},{3,2},{4,7},{5,4},{6,5},{7,6},{8,11},{9,8},{10,9... | collective-permute-start | bytes 1179656 | tf_op jit(solution)/shard_map/ppermute | solution.py:358
  215.2 12.7 %copy-start.11 = (bf16[512,384]{1,0:T(8,128)(2,1)}, bf16[512,384]{1,0:T(8,128)(2,1)S(1)}, u32[]{:S(2)}) copy-start(bf16[512,384]{1,0:T(8,128)(2,1)S(1)} %collective-permute-done.25.left) | copy-start | bytes 1179652
  215.2 12.7 %collective-permute-start.26 = (bf16[256,384]{1,0:T(8,128)(2,1)S(1)}, bf16[256,384]{1,0:T(8,128)(2,1)S(1)}, u32[]{:S(2)}, u32[]{:S(2)}) collective-permute-start(bf16[256,384]{1,0:T(8,128)(2,1)S(1)} %slice.53), channel_id=1, source_target_pairs={{0,1},{1,2},{2,3},{3,0},{4,5},{5,6},{6,7},{7,4},{8,9},{9,10},{10,1... | collective-permute-start | bytes 589832 | tf_op jit(solution)/shard_map/ppermute | solution.py:362
  215.3 12.6 %copy-start.12 = (bf16[512,384]{1,0:T(8,128)(2,1)}, bf16[512,384]{1,0:T(8,128)(2,1)S(1)}, u32[]{:S(2)}) copy-start(bf16[512,384]{1,0:T(8,128)(2,1)S(1)} %collective-permute-done.24.right) | copy-start | bytes 1179652
  215.4 12.6 %collective-permute-start.27 = (bf16[256,384]{1,0:T(8,128)(2,1)S(1)}, bf16[256,384]{1,0:T(8,128)(2,1)S(1)}, u32[]{:S(2)}, u32[]{:S(2)}) collective-permute-start(bf16[256,384]{1,0:T(8,128)(2,1)S(1)} %slice.54), channel_id=1, source_target_pairs={{0,3},{1,0},{2,1},{3,2},{4,7},{5,4},{6,5},{7,6},{8,11},{9,8},{10,9... | collective-permute-start | bytes 589832 | tf_op jit(solution)/shard_map/ppermute | solution.py:362
  223.7 10.7 %copy-start.13 = (bf16[512,384]{1,0:T(8,128)(2,1)}, bf16[512,384]{1,0:T(8,128)(2,1)S(1)}, u32[]{:S(2)}) copy-start(bf16[512,384]{1,0:T(8,128)(2,1)S(1)} %collective-permute-done.21.left) | copy-start | bytes 1179652
  223.7 10.7 %collective-permute-start.22 = (bf16[256,384]{1,0:T(8,128)(2,1)S(1)}, bf16[256,384]{1,0:T(8,128)(2,1)S(1)}, u32[]{:S(2)}, u32[]{:S(2)}) collective-permute-start(bf16[256,384]{1,0:T(8,128)(2,1)S(1)} %slice.51), channel_id=1, source_target_pairs={{0,1},{1,2},{2,3},{3,0},{4,5},{5,6},{6,7},{7,4},{8,9},{9,10},{10,1... | collective-permute-start | bytes 589832 | tf_op jit(solution)/shard_map/ppermute | solution.py:362
  223.8 10.6 %copy-start.14 = (bf16[512,384]{1,0:T(8,128)(2,1)}, bf16[512,384]{1,0:T(8,128)(2,1)S(1)}, u32[]{:S(2)}) copy-start(bf16[512,384]{1,0:T(8,128)(2,1)S(1)} %collective-permute-done.20.right) | copy-start | bytes 1179652
  223.9 10.6 %collective-permute-start.23 = (bf16[256,384]{1,0:T(8,128)(2,1)S(1)}, bf16[256,384]{1,0:T(8,128)(2,1)S(1)}, u32[]{:S(2)}, u32[]{:S(2)}) collective-permute-start(bf16[256,384]{1,0:T(8,128)(2,1)S(1)} %slice.52), channel_id=1, source_target_pairs={{0,3},{1,0},{2,1},{3,2},{4,7},{5,4},{6,5},{7,6},{8,11},{9,8},{10,9... | collective-permute-start | bytes 589832 | tf_op jit(solution)/shard_map/ppermute | solution.py:362
  241.0 37.4 %copy-start.17 = (bf16[128,1024]{1,0:T(8,128)(2,1)S(1)}, bf16[128,1024]{1,0:T(8,128)(2,1)}, u32[]{:S(2)}) copy-start(bf16[128,1024]{1,0:T(8,128)(2,1)} %get-tuple-element.39) | copy-start | bytes 786436
  (15 other events, 15.8 us)
Sparse Core Ops, SparseCore 0:
  9.7 34.6 all-gather.2

commit v3 on v2

--- a/solution.py
+++ b/solution.py
@@ -150,7 +150,7 @@
 
 
 def project_kernel(
-    index, rows, weight, far_top, far_low, right_top, right_low, left_top, left_low, mine
+    index, rows, weight, done0, done1, far_top, far_low, right_top, right_low, left_top, left_low, mine
 ):
     def product(distance):
         first = ((index[0] + distance) % 4) * 2
@@ -431,18 +431,18 @@
     far_w0 = lax.ppermute(lax.ppermute(far0, "tensor", RIGHT), "tensor", RIGHT)
     far_w1 = lax.ppermute(lax.ppermute(far1, "tensor", LEFT), "tensor", LEFT)
     for_right, for_left = run_columns(x_ref, down_weight, own_gain, ((1, 0), (3, 0)), 2, sent)
-    (weight,) = after((weight,), far_w0, far_w1, for_right, for_left, send0)
+    (weight,) = after((weight,), for_right, for_left, send0)
 
     half = jax.ShapeDtypeStruct((256, 256), BF16)
     *partial, mine = pl.pallas_call(
         project_kernel,
         out_shape=[half] * 6 + [jax.ShapeDtypeStruct((512, 256), F32)],
-        in_specs=[whole(pltpu.SMEM)] + [whole()] * 2,
+        in_specs=[whole(pltpu.SMEM)] + [whole()] * 2 + [whole(pltpu.HBM)] * 2,
         out_specs=[whole()] * 7,
         compiler_params=params(VMEM),
         cost_estimate=NO_COST,
         name="project",
-    )(x_ref, spread, weight)
+    )(x_ref, spread, weight, far_w0, far_w1)
     sums = ring_scatter(*partial)
     onward = pl.pallas_call(
         route_kernel,

time: 288 us -> 286 us (level)
    ppermute x2, waiting for transfers between devices: 10.9 us -> 5.31 us  [per_device(): far_w0 = lax.ppermute(lax.ppermute(far0, 'tensor', RIGHT), 'tensor', RIGHT)]
    all_to_all x1, waiting for transfers between devices: 0.01 us -> 5.61 us  [per_device(): lax.all_to_all(sent.reshape(32, 16, PART + 256), DP, 0, 0, tiled=True)]
  transfers between devices with their start and end apart: 31 -> 31, of which waited for: 13 -> 14; matrix products, arithmetic and copies ran while one was open for 4% -> 4% of each run, Pallas kernels for 16% -> 16%
where the time goes in v3:
time: 286 us; the launch traced here: 285 us
  blocking collectives  81.3 us (28%)
  waiting for transfers between devices  61.2 us (21%)
  Pallas kernels  56.5 us (20%)
  starting transfers between devices  49.7 us (17%)
  between operations  14.4 us (5%)
  local copies, waits for them, and re-layouts  13.8 us (5%)
  other arithmetic  4.82 us (2%)
  matrix products  3.47 us (1%)
    all_to_all x1, blocking collectives, per_device(): back = lax.all_to_all(back.reshape(32, 2 * CAP, PART), DP, 0, 0, tiled=True)  37.4 us
    ppermute x4, waiting for transfers between devices, ring_gather(): right = lax.ppermute(block, axis, LEFT)  33.6 us
    all_to_all x1, blocking collectives, per_device(): landed = lax.all_to_all(onward, DP, 0, 0, tiled=True)  22.5 us
    all_to_all x1, blocking collectives, exchange(): lax.all_to_all(rows.reshape(32, CAP, PART), DP, 0, 0, tiled=True)  21.5 us
    pallas_call x2, Pallas kernels, run_near(): pl.pallas_call(near_kernel, grid_spec=pltpu.PrefetchScalarGridSpec(num_sc...  15 us
    ppermute x4, starting transfers between devices, ring_gather(): lax.ppermute(lower, axis, LEFT)  11.2 us
    pallas_call x2, Pallas kernels, run_down(): pl.pallas_call(functools.partial(down_kernel, local), out_shape=jax.Shape...  10.3 us
    unnamed x68, local copies, waits for them, and re-layouts  10.1 us
  transfers between devices with their start and end apart: 31, of which 14 were waited for; matrix products, arithmetic and copies ran while one was open for 4% of the time, Pallas kernels for 16%

profile of v3, /device:TPU:1, one launch (start us, length us, event | category | flops | bytes accessed | tf_op | source)
XLA Modules:
  0.0 285.3 jit_solution(3390582112653007468)
XLA Ops:
  7.9 3.3 %columns.3 = (bf16[400,1024]{1,0:T(8,128)(2,1)}, bf16[400,1024]{1,0:T(8,128)(2,1)}) custom-call(s32[1]{0:T(128)} %bitcast.index, bf16[2,384,4096]{2,1,0:T(8,128)(2,1)} %own_w.3, f32[1,1024]{1,0:T(1,128)} %bitcast.34), custom_call_target="tpu_custom_call" | custom-call | tf_op jit(solution)/shard_map/columns/pallas_call | solution.py:140
  11.2 2.1 collective-permute-start
  13.3 1.4 collective-permute-start.2
  14.6 3.5 %attend.1.rest_0_ = bf16[4,4,2,16,1280]{4,3,2,1,0:T(8,128)(2,1)} custom-call(s32[1]{0:T(128)} %bitcast.1.index, s32[4,64]{1,0:T(4,128)} %bitcast.43, bf16[128,1024]{1,0:T(8,128)(2,1)} %queries_in.1, bf16[128,128]{1,0:T(8,128)(2,1)} %keys_in.1, bf16[128,128]{1,0:T(8,128)(2,1)} %values_in.1, bf16[128,1024]{1,0:T(8,128)(2,1)} %residual_in.1), custom_call_target="tpu_custom_call" | custom-call | tf_op jit(solution)/shard_map/attend/pallas_call | solution.py:400
  18.2 9.5 %all-to-all-start = ((bf16[32,16,1280]{2,1,0:T(8,128)(2,1)}), bf16[32,16,1280]{2,1,0:T(8,128)(2,1)S(1)}, u32[]{:S(2)}, u32[]{:S(2)}) async-start(bf16[32,16,1280]{2,1,0:T(8,128)(2,1)} %bitcast.26), calls=%async_computation | async-start | bytes 2621440 | tf_op jit(solution)/shard_map/all_to_all | solution.py:416
  27.7 4.7 %collective-permute-done = bf16[400,1024]{1,0:T(8,128)(2,1)} collective-permute-done((bf16[400,1024]{1,0:T(8,128)(2,1)}, bf16[400,1024]{1,0:T(8,128)(2,1)}, u32[]{:S(2)}, u32[]{:S(2)}) %collective-permute-start) | collective-permute-done | bytes 819232 | tf_op jit(solution)/shard_map/ppermute | solution.py:431
  32.7 2.4 collective-permute-start.3
  35.1 4.3 %columns.2 = (bf16[784,1024]{1,0:T(8,128)(2,1)}, bf16[784,1024]{1,0:T(8,128)(2,1)}) custom-call(s32[1]{0:T(128)} %bitcast.index, bf16[2,384,4096]{2,1,0:T(8,128)(2,1)} %own_w.3, f32[1,1024]{1,0:T(1,128)} %bitcast.35, bf16[4,4,2,16,1280]{4,3,2,1,0:T(8,128)(2,1)} %attend.1.rest_0_), custom_call_target="tpu_custom_call" | custom-call | tf_op jit(solution)/shard_map/columns/pallas_call | solution.py:140
  42.3 3.4 %tables.1 = (bf16[512,128]{1,0:T(8,128)(2,1)}, bf16[512,128]{1,0:T(8,128)(2,1)}, bf16[128,1024]{1,0:T(8,128)(2,1)}) custom-call(s32[8,128]{1,0:T(8,128)} %bitcast.37, s32[8,128]{1,0:T(8,128)} %bitcast.38, s32[8,128]{1,0:T(8,128)} %bitcast.39, s32[128,8]{1,0:T(8,128)} %copy.26.routes, s32[128,8]{1,0:T(8,128)} %copy.27.slots, s32[128,8]{1,0:T(8,128)} %copy.28.dropped, ...), custom_call_target="tpu_custom_call" | custom-call | tf_op jit(solution)/shard_map/tables/pallas_call | solution.py:419
  45.7 5.6 %all-to-all-done = bf16[32,16,1280]{2,1,0:T(8,128)(2,1)S(1)} async-done(((bf16[32,16,1280]{2,1,0:T(8,128)(2,1)}), bf16[32,16,1280]{2,1,0:T(8,128)(2,1)S(1)}, u32[]{:S(2)}, u32[]{:S(2)}) %all-to-all-start) | async-done | bytes 1310752 | tf_op jit(solution)/shard_map/all_to_all | solution.py:416
  53.0 4.1 %project.1 = (bf16[256,256]{1,0:T(8,128)(2,1)}, bf16[256,256]{1,0:T(8,128)(2,1)}, bf16[256,256]{1,0:T(8,128)(2,1)}, bf16[256,256]{1,0:T(8,128)(2,1)}, bf16[256,2...) custom-call(s32[1]{0:T(128)} %bitcast.index, bf16[512,1280]{1,0:T(8,128)(2,1)} %bitcast.31, ...), custom_call_target="tpu_custom_call" | custom-call | tf_op jit(solution)/shard_map/project/pallas_call | solution.py:437
  57.9 1.2 collective-permute-start.6
  59.1 1.5 collective-permute-start.7
  61.2 1.1 collective-permute-done.4
  62.3 0.9 add_convert_fusion.1
  63.4 1.6 collective-permute-done.8
  65.9 2.4 collective-permute-start.9
  68.4 1.9 collective-permute-done.9.two_low
  70.9 2.1 route.1.refs_2_
  73.9 2.2 collective-permute-start.11
  76.1 22.5 %all_to_all.25 = bf16[32,16,256]{2,1,0:T(8,128)(2,1)} all-to-all(bf16[32,16,256]{2,1,0:T(8,128)(2,1)S(1)} %copy-done.6), channel_id=1, replica_groups=mesh['y'=4,'z'=4,'core'=2,'tensor'=4] {'y','z','core'}, dimensions={0} | all-to-all | bytes 524288 | tf_op jit(solution)/shard_map/all_to_all | solution.py:457
  98.7 2.4 stream.1
  101.1 21.5 %all_to_all.26 = bf16[32,16,1024]{2,1,0:T(8,128)(2,1)} all-to-all(bf16[32,16,1024]{2,1,0:T(8,128)(2,1)} %bitcast.32), channel_id=1, replica_groups=mesh['y'=4,'z'=4,'core'=2,'tensor'=4] {'y','z','core'}, dimensions={0} | all-to-all | bytes 2097152 | tf_op jit(solution)/shard_map/all_to_all | solution.py:477
  122.6 1.2 copy-done
  124.3 1.7 collective-permute-start.14
  125.9 2.3 convolution_convert_fusion
  128.3 4.4 %all-to-all-start.2 = ((bf16[32,16,1024]{2,1,0:T(8,128)(2,1)}), bf16[32,16,1024]{2,1,0:T(8,128)(2,1)S(1)}, u32[]{:S(2)}, u32[]{:S(2)}) async-start(bf16[32,16,1024]{2,1,0:T(8,128)(2,1)} %bitcast.11), calls=%async_computation.2 | async-start | bytes 2097152 | tf_op jit(solution)/shard_map/all_to_all | solution.py:477
  132.7 16.4 %collective-permute-done.14.right = bf16[512,1024]{1,0:T(8,128)(2,1)S(1)} collective-permute-done((bf16[512,1024]{1,0:T(8,128)(2,1)}, bf16[512,1024]{1,0:T(8,128)(2,1)S(1)}, u32[]{:S(2)}, u32[]{:S(2)}) %collective-permute-start.14) | collective-permute-done | bytes 1048608 | tf_op jit(solution)/shard_map/ppermute | solution.py:358
  150.0 2.9 %collective-permute-start.15 = (bf16[256,1024]{1,0:T(8,128)(2,1)}, bf16[256,1024]{1,0:T(8,128)(2,1)}, u32[]{:S(2)}, u32[]{:S(2)}) collective-permute-start(bf16[256,1024]{1,0:T(8,128)(2,1)} %slice.45), channel_id=1, source_target_pairs={{0,3},{1,0},{2,1},{3,2},{4,7},{5,4},{6,5},{7,6},{8,11},{9,8},{10,9... | collective-permute-start | bytes 1572872 | tf_op jit(solution)/shard_map/ppermute | solution.py:362
  156.8 7.5 %near.2 = (f32[512,768]{1,0:T(8,128)}, f32[512,1]{1,0:T(8,128)}) custom-call(s32[1]{0:T(128)} %bitcast.index, bf16[512,1024]{1,0:T(8,128)(2,1)} %after.8.own, bf16[512,1024]{1,0:T(8,128)(2,1)} %copy-done.7, bf16[512,1024]{1,0:T(8,128)(2,1)} %copy-done.8, f32[4,1,1024]{2,1,0:T(1,128)} %pad_maximum_fusion.gain, bf16[2,4096,384]{2,1,0:T(8,128)(2,1)} %gate_w.7, ...), custom_call_target="tpu_custom_call" | custom-call | tf_op jit(solution)/shard_map/near/pallas_call | solution.py:264
  164.3 3.2 %collective-permute-done.13.refs_1_.top = bf16[256,1024]{1,0:T(8,128)(2,1)} collective-permute-done((bf16[256,1024]{1,0:T(8,128)(2,1)}, bf16[256,1024]{1,0:T(8,128)(2,1)}, u32[]{:S(2)}, u32[]{:S(2)}) %collective-permute-start.13) | collective-permute-done | bytes 524320 | tf_op jit(solution)/shard_map/ppermute | solution.py:362
  168.0 1.0 collective-permute-start.16
  169.0 4.1 %far.2.refs_2_.refs_0_ = bf16[512,384]{1,0:T(8,128)(2,1)} custom-call(s32[1]{0:T(128)} %bitcast.index, bf16[256,1024]{1,0:T(8,128)(2,1)} %collective-permute-done.13.refs_1_.top, bf16[256,1024]{1,0:T(8,128)(2,1)} %collective-permute-done.15.refs_2_.low, f32[512,768]{1,0:T(8,128)} %get-tuple-element.45.total, f32[512,1]{1,0:T(8,128)} %get-tuple-element.44.refs_3_.squares, ...), custom_call_target="tpu_custom_call" | custom-call | tf_op jit(solution)/shard_map/far/pallas_call | solution.py:286
  173.1 17.2 %collective-permute-done.17.right = bf16[512,1024]{1,0:T(8,128)(2,1)S(1)} collective-permute-done((bf16[512,1024]{1,0:T(8,128)(2,1)}, bf16[512,1024]{1,0:T(8,128)(2,1)S(1)}, u32[]{:S(2)}, u32[]{:S(2)}) %collective-permute-start.17) | collective-permute-done | bytes 1048608 | tf_op jit(solution)/shard_map/ppermute | solution.py:358
  191.1 1.2 collective-permute-done.16.left
  193.2 2.7 collective-permute-start.19
  195.9 7.5 %near.3 = (f32[512,768]{1,0:T(8,128)}, f32[512,1]{1,0:T(8,128)}) custom-call(s32[1]{0:T(128)} %bitcast.index, bf16[512,1024]{1,0:T(8,128)(2,1)} %after.9.own, bf16[512,1024]{1,0:T(8,128)(2,1)} %copy-done.9, bf16[512,1024]{1,0:T(8,128)(2,1)} %copy-done.10, f32[4,1,1024]{2,1,0:T(1,128)} %pad_maximum_fusion.gain, bf16[2,4096,384]{2,1,0:T(8,128)(2,1)} %gate_w.7, ...), custom_call_target="tpu_custom_call" | custom-call | tf_op jit(solution)/shard_map/near/pallas_call | solution.py:264
  203.5 2.7 collective-permute-start.24
  207.1 4.1 %far.3.own = bf16[512,384]{1,0:T(8,128)(2,1)} custom-call(s32[1]{0:T(128)} %bitcast.index, bf16[256,1024]{1,0:T(8,128)(2,1)} %copy-done.15, bf16[256,1024]{1,0:T(8,128)(2,1)} %copy-done.16, f32[512,768]{1,0:T(8,128)} %get-tuple-element.48.total, f32[512,1]{1,0:T(8,128)} %get-tuple-element.49.squares.refs_1_, f32[4,1,1024]{2,1,0:T(1,128)} %pad_maximum_fusion.gain, ...), custom_call_target="tpu_custom_call" | custom-call | tf_op jit(solution)/shard_map/far/pallas_call | solution.py:286
  211.2 2.7 collective-permute-start.20
  214.3 2.7 collective-permute-start.27
  217.0 5.6 %collective-permute-done.21.left = bf16[512,384]{1,0:T(8,128)(2,1)S(1)} collective-permute-done((bf16[512,384]{1,0:T(8,128)(2,1)}, bf16[512,384]{1,0:T(8,128)(2,1)S(1)}, u32[]{:S(2)}, u32[]{:S(2)}) %collective-permute-start.21) | collective-permute-done | bytes 393248 | tf_op jit(solution)/shard_map/ppermute | solution.py:357
  222.8 2.9 %collective-permute-start.23 = (bf16[256,384]{1,0:T(8,128)(2,1)S(1)}, bf16[256,384]{1,0:T(8,128)(2,1)S(1)}, u32[]{:S(2)}, u32[]{:S(2)}) collective-permute-start(bf16[256,384]{1,0:T(8,128)(2,1)S(1)} %slice.52), channel_id=1, source_target_pairs={{0,3},{1,0},{2,1},{3,2},{4,7},{5,4},{6,5},{7,6},{8,11},{9,8},{10,9... | collective-permute-start | bytes 589832 | tf_op jit(solution)/shard_map/ppermute | solution.py:362
  225.7 1.1 collective-permute-done.26.top
  228.2 5.1 %down.2.rest_0_ = bf16[32,2,16,1024]{3,2,1,0:T(8,128)(2,1)} custom-call(s32[1]{0:T(128)} %bitcast.index, bf16[512,384]{1,0:T(8,128)(2,1)} %after.11.own, bf16[512,384]{1,0:T(8,128)(2,1)} %copy-done.12, bf16[512,384]{1,0:T(8,128)(2,1)} %copy-done.11, bf16[256,384]{1,0:T(8,128)(2,1)} %copy-done.21, bf16[256,384]{1,0:T(8,128)(2,1)} %copy-done.22, ...), custom_call_target="tpu_custom_call" | custom-call | tf_op jit(solution)/shard_map/down/pallas_call | solution.py:337
  234.7 5.1 %down.3 = bf16[32,2,16,1024]{3,2,1,0:T(8,128)(2,1)} custom-call(s32[1]{0:T(128)} %bitcast.index, bf16[512,384]{1,0:T(8,128)(2,1)} %far.3.own, bf16[512,384]{1,0:T(8,128)(2,1)} %copy-done.14, bf16[512,384]{1,0:T(8,128)(2,1)} %copy-done.13, bf16[256,384]{1,0:T(8,128)(2,1)} %copy-done.19, bf16[256,384]{1,0:T(8,128)(2,1)} %copy-done.20, ...), custom_call_target="tpu_custom_call", output_to_operand_aliasing={{}: (10, {})} | custom-call | tf_op jit(solution)/shard_map/down/pallas_call | solution.py:337
  239.9 37.4 %all_to_all.27 = bf16[32,32,1024]{2,1,0:T(8,128)(2,1)S(1)} all-to-all(bf16[32,32,1024]{2,1,0:T(8,128)(2,1)} %bitcast.25), channel_id=1, replica_groups=mesh['y'=4,'z'=4,'core'=2,'tensor'=4] {'y','z','core'}, dimensions={0} | all-to-all | bytes 4194304 | tf_op jit(solution)/shard_map/all_to_all | solution.py:498
  277.3 1.1 convolution_convert_fusion.1
  (121 shorter events, 21.7 us)
Async XLA Ops:
  7.2 38.5 %all-gather.3.cloned.1.call-start = ((), (), s32[]{:S(2)}) async-start(), calls=%async_computation.5 | async-start | bytes 2359296 | tf_op jit(solution)/shard_map/all_gather | solution.py:398
  11.2 21.2 %collective-permute-start = (bf16[400,1024]{1,0:T(8,128)(2,1)}, bf16[400,1024]{1,0:T(8,128)(2,1)}, u32[]{:S(2)}, u32[]{:S(2)}) collective-permute-start(bf16[400,1024]{1,0:T(8,128)(2,1)} %get-tuple-element.29), channel_id=1, source_target_pairs={{0,1},{1,2},{2,3},{3,0},{4,5},{5,6},{6,7},{7,4},{8,9},{9,10},{10,1... | collective-permute-start | bytes 2457608 | tf_op jit(solution)/shard_map/ppermute | solution.py:431
  13.3 19.4 %collective-permute-start.2 = (bf16[400,1024]{1,0:T(8,128)(2,1)}, bf16[400,1024]{1,0:T(8,128)(2,1)}, u32[]{:S(2)}, u32[]{:S(2)}) collective-permute-start(bf16[400,1024]{1,0:T(8,128)(2,1)} %get-tuple-element.30), channel_id=1, source_target_pairs={{0,3},{1,0},{2,1},{3,2},{4,7},{5,4},{6,5},{7,6},{8,11},{9,8},{10,9... | collective-permute-start | bytes 2457608 | tf_op jit(solution)/shard_map/ppermute | solution.py:432
  18.2 33.1 %all-to-all-start = ((bf16[32,16,1280]{2,1,0:T(8,128)(2,1)}), bf16[32,16,1280]{2,1,0:T(8,128)(2,1)S(1)}, u32[]{:S(2)}, u32[]{:S(2)}) async-start(bf16[32,16,1280]{2,1,0:T(8,128)(2,1)} %bitcast.26), calls=%async_computation | async-start | bytes 2621440 | tf_op jit(solution)/shard_map/all_to_all | solution.py:416
  27.6 11.7 %copy-start.31 = (f32[128,8]{0,1:T(8,128)S(1)}, f32[128,8]{0,1:T(8,128)}, u32[]{:S(2)}) copy-start(f32[128,8]{0,1:T(8,128)} %param.26) | copy-start | bytes 12292
  27.6 12.5 %copy-start.28 = (s32[128,8]{0,1:T(8,128)S(1)}, s32[128,8]{0,1:T(8,128)}, u32[]{:S(2)}) copy-start(s32[128,8]{0,1:T(8,128)} %param.23) | copy-start | bytes 12292
  27.6 13.2 %copy-start.29 = (s32[128,8]{0,1:T(8,128)S(1)}, s32[128,8]{0,1:T(8,128)}, u32[]{:S(2)}) copy-start(s32[128,8]{0,1:T(8,128)} %param.24) | copy-start | bytes 12292
  27.7 13.9 %copy-start.30 = (s32[128,8]{0,1:T(8,128)S(1)}, s32[128,8]{0,1:T(8,128)}, u32[]{:S(2)}) copy-start(s32[128,8]{0,1:T(8,128)} %param.25) | copy-start | bytes 12292
  32.4 19.5 %collective-permute-start.1 = (bf16[400,1024]{1,0:T(8,128)(2,1)}, bf16[400,1024]{1,0:T(8,128)(2,1)S(1)}, u32[]{:S(2)}, u32[]{:S(2)}) collective-permute-start(bf16[400,1024]{1,0:T(8,128)(2,1)} %collective-permute-done), channel_id=1, source_target_pairs={{0,1},{1,2},{2,3},{3,0},{4,5},{5,6},{6,7},{7,4},{8,9},{9,10},{10,1... | collective-permute-start | bytes 2457608 | tf_op jit(solution)/shard_map/ppermute | solution.py:431
  32.7 19.2 %collective-permute-start.3 = (bf16[400,1024]{1,0:T(8,128)(2,1)}, bf16[400,1024]{1,0:T(8,128)(2,1)S(1)}, u32[]{:S(2)}, u32[]{:S(2)}) collective-permute-start(bf16[400,1024]{1,0:T(8,128)(2,1)} %collective-permute-done.2), channel_id=1, source_target_pairs={{0,3},{1,0},{2,1},{3,2},{4,7},{5,4},{6,5},{7,6},{8,11},{9,8},{10,9... | collective-permute-start | bytes 2457608 | tf_op jit(solution)/shard_map/ppermute | solution.py:432
  57.1 5.2 %collective-permute-start.4 = (bf16[256,256]{1,0:T(8,128)(2,1)}, bf16[256,256]{1,0:T(8,128)(2,1)S(1)}, u32[]{:S(2)}, u32[]{:S(2)}) collective-permute-start(bf16[256,256]{1,0:T(8,128)(2,1)} %get-tuple-element.33), channel_id=1, source_target_pairs={{0,1},{1,2},{2,3},{3,0},{4,5},{5,6},{6,7},{7,4},{8,9},{9,10},{10,1... | collective-permute-start | bytes 393224 | tf_op jit(solution)/shard_map/ppermute | solution.py:366
  57.9 10.3 %collective-permute-start.6 = (bf16[256,256]{1,0:T(8,128)(2,1)}, bf16[256,256]{1,0:T(8,128)(2,1)S(1)}, u32[]{:S(2)}, u32[]{:S(2)}) collective-permute-start(bf16[256,256]{1,0:T(8,128)(2,1)} %get-tuple-element.34), channel_id=1, source_target_pairs={{0,1},{1,2},{2,3},{3,0},{4,5},{5,6},{6,7},{7,4},{8,9},{9,10},{10,1... | collective-permute-start | bytes 393224 | tf_op jit(solution)/shard_map/ppermute | solution.py:368
  59.1 9.1 %collective-permute-start.7 = (bf16[256,256]{1,0:T(8,128)(2,1)}, bf16[256,256]{1,0:T(8,128)(2,1)S(1)}, u32[]{:S(2)}, u32[]{:S(2)}) collective-permute-start(bf16[256,256]{1,0:T(8,128)(2,1)} %get-tuple-element.35), channel_id=1, source_target_pairs={{0,3},{1,0},{2,1},{3,2},{4,7},{5,4},{6,5},{7,6},{8,11},{9,8},{10,9... | collective-permute-start | bytes 393224 | tf_op jit(solution)/shard_map/ppermute | solution.py:369
  60.6 4.3 %collective-permute-start.8 = (bf16[256,256]{1,0:T(8,128)(2,1)}, bf16[256,256]{1,0:T(8,128)(2,1)S(1)}, u32[]{:S(2)}, u32[]{:S(2)}) collective-permute-start(bf16[256,256]{1,0:T(8,128)(2,1)} %get-tuple-element.37), channel_id=1, source_target_pairs={{0,3},{1,0},{2,1},{3,2},{4,7},{5,4},{6,5},{7,6},{8,11},{9,8},{10,9... | collective-permute-start | bytes 393224 | tf_op jit(solution)/shard_map/ppermute | solution.py:367
  63.3 5.1 %collective-permute-start.5 = (bf16[256,256]{1,0:T(8,128)(2,1)S(1)}, bf16[256,256]{1,0:T(8,128)(2,1)S(1)}, u32[]{:S(2)}, u32[]{:S(2)}) collective-permute-start(bf16[256,256]{1,0:T(8,128)(2,1)S(1)} %add_convert_fusion.1), channel_id=1, source_target_pairs={{0,1},{1,2},{2,3},{3,0},{4,5},{5,6},{6,7},{7,4},{8,9},{9,10},{10,1... | collective-permute-start | bytes 393224 | tf_op jit(solution)/shard_map/ppermute | solution.py:372
  65.9 4.3 %collective-permute-start.9 = (bf16[256,256]{1,0:T(8,128)(2,1)S(1)}, bf16[256,256]{1,0:T(8,128)(2,1)S(1)}, u32[]{:S(2)}, u32[]{:S(2)}) collective-permute-start(bf16[256,256]{1,0:T(8,128)(2,1)S(1)} %add_convert_fusion), channel_id=1, source_target_pairs={{0,3},{1,0},{2,1},{3,2},{4,7},{5,4},{6,5},{7,6},{8,11},{9,8},{10,9... | collective-permute-start | bytes 393224 | tf_op jit(solution)/shard_map/ppermute | solution.py:373
  68.3 1.9 copy-start.23
  73.0 3.2 %copy-start.6 = (bf16[32,16,256]{2,1,0:T(8,128)(2,1)S(1)}, bf16[32,16,256]{2,1,0:T(8,128)(2,1)}, u32[]{:S(2)}) copy-start(bf16[32,16,256]{2,1,0:T(8,128)(2,1)} %route.1.refs_2_) | copy-start | bytes 786436
  73.0 49.6 %collective-permute-start.10 = (bf16[784,1024]{1,0:T(8,128)(2,1)}, bf16[784,1024]{1,0:T(8,128)(2,1)S(1)}, u32[]{:S(2)}, u32[]{:S(2)}) collective-permute-start(bf16[784,1024]{1,0:T(8,128)(2,1)} %get-tuple-element.42), channel_id=1, source_target_pairs={{0,1},{1,2},{2,3},{3,0},{4,5},{5,6},{6,7},{7,4},{8,9},{9,10},{10,1... | collective-permute-start | bytes 4816904 | tf_op jit(solution)/shard_map/ppermute | solution.py:459
  73.9 48.7 %collective-permute-start.11 = (bf16[784,1024]{1,0:T(8,128)(2,1)}, bf16[784,1024]{1,0:T(8,128)(2,1)S(1)}, u32[]{:S(2)}, u32[]{:S(2)}) collective-permute-start(bf16[784,1024]{1,0:T(8,128)(2,1)} %get-tuple-element.43), channel_id=1, source_target_pairs={{0,3},{1,0},{2,1},{3,2},{4,7},{5,4},{6,5},{7,6},{8,11},{9,8},{10,9... | collective-permute-start | bytes 4816904 | tf_op jit(solution)/shard_map/ppermute | solution.py:460
  124.3 24.8 %collective-permute-start.14 = (bf16[512,1024]{1,0:T(8,128)(2,1)}, bf16[512,1024]{1,0:T(8,128)(2,1)S(1)}, u32[]{:S(2)}, u32[]{:S(2)}) collective-permute-start(bf16[512,1024]{1,0:T(8,128)(2,1)} %after.8.own), channel_id=1, source_target_pairs={{0,3},{1,0},{2,1},{3,2},{4,7},{5,4},{6,5},{7,6},{8,11},{9,8},{10,9... | collective-permute-start | bytes 3145736 | tf_op jit(solution)/shard_map/ppermute | solution.py:358
  125.9 26.9 %collective-permute-start.12 = (bf16[512,1024]{1,0:T(8,128)(2,1)}, bf16[512,1024]{1,0:T(8,128)(2,1)S(1)}, u32[]{:S(2)}, u32[]{:S(2)}) collective-permute-start(bf16[512,1024]{1,0:T(8,128)(2,1)} %after.8.own), channel_id=1, source_target_pairs={{0,1},{1,2},{2,3},{3,0},{4,5},{5,6},{6,7},{7,4},{8,9},{9,10},{10,1... | collective-permute-start | bytes 3145736 | tf_op jit(solution)/shard_map/ppermute | solution.py:357
  128.3 27.9 %copy-start.27 = (f32[1024]{0:T(1024)S(1)}, f32[1024]{0:T(1024)}, u32[]{:S(2)}) copy-start(f32[1024]{0:T(1024)} %param.22) | copy-start | bytes 12292
  128.3 36.0 %all-to-all-start.2 = ((bf16[32,16,1024]{2,1,0:T(8,128)(2,1)}), bf16[32,16,1024]{2,1,0:T(8,128)(2,1)S(1)}, u32[]{:S(2)}, u32[]{:S(2)}) async-start(bf16[32,16,1024]{2,1,0:T(8,128)(2,1)} %bitcast.11), calls=%async_computation.2 | async-start | bytes 2097152 | tf_op jit(solution)/shard_map/all_to_all | solution.py:477
  149.1 7.7 %copy-start.7 = (bf16[512,1024]{1,0:T(8,128)(2,1)}, bf16[512,1024]{1,0:T(8,128)(2,1)S(1)}, u32[]{:S(2)}) copy-start(bf16[512,1024]{1,0:T(8,128)(2,1)S(1)} %collective-permute-done.14.right) | copy-start | bytes 3145732
  150.0 14.3 %collective-permute-start.15 = (bf16[256,1024]{1,0:T(8,128)(2,1)}, bf16[256,1024]{1,0:T(8,128)(2,1)}, u32[]{:S(2)}, u32[]{:S(2)}) collective-permute-start(bf16[256,1024]{1,0:T(8,128)(2,1)} %slice.45), channel_id=1, source_target_pairs={{0,3},{1,0},{2,1},{3,2},{4,7},{5,4},{6,5},{7,6},{8,11},{9,8},{10,9... | collective-permute-start | bytes 1572872 | tf_op jit(solution)/shard_map/ppermute | solution.py:362
  152.9 3.9 %copy-start.8 = (bf16[512,1024]{1,0:T(8,128)(2,1)}, bf16[512,1024]{1,0:T(8,128)(2,1)S(1)}, u32[]{:S(2)}) copy-start(bf16[512,1024]{1,0:T(8,128)(2,1)S(1)} %collective-permute-done.12.left) | copy-start | bytes 3145732
  153.8 13.7 %collective-permute-start.13 = (bf16[256,1024]{1,0:T(8,128)(2,1)}, bf16[256,1024]{1,0:T(8,128)(2,1)}, u32[]{:S(2)}, u32[]{:S(2)}) collective-permute-start(bf16[256,1024]{1,0:T(8,128)(2,1)} %slice.44), channel_id=1, source_target_pairs={{0,1},{1,2},{2,3},{3,0},{4,5},{5,6},{6,7},{7,4},{8,9},{9,10},{10,1... | collective-permute-start | bytes 1572872 | tf_op jit(solution)/shard_map/ppermute | solution.py:362
  164.3 3.2 %copy-start.2 = (bf16[32,16,1024]{2,1,0:T(8,128)(2,1)}, bf16[32,16,1024]{2,1,0:T(8,128)(2,1)S(1)}, u32[]{:S(2)}) copy-start(bf16[32,16,1024]{2,1,0:T(8,128)(2,1)S(1)} %all-to-all-done.2) | copy-start | bytes 3145732
  167.5 22.7 %collective-permute-start.17 = (bf16[512,1024]{1,0:T(8,128)(2,1)}, bf16[512,1024]{1,0:T(8,128)(2,1)S(1)}, u32[]{:S(2)}, u32[]{:S(2)}) collective-permute-start(bf16[512,1024]{1,0:T(8,128)(2,1)} %after.9.own), channel_id=1, source_target_pairs={{0,3},{1,0},{2,1},{3,2},{4,7},{5,4},{6,5},{7,6},{8,11},{9,8},{10,9... | collective-permute-start | bytes 3145736 | tf_op jit(solution)/shard_map/ppermute | solution.py:358
  168.0 24.3 %collective-permute-start.16 = (bf16[512,1024]{1,0:T(8,128)(2,1)}, bf16[512,1024]{1,0:T(8,128)(2,1)S(1)}, u32[]{:S(2)}, u32[]{:S(2)}) collective-permute-start(bf16[512,1024]{1,0:T(8,128)(2,1)} %after.9.own), channel_id=1, source_target_pairs={{0,1},{1,2},{2,3},{3,0},{4,5},{5,6},{6,7},{7,4},{8,9},{9,10},{10,1... | collective-permute-start | bytes 3145736 | tf_op jit(solution)/shard_map/ppermute | solution.py:357
  190.2 5.6 %copy-start.9 = (bf16[512,1024]{1,0:T(8,128)(2,1)}, bf16[512,1024]{1,0:T(8,128)(2,1)S(1)}, u32[]{:S(2)}) copy-start(bf16[512,1024]{1,0:T(8,128)(2,1)S(1)} %collective-permute-done.17.right) | copy-start | bytes 3145732
  192.3 3.6 %copy-start.10 = (bf16[512,1024]{1,0:T(8,128)(2,1)}, bf16[512,1024]{1,0:T(8,128)(2,1)S(1)}, u32[]{:S(2)}) copy-start(bf16[512,1024]{1,0:T(8,128)(2,1)S(1)} %collective-permute-done.16.left) | copy-start | bytes 3145732
  193.2 12.9 %collective-permute-start.18 = (bf16[256,1024]{1,0:T(8,128)(2,1)}, bf16[256,1024]{1,0:T(8,128)(2,1)S(1)}, u32[]{:S(2)}, u32[]{:S(2)}) collective-permute-start(bf16[256,1024]{1,0:T(8,128)(2,1)} %get-tuple-element.46), channel_id=1, source_target_pairs={{0,1},{1,2},{2,3},{3,0},{4,5},{5,6},{6,7},{7,4},{8,9},{9,10},{10,1... | collective-permute-start | bytes 1572872 | tf_op jit(solution)/shard_map/ppermute | solution.py:362
  193.2 12.9 %collective-permute-start.19 = (bf16[256,1024]{1,0:T(8,128)(2,1)}, bf16[256,1024]{1,0:T(8,128)(2,1)S(1)}, u32[]{:S(2)}, u32[]{:S(2)}) collective-permute-start(bf16[256,1024]{1,0:T(8,128)(2,1)} %get-tuple-element.47), channel_id=1, source_target_pairs={{0,3},{1,0},{2,1},{3,2},{4,7},{5,4},{6,5},{7,6},{8,11},{9,8},{10,9... | collective-permute-start | bytes 1572872 | tf_op jit(solution)/shard_map/ppermute | solution.py:362
  203.4 10.8 %collective-permute-start.25 = (bf16[512,384]{1,0:T(8,128)(2,1)}, bf16[512,384]{1,0:T(8,128)(2,1)S(1)}, u32[]{:S(2)}, u32[]{:S(2)}) collective-permute-start(bf16[512,384]{1,0:T(8,128)(2,1)} %after.11.own), channel_id=1, source_target_pairs={{0,1},{1,2},{2,3},{3,0},{4,5},{5,6},{6,7},{7,4},{8,9},{9,10},{10,1... | collective-permute-start | bytes 1179656 | tf_op jit(solution)/shard_map/ppermute | solution.py:357
  203.5 10.8 %collective-permute-start.24 = (bf16[512,384]{1,0:T(8,128)(2,1)}, bf16[512,384]{1,0:T(8,128)(2,1)S(1)}, u32[]{:S(2)}, u32[]{:S(2)}) collective-permute-start(bf16[512,384]{1,0:T(8,128)(2,1)} %after.11.own), channel_id=1, source_target_pairs={{0,3},{1,0},{2,1},{3,2},{4,7},{5,4},{6,5},{7,6},{8,11},{9,8},{10,9... | collective-permute-start | bytes 1179656 | tf_op jit(solution)/shard_map/ppermute | solution.py:358
  211.2 11.4 %collective-permute-start.21 = (bf16[512,384]{1,0:T(8,128)(2,1)}, bf16[512,384]{1,0:T(8,128)(2,1)S(1)}, u32[]{:S(2)}, u32[]{:S(2)}) collective-permute-start(bf16[512,384]{1,0:T(8,128)(2,1)} %far.3.own), channel_id=1, source_target_pairs={{0,1},{1,2},{2,3},{3,0},{4,5},{5,6},{6,7},{7,4},{8,9},{9,10},{10,1... | collective-permute-start | bytes 1179656 | tf_op jit(solution)/shard_map/ppermute | solution.py:357
  211.2 11.5 %collective-permute-start.20 = (bf16[512,384]{1,0:T(8,128)(2,1)}, bf16[512,384]{1,0:T(8,128)(2,1)S(1)}, u32[]{:S(2)}, u32[]{:S(2)}) collective-permute-start(bf16[512,384]{1,0:T(8,128)(2,1)} %far.3.own), channel_id=1, source_target_pairs={{0,3},{1,0},{2,1},{3,2},{4,7},{5,4},{6,5},{7,6},{8,11},{9,8},{10,9... | collective-permute-start | bytes 1179656 | tf_op jit(solution)/shard_map/ppermute | solution.py:358
  214.1 12.7 %copy-start.11 = (bf16[512,384]{1,0:T(8,128)(2,1)}, bf16[512,384]{1,0:T(8,128)(2,1)S(1)}, u32[]{:S(2)}) copy-start(bf16[512,384]{1,0:T(8,128)(2,1)S(1)} %collective-permute-done.25.left) | copy-start | bytes 1179652
  214.2 12.7 %collective-permute-start.26 = (bf16[256,384]{1,0:T(8,128)(2,1)S(1)}, bf16[256,384]{1,0:T(8,128)(2,1)S(1)}, u32[]{:S(2)}, u32[]{:S(2)}) collective-permute-start(bf16[256,384]{1,0:T(8,128)(2,1)S(1)} %slice.53), channel_id=1, source_target_pairs={{0,1},{1,2},{2,3},{3,0},{4,5},{5,6},{6,7},{7,4},{8,9},{9,10},{10,1... | collective-permute-start | bytes 589832 | tf_op jit(solution)/shard_map/ppermute | solution.py:362
  214.3 12.6 %copy-start.12 = (bf16[512,384]{1,0:T(8,128)(2,1)}, bf16[512,384]{1,0:T(8,128)(2,1)S(1)}, u32[]{:S(2)}) copy-start(bf16[512,384]{1,0:T(8,128)(2,1)S(1)} %collective-permute-done.24.right) | copy-start | bytes 1179652
  214.3 12.6 %collective-permute-start.27 = (bf16[256,384]{1,0:T(8,128)(2,1)S(1)}, bf16[256,384]{1,0:T(8,128)(2,1)S(1)}, u32[]{:S(2)}, u32[]{:S(2)}) collective-permute-start(bf16[256,384]{1,0:T(8,128)(2,1)S(1)} %slice.54), channel_id=1, source_target_pairs={{0,3},{1,0},{2,1},{3,2},{4,7},{5,4},{6,5},{7,6},{8,11},{9,8},{10,9... | collective-permute-start | bytes 589832 | tf_op jit(solution)/shard_map/ppermute | solution.py:362
  222.7 10.7 %copy-start.13 = (bf16[512,384]{1,0:T(8,128)(2,1)}, bf16[512,384]{1,0:T(8,128)(2,1)S(1)}, u32[]{:S(2)}) copy-start(bf16[512,384]{1,0:T(8,128)(2,1)S(1)} %collective-permute-done.21.left) | copy-start | bytes 1179652
  222.7 10.7 %collective-permute-start.22 = (bf16[256,384]{1,0:T(8,128)(2,1)S(1)}, bf16[256,384]{1,0:T(8,128)(2,1)S(1)}, u32[]{:S(2)}, u32[]{:S(2)}) collective-permute-start(bf16[256,384]{1,0:T(8,128)(2,1)S(1)} %slice.51), channel_id=1, source_target_pairs={{0,1},{1,2},{2,3},{3,0},{4,5},{5,6},{6,7},{7,4},{8,9},{9,10},{10,1... | collective-permute-start | bytes 589832 | tf_op jit(solution)/shard_map/ppermute | solution.py:362
  222.8 10.6 %copy-start.14 = (bf16[512,384]{1,0:T(8,128)(2,1)}, bf16[512,384]{1,0:T(8,128)(2,1)S(1)}, u32[]{:S(2)}) copy-start(bf16[512,384]{1,0:T(8,128)(2,1)S(1)} %collective-permute-done.20.right) | copy-start | bytes 1179652
  222.8 10.6 %collective-permute-start.23 = (bf16[256,384]{1,0:T(8,128)(2,1)S(1)}, bf16[256,384]{1,0:T(8,128)(2,1)S(1)}, u32[]{:S(2)}, u32[]{:S(2)}) collective-permute-start(bf16[256,384]{1,0:T(8,128)(2,1)S(1)} %slice.52), channel_id=1, source_target_pairs={{0,3},{1,0},{2,1},{3,2},{4,7},{5,4},{6,5},{7,6},{8,11},{9,8},{10,9... | collective-permute-start | bytes 589832 | tf_op jit(solution)/shard_map/ppermute | solution.py:362
  239.9 37.4 %copy-start.17 = (bf16[128,1024]{1,0:T(8,128)(2,1)S(1)}, bf16[128,1024]{1,0:T(8,128)(2,1)}, u32[]{:S(2)}) copy-start(bf16[128,1024]{1,0:T(8,128)(2,1)} %get-tuple-element.39) | copy-start | bytes 786436
  (15 other events, 16.6 us)
Sparse Core Ops, SparseCore 0:
  9.7 34.6 all-gather.2

commit v4 on v3

--- a/solution.py
+++ b/solution.py
@@ -485,7 +485,7 @@
     weights = (gate_weight, up_weight)
     right0, left0, top0, low0 = ring_gather(held0)
     partial0 = run_near(x_ref, 0, (held0, right0, left0), gains, *weights)
-    (held1,) = after((exchange(bins1),), top0, low0, partial0[1])
+    (held1,) = after((exchange(bins1),), partial0[1])
     hidden0 = run_far(x_ref, 0, (top0, low0), partial0, gains, *weights)
     right1, left1, top1, low1 = ring_gather(held1, done=(hidden0,))
     partial1 = run_near(x_ref, 1, (held1, right1, left1), gains, *weights)

time: 286 us -> 299 us (1.045)
  waiting for transfers between devices: 61.2 us -> 68.8 us
  local copies, waits for them, and re-layouts: 13.8 us -> 17 us
    ppermute x4, waiting for transfers between devices: 33.6 us -> 0.01 us  [ring_gather(): right = lax.ppermute(block, axis, LEFT)]
    ppermute x4, waiting for transfers between devices: 4.34 us -> 32.9 us  [ring_gather(): lax.ppermute(upper, axis, RIGHT)]
    ppermute x4, waiting for transfers between devices: 7.06 us -> 19.7 us  [ring_gather(): left = lax.ppermute(block, axis, RIGHT)]
    unnamed x68 -> x74, local copies, waits for them, and re-layouts: 10.1 us -> 14 us
  transfers between devices with their start and end apart: 31 -> 31, of which waited for: 14 -> 11; matrix products, arithmetic and copies ran while one was open for 4% -> 4% of each run, Pallas kernels for 16% -> 15%
where the time goes in v4:
time: 299 us; the launch traced here: 297 us
  blocking collectives  81.4 us (27%)
  waiting for transfers between devices  68.8 us (23%)
  Pallas kernels  56.8 us (19%)
  starting transfers between devices  50.7 us (17%)
  local copies, waits for them, and re-layouts  17 us (6%)
  between operations  14.5 us (5%)
  other arithmetic  4.83 us (2%)
  matrix products  3.44 us (1%)
    all_to_all x1, blocking collectives, per_device(): back = lax.all_to_all(back.reshape(32, 2 * CAP, PART), DP, 0, 0, tiled=True)  37.5 us
    ppermute x4, waiting for transfers between devices, ring_gather(): lax.ppermute(upper, axis, RIGHT)  32.9 us
    all_to_all x1, blocking collectives, per_device(): landed = lax.all_to_all(onward, DP, 0, 0, tiled=True)  22.5 us
    all_to_all x1, blocking collectives, exchange(): lax.all_to_all(rows.reshape(32, CAP, PART), DP, 0, 0, tiled=True)  21.5 us
    ppermute x4, waiting for transfers between devices, ring_gather(): left = lax.ppermute(block, axis, RIGHT)  19.7 us
    pallas_call x2, Pallas kernels, run_near(): pl.pallas_call(near_kernel, grid_spec=pltpu.PrefetchScalarGridSpec(num_sc...  15.1 us
    unnamed x74, local copies, waits for them, and re-layouts  14 us
    ppermute x4, starting transfers between devices, ring_gather(): lax.ppermute(lower, axis, LEFT)  11 us
  transfers between devices with their start and end apart: 31, of which 11 were waited for; matrix products, arithmetic and copies ran while one was open for 4% of the time, Pallas kernels for 15%

profile of v4, /device:TPU:1, one launch (start us, length us, event | category | flops | bytes accessed | tf_op | source)
XLA Modules:
  0.0 297.4 jit_solution(15539619206207220025)
XLA Ops:
  7.9 3.3 %columns.3 = (bf16[400,1024]{1,0:T(8,128)(2,1)}, bf16[400,1024]{1,0:T(8,128)(2,1)}) custom-call(s32[1]{0:T(128)} %bitcast.index, bf16[2,384,4096]{2,1,0:T(8,128)(2,1)} %own_w.3, f32[1,1024]{1,0:T(1,128)} %bitcast.34), custom_call_target="tpu_custom_call" | custom-call | tf_op jit(solution)/shard_map/columns/pallas_call | solution.py:140
  11.2 2.1 collective-permute-start
  13.3 1.4 collective-permute-start.2
  14.6 3.6 %attend.1.rest_0_ = bf16[4,4,2,16,1280]{4,3,2,1,0:T(8,128)(2,1)} custom-call(s32[1]{0:T(128)} %bitcast.1.index, s32[4,64]{1,0:T(4,128)} %bitcast.43, bf16[128,1024]{1,0:T(8,128)(2,1)} %queries_in.1, bf16[128,128]{1,0:T(8,128)(2,1)} %keys_in.1, bf16[128,128]{1,0:T(8,128)(2,1)} %values_in.1, bf16[128,1024]{1,0:T(8,128)(2,1)} %residual_in.1), custom_call_target="tpu_custom_call" | custom-call | tf_op jit(solution)/shard_map/attend/pallas_call | solution.py:400
  18.3 9.5 %all-to-all-start = ((bf16[32,16,1280]{2,1,0:T(8,128)(2,1)}), bf16[32,16,1280]{2,1,0:T(8,128)(2,1)S(1)}, u32[]{:S(2)}, u32[]{:S(2)}) async-start(bf16[32,16,1280]{2,1,0:T(8,128)(2,1)} %bitcast.26), calls=%async_computation | async-start | bytes 2621440 | tf_op jit(solution)/shard_map/all_to_all | solution.py:416
  27.8 4.6 %collective-permute-done = bf16[400,1024]{1,0:T(8,128)(2,1)} collective-permute-done((bf16[400,1024]{1,0:T(8,128)(2,1)}, bf16[400,1024]{1,0:T(8,128)(2,1)}, u32[]{:S(2)}, u32[]{:S(2)}) %collective-permute-start) | collective-permute-done | bytes 819232 | tf_op jit(solution)/shard_map/ppermute | solution.py:431
  32.7 2.4 collective-permute-start.3
  35.1 4.3 %columns.2 = (bf16[784,1024]{1,0:T(8,128)(2,1)}, bf16[784,1024]{1,0:T(8,128)(2,1)}) custom-call(s32[1]{0:T(128)} %bitcast.index, bf16[2,384,4096]{2,1,0:T(8,128)(2,1)} %own_w.3, f32[1,1024]{1,0:T(1,128)} %bitcast.35, bf16[4,4,2,16,1280]{4,3,2,1,0:T(8,128)(2,1)} %attend.1.rest_0_), custom_call_target="tpu_custom_call" | custom-call | tf_op jit(solution)/shard_map/columns/pallas_call | solution.py:140
  42.3 3.4 %tables.1 = (bf16[512,128]{1,0:T(8,128)(2,1)}, bf16[512,128]{1,0:T(8,128)(2,1)}, bf16[128,1024]{1,0:T(8,128)(2,1)}) custom-call(s32[8,128]{1,0:T(8,128)} %bitcast.37, s32[8,128]{1,0:T(8,128)} %bitcast.38, s32[8,128]{1,0:T(8,128)} %bitcast.39, s32[128,8]{1,0:T(8,128)} %copy.26.routes, s32[128,8]{1,0:T(8,128)} %copy.27.slots, s32[128,8]{1,0:T(8,128)} %copy.28.dropped, ...), custom_call_target="tpu_custom_call" | custom-call | tf_op jit(solution)/shard_map/tables/pallas_call | solution.py:419
  45.7 5.5 %all-to-all-done = bf16[32,16,1280]{2,1,0:T(8,128)(2,1)S(1)} async-done(((bf16[32,16,1280]{2,1,0:T(8,128)(2,1)}), bf16[32,16,1280]{2,1,0:T(8,128)(2,1)S(1)}, u32[]{:S(2)}, u32[]{:S(2)}) %all-to-all-start) | async-done | bytes 1310752 | tf_op jit(solution)/shard_map/all_to_all | solution.py:416
  53.1 4.1 %project.1 = (bf16[256,256]{1,0:T(8,128)(2,1)}, bf16[256,256]{1,0:T(8,128)(2,1)}, bf16[256,256]{1,0:T(8,128)(2,1)}, bf16[256,256]{1,0:T(8,128)(2,1)}, bf16[256,2...) custom-call(s32[1]{0:T(128)} %bitcast.index, bf16[512,1280]{1,0:T(8,128)(2,1)} %bitcast.31, ...), custom_call_target="tpu_custom_call" | custom-call | tf_op jit(solution)/shard_map/project/pallas_call | solution.py:437
  58.1 1.2 collective-permute-start.6
  59.3 1.5 collective-permute-start.7
  61.3 1.1 collective-permute-done.4
  63.4 1.6 collective-permute-done.8
  66.0 2.4 collective-permute-start.9
  68.5 1.9 collective-permute-done.9.two_low
  71.0 2.1 route.1.refs_2_
  74.0 2.3 collective-permute-start.11
  76.3 22.5 %all_to_all.25 = bf16[32,16,256]{2,1,0:T(8,128)(2,1)} all-to-all(bf16[32,16,256]{2,1,0:T(8,128)(2,1)S(1)} %copy-done.6), channel_id=1, replica_groups=mesh['y'=4,'z'=4,'core'=2,'tensor'=4] {'y','z','core'}, dimensions={0} | all-to-all | bytes 524288 | tf_op jit(solution)/shard_map/all_to_all | solution.py:457
  98.8 2.4 stream.1
  101.1 21.5 %all_to_all.26 = bf16[32,16,1024]{2,1,0:T(8,128)(2,1)} all-to-all(bf16[32,16,1024]{2,1,0:T(8,128)(2,1)} %bitcast.32), channel_id=1, replica_groups=mesh['y'=4,'z'=4,'core'=2,'tensor'=4] {'y','z','core'}, dimensions={0} | all-to-all | bytes 2097152 | tf_op jit(solution)/shard_map/all_to_all | solution.py:477
  122.6 1.1 copy-done
  124.3 2.7 collective-permute-start.12
  127.0 2.3 convolution_convert_fusion
  129.3 4.5 %all-to-all-start.2 = ((bf16[32,16,1024]{2,1,0:T(8,128)(2,1)}), bf16[32,16,1024]{2,1,0:T(8,128)(2,1)S(1)}, u32[]{:S(2)}, u32[]{:S(2)}) async-start(bf16[32,16,1024]{2,1,0:T(8,128)(2,1)} %bitcast.11), calls=%async_computation.2 | async-start | bytes 2097152 | tf_op jit(solution)/shard_map/all_to_all | solution.py:477
  136.8 13.6 %collective-permute-done.13.left = bf16[512,1024]{1,0:T(8,128)(2,1)S(1)} collective-permute-done((bf16[512,1024]{1,0:T(8,128)(2,1)}, bf16[512,1024]{1,0:T(8,128)(2,1)S(1)}, u32[]{:S(2)}, u32[]{:S(2)}) %collective-permute-start.13) | collective-permute-done | bytes 1048608 | tf_op jit(solution)/shard_map/ppermute | solution.py:357
  150.4 1.0 copy-done.11
  152.3 7.5 %near.2 = (f32[512,768]{1,0:T(8,128)}, f32[512,1]{1,0:T(8,128)}) custom-call(s32[1]{0:T(128)} %bitcast.index, bf16[512,1024]{1,0:T(8,128)(2,1)} %after.8.own, bf16[512,1024]{1,0:T(8,128)(2,1)} %copy-done.9, bf16[512,1024]{1,0:T(8,128)(2,1)} %copy-done.11, f32[4,1,1024]{2,1,0:T(1,128)} %pad_maximum_fusion.gain, bf16[2,4096,384]{2,1,0:T(8,128)(2,1)} %gate_w.7, ...), custom_call_target="tpu_custom_call" | custom-call | tf_op jit(solution)/shard_map/near/pallas_call | solution.py:264
  159.9 1.0 copy-done.2
  160.8 1.4 collective-permute-start.15
  162.3 1.1 slice.49
  163.5 2.7 collective-permute-start.17
  166.2 31.7 %collective-permute-done.16.top = bf16[256,1024]{1,0:T(8,128)(2,1)S(1)} collective-permute-done((bf16[256,1024]{1,0:T(8,128)(2,1)S(1)}, bf16[256,1024]{1,0:T(8,128)(2,1)S(1)}, u32[]{:S(2)}, u32[]{:S(2)}) %collective-permute-start.16) | collective-permute-done | bytes 524320 | tf_op jit(solution)/shard_map/ppermute | solution.py:362
  198.9 4.1 %far.2.refs_2_.refs_0_ = bf16[512,384]{1,0:T(8,128)(2,1)} custom-call(s32[1]{0:T(128)} %bitcast.index, bf16[256,1024]{1,0:T(8,128)(2,1)} %copy-done.18, bf16[256,1024]{1,0:T(8,128)(2,1)} %copy-done.19, f32[512,768]{1,0:T(8,128)} %get-tuple-element.45.total, f32[512,1]{1,0:T(8,128)} %get-tuple-element.44.refs_1_.squares, f32[4,1,1024]{2,1,0:T(1,128)} %pad_maximum_fusion.gain, ...), custom_call_target="tpu_custom_call" | custom-call | tf_op jit(solution)/shard_map/far/pallas_call | solution.py:286
  204.8 2.7 collective-permute-start.19
  207.5 7.5 %near.3 = (f32[512,768]{1,0:T(8,128)}, f32[512,1]{1,0:T(8,128)}) custom-call(s32[1]{0:T(128)} %bitcast.index, bf16[512,1024]{1,0:T(8,128)(2,1)} %after.9.own, bf16[512,1024]{1,0:T(8,128)(2,1)} %copy-done.7, bf16[512,1024]{1,0:T(8,128)(2,1)} %copy-done.8, f32[4,1,1024]{2,1,0:T(1,128)} %pad_maximum_fusion.gain, bf16[2,4096,384]{2,1,0:T(8,128)(2,1)} %gate_w.7, ...), custom_call_target="tpu_custom_call" | custom-call | tf_op jit(solution)/shard_map/near/pallas_call | solution.py:264
  215.1 2.7 collective-permute-start.24
  218.8 4.1 %far.3.own = bf16[512,384]{1,0:T(8,128)(2,1)} custom-call(s32[1]{0:T(128)} %bitcast.index, bf16[256,1024]{1,0:T(8,128)(2,1)} %copy-done.16, bf16[256,1024]{1,0:T(8,128)(2,1)} %copy-done.17, f32[512,768]{1,0:T(8,128)} %get-tuple-element.48.total, f32[512,1]{1,0:T(8,128)} %get-tuple-element.49.squares.refs_1_, f32[4,1,1024]{2,1,0:T(1,128)} %pad_maximum_fusion.gain, ...), custom_call_target="tpu_custom_call" | custom-call | tf_op jit(solution)/shard_map/far/pallas_call | solution.py:286
  222.8 2.7 collective-permute-start.20
  226.1 2.7 collective-permute-start.27
  228.8 5.7 %collective-permute-done.21.left = bf16[512,384]{1,0:T(8,128)(2,1)S(1)} collective-permute-done((bf16[512,384]{1,0:T(8,128)(2,1)}, bf16[512,384]{1,0:T(8,128)(2,1)S(1)}, u32[]{:S(2)}, u32[]{:S(2)}) %collective-permute-start.21) | collective-permute-done | bytes 393248 | tf_op jit(solution)/shard_map/ppermute | solution.py:357
  234.7 2.9 collective-permute-start.23
  237.6 1.1 collective-permute-done.26.top
  240.1 5.2 %down.2.rest_0_ = bf16[32,2,16,1024]{3,2,1,0:T(8,128)(2,1)} custom-call(s32[1]{0:T(128)} %bitcast.index, bf16[512,384]{1,0:T(8,128)(2,1)} %after.11.own, bf16[512,384]{1,0:T(8,128)(2,1)} %copy-done.13, bf16[512,384]{1,0:T(8,128)(2,1)} %copy-done.12, bf16[256,384]{1,0:T(8,128)(2,1)} %copy-done.24, bf16[256,384]{1,0:T(8,128)(2,1)} %copy-done.25, ...), custom_call_target="tpu_custom_call" | custom-call | tf_op jit(solution)/shard_map/down/pallas_call | solution.py:337
  246.7 5.2 %down.3 = bf16[32,2,16,1024]{3,2,1,0:T(8,128)(2,1)} custom-call(s32[1]{0:T(128)} %bitcast.index, bf16[512,384]{1,0:T(8,128)(2,1)} %far.3.own, bf16[512,384]{1,0:T(8,128)(2,1)} %copy-done.15, bf16[512,384]{1,0:T(8,128)(2,1)} %copy-done.14, bf16[256,384]{1,0:T(8,128)(2,1)} %copy-done.22, bf16[256,384]{1,0:T(8,128)(2,1)} %copy-done.23, ...), custom_call_target="tpu_custom_call", output_to_operand_aliasing={{}: (10, {})} | custom-call | tf_op jit(solution)/shard_map/down/pallas_call | solution.py:337
  252.0 37.5 %all_to_all.27 = bf16[32,32,1024]{2,1,0:T(8,128)(2,1)S(1)} all-to-all(bf16[32,32,1024]{2,1,0:T(8,128)(2,1)} %bitcast.25), channel_id=1, replica_groups=mesh['y'=4,'z'=4,'core'=2,'tensor'=4] {'y','z','core'}, dimensions={0} | all-to-all | bytes 4194304 | tf_op jit(solution)/shard_map/all_to_all | solution.py:498
  289.4 1.1 convolution_convert_fusion.1
  (127 shorter events, 22.6 us)
Async XLA Ops:
  7.2 38.5 %all-gather.3.cloned.1.call-start = ((), (), s32[]{:S(2)}) async-start(), calls=%async_computation.5 | async-start | bytes 2359296 | tf_op jit(solution)/shard_map/all_gather | solution.py:398
  11.2 21.2 %collective-permute-start = (bf16[400,1024]{1,0:T(8,128)(2,1)}, bf16[400,1024]{1,0:T(8,128)(2,1)}, u32[]{:S(2)}, u32[]{:S(2)}) collective-permute-start(bf16[400,1024]{1,0:T(8,128)(2,1)} %get-tuple-element.29), channel_id=1, source_target_pairs={{0,1},{1,2},{2,3},{3,0},{4,5},{5,6},{6,7},{7,4},{8,9},{9,10},{10,1... | collective-permute-start | bytes 2457608 | tf_op jit(solution)/shard_map/ppermute | solution.py:431
  13.3 19.4 %collective-permute-start.2 = (bf16[400,1024]{1,0:T(8,128)(2,1)}, bf16[400,1024]{1,0:T(8,128)(2,1)}, u32[]{:S(2)}, u32[]{:S(2)}) collective-permute-start(bf16[400,1024]{1,0:T(8,128)(2,1)} %get-tuple-element.30), channel_id=1, source_target_pairs={{0,3},{1,0},{2,1},{3,2},{4,7},{5,4},{6,5},{7,6},{8,11},{9,8},{10,9... | collective-permute-start | bytes 2457608 | tf_op jit(solution)/shard_map/ppermute | solution.py:432
  18.3 33.0 %all-to-all-start = ((bf16[32,16,1280]{2,1,0:T(8,128)(2,1)}), bf16[32,16,1280]{2,1,0:T(8,128)(2,1)S(1)}, u32[]{:S(2)}, u32[]{:S(2)}) async-start(bf16[32,16,1280]{2,1,0:T(8,128)(2,1)} %bitcast.26), calls=%async_computation | async-start | bytes 2621440 | tf_op jit(solution)/shard_map/all_to_all | solution.py:416
  27.7 11.7 %copy-start.34 = (f32[128,8]{0,1:T(8,128)S(1)}, f32[128,8]{0,1:T(8,128)}, u32[]{:S(2)}) copy-start(f32[128,8]{0,1:T(8,128)} %param.26) | copy-start | bytes 12292
  27.7 12.4 %copy-start.31 = (s32[128,8]{0,1:T(8,128)S(1)}, s32[128,8]{0,1:T(8,128)}, u32[]{:S(2)}) copy-start(s32[128,8]{0,1:T(8,128)} %param.23) | copy-start | bytes 12292
  27.7 13.1 %copy-start.32 = (s32[128,8]{0,1:T(8,128)S(1)}, s32[128,8]{0,1:T(8,128)}, u32[]{:S(2)}) copy-start(s32[128,8]{0,1:T(8,128)} %param.24) | copy-start | bytes 12292
  27.8 13.8 %copy-start.33 = (s32[128,8]{0,1:T(8,128)S(1)}, s32[128,8]{0,1:T(8,128)}, u32[]{:S(2)}) copy-start(s32[128,8]{0,1:T(8,128)} %param.25) | copy-start | bytes 12292
  32.4 19.5 %collective-permute-start.1 = (bf16[400,1024]{1,0:T(8,128)(2,1)}, bf16[400,1024]{1,0:T(8,128)(2,1)S(1)}, u32[]{:S(2)}, u32[]{:S(2)}) collective-permute-start(bf16[400,1024]{1,0:T(8,128)(2,1)} %collective-permute-done), channel_id=1, source_target_pairs={{0,1},{1,2},{2,3},{3,0},{4,5},{5,6},{6,7},{7,4},{8,9},{9,10},{10,1... | collective-permute-start | bytes 2457608 | tf_op jit(solution)/shard_map/ppermute | solution.py:431
  32.7 19.2 %collective-permute-start.3 = (bf16[400,1024]{1,0:T(8,128)(2,1)}, bf16[400,1024]{1,0:T(8,128)(2,1)S(1)}, u32[]{:S(2)}, u32[]{:S(2)}) collective-permute-start(bf16[400,1024]{1,0:T(8,128)(2,1)} %collective-permute-done.2), channel_id=1, source_target_pairs={{0,3},{1,0},{2,1},{3,2},{4,7},{5,4},{6,5},{7,6},{8,11},{9,8},{10,9... | collective-permute-start | bytes 2457608 | tf_op jit(solution)/shard_map/ppermute | solution.py:432
  57.2 5.2 %collective-permute-start.4 = (bf16[256,256]{1,0:T(8,128)(2,1)}, bf16[256,256]{1,0:T(8,128)(2,1)S(1)}, u32[]{:S(2)}, u32[]{:S(2)}) collective-permute-start(bf16[256,256]{1,0:T(8,128)(2,1)} %get-tuple-element.33), channel_id=1, source_target_pairs={{0,1},{1,2},{2,3},{3,0},{4,5},{5,6},{6,7},{7,4},{8,9},{9,10},{10,1... | collective-permute-start | bytes 393224 | tf_op jit(solution)/shard_map/ppermute | solution.py:366
  58.1 10.3 %collective-permute-start.6 = (bf16[256,256]{1,0:T(8,128)(2,1)}, bf16[256,256]{1,0:T(8,128)(2,1)S(1)}, u32[]{:S(2)}, u32[]{:S(2)}) collective-permute-start(bf16[256,256]{1,0:T(8,128)(2,1)} %get-tuple-element.34), channel_id=1, source_target_pairs={{0,1},{1,2},{2,3},{3,0},{4,5},{5,6},{6,7},{7,4},{8,9},{9,10},{10,1... | collective-permute-start | bytes 393224 | tf_op jit(solution)/shard_map/ppermute | solution.py:368
  59.3 9.1 %collective-permute-start.7 = (bf16[256,256]{1,0:T(8,128)(2,1)}, bf16[256,256]{1,0:T(8,128)(2,1)S(1)}, u32[]{:S(2)}, u32[]{:S(2)}) collective-permute-start(bf16[256,256]{1,0:T(8,128)(2,1)} %get-tuple-element.35), channel_id=1, source_target_pairs={{0,3},{1,0},{2,1},{3,2},{4,7},{5,4},{6,5},{7,6},{8,11},{9,8},{10,9... | collective-permute-start | bytes 393224 | tf_op jit(solution)/shard_map/ppermute | solution.py:369
  60.8 4.3 %collective-permute-start.8 = (bf16[256,256]{1,0:T(8,128)(2,1)}, bf16[256,256]{1,0:T(8,128)(2,1)S(1)}, u32[]{:S(2)}, u32[]{:S(2)}) collective-permute-start(bf16[256,256]{1,0:T(8,128)(2,1)} %get-tuple-element.37), channel_id=1, source_target_pairs={{0,3},{1,0},{2,1},{3,2},{4,7},{5,4},{6,5},{7,6},{8,11},{9,8},{10,9... | collective-permute-start | bytes 393224 | tf_op jit(solution)/shard_map/ppermute | solution.py:367
  63.4 5.1 %collective-permute-start.5 = (bf16[256,256]{1,0:T(8,128)(2,1)S(1)}, bf16[256,256]{1,0:T(8,128)(2,1)S(1)}, u32[]{:S(2)}, u32[]{:S(2)}) collective-permute-start(bf16[256,256]{1,0:T(8,128)(2,1)S(1)} %add_convert_fusion.1), channel_id=1, source_target_pairs={{0,1},{1,2},{2,3},{3,0},{4,5},{5,6},{6,7},{7,4},{8,9},{9,10},{10,1... | collective-permute-start | bytes 393224 | tf_op jit(solution)/shard_map/ppermute | solution.py:372
  66.0 4.3 %collective-permute-start.9 = (bf16[256,256]{1,0:T(8,128)(2,1)S(1)}, bf16[256,256]{1,0:T(8,128)(2,1)S(1)}, u32[]{:S(2)}, u32[]{:S(2)}) collective-permute-start(bf16[256,256]{1,0:T(8,128)(2,1)S(1)} %add_convert_fusion), channel_id=1, source_target_pairs={{0,3},{1,0},{2,1},{3,2},{4,7},{5,4},{6,5},{7,6},{8,11},{9,8},{10,9... | collective-permute-start | bytes 393224 | tf_op jit(solution)/shard_map/ppermute | solution.py:373
  68.4 1.9 copy-start.26
  68.4 1.9 copy-start.27
  73.1 3.2 %copy-start.6 = (bf16[32,16,256]{2,1,0:T(8,128)(2,1)S(1)}, bf16[32,16,256]{2,1,0:T(8,128)(2,1)}, u32[]{:S(2)}) copy-start(bf16[32,16,256]{2,1,0:T(8,128)(2,1)} %route.1.refs_2_) | copy-start | bytes 786436
  73.1 49.5 %collective-permute-start.10 = (bf16[784,1024]{1,0:T(8,128)(2,1)}, bf16[784,1024]{1,0:T(8,128)(2,1)S(1)}, u32[]{:S(2)}, u32[]{:S(2)}) collective-permute-start(bf16[784,1024]{1,0:T(8,128)(2,1)} %get-tuple-element.42), channel_id=1, source_target_pairs={{0,1},{1,2},{2,3},{3,0},{4,5},{5,6},{6,7},{7,4},{8,9},{9,10},{10,1... | collective-permute-start | bytes 4816904 | tf_op jit(solution)/shard_map/ppermute | solution.py:459
  74.0 48.6 %collective-permute-start.11 = (bf16[784,1024]{1,0:T(8,128)(2,1)}, bf16[784,1024]{1,0:T(8,128)(2,1)S(1)}, u32[]{:S(2)}, u32[]{:S(2)}) collective-permute-start(bf16[784,1024]{1,0:T(8,128)(2,1)} %get-tuple-element.43), channel_id=1, source_target_pairs={{0,3},{1,0},{2,1},{3,2},{4,7},{5,4},{6,5},{7,6},{8,11},{9,8},{10,9... | collective-permute-start | bytes 4816904 | tf_op jit(solution)/shard_map/ppermute | solution.py:460
  124.3 2.7 copy-start.21
  124.3 11.8 %copy-start.30 = (f32[1024]{0:T(1024)S(1)}, f32[1024]{0:T(1024)}, u32[]{:S(2)}) copy-start(f32[1024]{0:T(1024)} %param.22) | copy-start | bytes 12292
  124.3 26.0 %collective-permute-start.13 = (bf16[512,1024]{1,0:T(8,128)(2,1)}, bf16[512,1024]{1,0:T(8,128)(2,1)S(1)}, u32[]{:S(2)}, u32[]{:S(2)}) collective-permute-start(bf16[512,1024]{1,0:T(8,128)(2,1)} %after.8.own), channel_id=1, source_target_pairs={{0,1},{1,2},{2,3},{3,0},{4,5},{5,6},{6,7},{7,4},{8,9},{9,10},{10,1... | collective-permute-start | bytes 3145736 | tf_op jit(solution)/shard_map/ppermute | solution.py:357
  124.3 26.0 %collective-permute-start.12 = (bf16[512,1024]{1,0:T(8,128)(2,1)}, bf16[512,1024]{1,0:T(8,128)(2,1)S(1)}, u32[]{:S(2)}, u32[]{:S(2)}) collective-permute-start(bf16[512,1024]{1,0:T(8,128)(2,1)} %after.8.own), channel_id=1, source_target_pairs={{0,3},{1,0},{2,1},{3,2},{4,7},{5,4},{6,5},{7,6},{8,11},{9,8},{10,9... | collective-permute-start | bytes 3145736 | tf_op jit(solution)/shard_map/ppermute | solution.py:358
  129.3 30.5 %all-to-all-start.2 = ((bf16[32,16,1024]{2,1,0:T(8,128)(2,1)}), bf16[32,16,1024]{2,1,0:T(8,128)(2,1)S(1)}, u32[]{:S(2)}, u32[]{:S(2)}) async-start(bf16[32,16,1024]{2,1,0:T(8,128)(2,1)} %bitcast.11), calls=%async_computation.2 | async-start | bytes 2097152 | tf_op jit(solution)/shard_map/all_to_all | solution.py:477
  159.8 3.7 %copy-start.10 = (bf16[512,1024]{1,0:T(8,128)(2,1)S(1)}, bf16[512,1024]{1,0:T(8,128)(2,1)}, u32[]{:S(2)}) copy-start(bf16[512,1024]{1,0:T(8,128)(2,1)} %copy-done.9) | copy-start | bytes 3145732
  160.8 42.2 %collective-permute-start.15 = (bf16[512,1024]{1,0:T(8,128)(2,1)}, bf16[512,1024]{1,0:T(8,128)(2,1)S(1)}, u32[]{:S(2)}, u32[]{:S(2)}) collective-permute-start(bf16[512,1024]{1,0:T(8,128)(2,1)} %after.9.own), channel_id=1, source_target_pairs={{0,3},{1,0},{2,1},{3,2},{4,7},{5,4},{6,5},{7,6},{8,11},{9,8},{10,9... | collective-permute-start | bytes 3145736 | tf_op jit(solution)/shard_map/ppermute | solution.py:358
  162.2 41.7 %collective-permute-start.14 = (bf16[512,1024]{1,0:T(8,128)(2,1)}, bf16[512,1024]{1,0:T(8,128)(2,1)S(1)}, u32[]{:S(2)}, u32[]{:S(2)}) collective-permute-start(bf16[512,1024]{1,0:T(8,128)(2,1)} %after.9.own), channel_id=1, source_target_pairs={{0,1},{1,2},{2,3},{3,0},{4,5},{5,6},{6,7},{7,4},{8,9},{9,10},{10,1... | collective-permute-start | bytes 3145736 | tf_op jit(solution)/shard_map/ppermute | solution.py:357
  163.4 34.6 %collective-permute-start.16 = (bf16[256,1024]{1,0:T(8,128)(2,1)S(1)}, bf16[256,1024]{1,0:T(8,128)(2,1)S(1)}, u32[]{:S(2)}, u32[]{:S(2)}) collective-permute-start(bf16[256,1024]{1,0:T(8,128)(2,1)S(1)} %slice.49), channel_id=1, source_target_pairs={{0,1},{1,2},{2,3},{3,0},{4,5},{5,6},{6,7},{7,4},{8,9},{9,10},{10,1... | collective-permute-start | bytes 1572872 | tf_op jit(solution)/shard_map/ppermute | solution.py:362
  163.5 34.5 %collective-permute-start.17 = (bf16[256,1024]{1,0:T(8,128)(2,1)S(1)}, bf16[256,1024]{1,0:T(8,128)(2,1)S(1)}, u32[]{:S(2)}, u32[]{:S(2)}) collective-permute-start(bf16[256,1024]{1,0:T(8,128)(2,1)S(1)} %slice.50), channel_id=1, source_target_pairs={{0,3},{1,0},{2,1},{3,2},{4,7},{5,4},{6,5},{7,6},{8,11},{9,8},{10,9... | collective-permute-start | bytes 1572872 | tf_op jit(solution)/shard_map/ppermute | solution.py:362
  203.0 4.5 %copy-start.7 = (bf16[512,1024]{1,0:T(8,128)(2,1)}, bf16[512,1024]{1,0:T(8,128)(2,1)S(1)}, u32[]{:S(2)}) copy-start(bf16[512,1024]{1,0:T(8,128)(2,1)S(1)} %collective-permute-done.15.right) | copy-start | bytes 3145732
  203.9 3.6 %copy-start.8 = (bf16[512,1024]{1,0:T(8,128)(2,1)}, bf16[512,1024]{1,0:T(8,128)(2,1)S(1)}, u32[]{:S(2)}) copy-start(bf16[512,1024]{1,0:T(8,128)(2,1)S(1)} %collective-permute-done.14.left) | copy-start | bytes 3145732
  204.8 13.0 %collective-permute-start.18 = (bf16[256,1024]{1,0:T(8,128)(2,1)}, bf16[256,1024]{1,0:T(8,128)(2,1)S(1)}, u32[]{:S(2)}, u32[]{:S(2)}) collective-permute-start(bf16[256,1024]{1,0:T(8,128)(2,1)} %get-tuple-element.46), channel_id=1, source_target_pairs={{0,1},{1,2},{2,3},{3,0},{4,5},{5,6},{6,7},{7,4},{8,9},{9,10},{10,1... | collective-permute-start | bytes 1572872 | tf_op jit(solution)/shard_map/ppermute | solution.py:362
  204.8 13.0 %collective-permute-start.19 = (bf16[256,1024]{1,0:T(8,128)(2,1)}, bf16[256,1024]{1,0:T(8,128)(2,1)S(1)}, u32[]{:S(2)}, u32[]{:S(2)}) collective-permute-start(bf16[256,1024]{1,0:T(8,128)(2,1)} %get-tuple-element.47), channel_id=1, source_target_pairs={{0,3},{1,0},{2,1},{3,2},{4,7},{5,4},{6,5},{7,6},{8,11},{9,8},{10,9... | collective-permute-start | bytes 1572872 | tf_op jit(solution)/shard_map/ppermute | solution.py:362
  215.1 10.9 %collective-permute-start.25 = (bf16[512,384]{1,0:T(8,128)(2,1)}, bf16[512,384]{1,0:T(8,128)(2,1)S(1)}, u32[]{:S(2)}, u32[]{:S(2)}) collective-permute-start(bf16[512,384]{1,0:T(8,128)(2,1)} %after.11.own), channel_id=1, source_target_pairs={{0,1},{1,2},{2,3},{3,0},{4,5},{5,6},{6,7},{7,4},{8,9},{9,10},{10,1... | collective-permute-start | bytes 1179656 | tf_op jit(solution)/shard_map/ppermute | solution.py:357
  215.1 10.9 %collective-permute-start.24 = (bf16[512,384]{1,0:T(8,128)(2,1)}, bf16[512,384]{1,0:T(8,128)(2,1)S(1)}, u32[]{:S(2)}, u32[]{:S(2)}) collective-permute-start(bf16[512,384]{1,0:T(8,128)(2,1)} %after.11.own), channel_id=1, source_target_pairs={{0,3},{1,0},{2,1},{3,2},{4,7},{5,4},{6,5},{7,6},{8,11},{9,8},{10,9... | collective-permute-start | bytes 1179656 | tf_op jit(solution)/shard_map/ppermute | solution.py:358
  222.8 11.7 %collective-permute-start.21 = (bf16[512,384]{1,0:T(8,128)(2,1)}, bf16[512,384]{1,0:T(8,128)(2,1)S(1)}, u32[]{:S(2)}, u32[]{:S(2)}) collective-permute-start(bf16[512,384]{1,0:T(8,128)(2,1)} %far.3.own), channel_id=1, source_target_pairs={{0,1},{1,2},{2,3},{3,0},{4,5},{5,6},{6,7},{7,4},{8,9},{9,10},{10,1... | collective-permute-start | bytes 1179656 | tf_op jit(solution)/shard_map/ppermute | solution.py:357
  222.8 11.8 %collective-permute-start.20 = (bf16[512,384]{1,0:T(8,128)(2,1)}, bf16[512,384]{1,0:T(8,128)(2,1)S(1)}, u32[]{:S(2)}, u32[]{:S(2)}) collective-permute-start(bf16[512,384]{1,0:T(8,128)(2,1)} %far.3.own), channel_id=1, source_target_pairs={{0,3},{1,0},{2,1},{3,2},{4,7},{5,4},{6,5},{7,6},{8,11},{9,8},{10,9... | collective-permute-start | bytes 1179656 | tf_op jit(solution)/shard_map/ppermute | solution.py:358
  226.0 12.8 %copy-start.12 = (bf16[512,384]{1,0:T(8,128)(2,1)}, bf16[512,384]{1,0:T(8,128)(2,1)S(1)}, u32[]{:S(2)}) copy-start(bf16[512,384]{1,0:T(8,128)(2,1)S(1)} %collective-permute-done.25.left) | copy-start | bytes 1179652
  226.0 12.8 %collective-permute-start.26 = (bf16[256,384]{1,0:T(8,128)(2,1)S(1)}, bf16[256,384]{1,0:T(8,128)(2,1)S(1)}, u32[]{:S(2)}, u32[]{:S(2)}) collective-permute-start(bf16[256,384]{1,0:T(8,128)(2,1)S(1)} %slice.53), channel_id=1, source_target_pairs={{0,1},{1,2},{2,3},{3,0},{4,5},{5,6},{6,7},{7,4},{8,9},{9,10},{10,1... | collective-permute-start | bytes 589832 | tf_op jit(solution)/shard_map/ppermute | solution.py:362
  226.1 12.7 %copy-start.13 = (bf16[512,384]{1,0:T(8,128)(2,1)}, bf16[512,384]{1,0:T(8,128)(2,1)S(1)}, u32[]{:S(2)}) copy-start(bf16[512,384]{1,0:T(8,128)(2,1)S(1)} %collective-permute-done.24.right) | copy-start | bytes 1179652
  226.1 12.6 %collective-permute-start.27 = (bf16[256,384]{1,0:T(8,128)(2,1)S(1)}, bf16[256,384]{1,0:T(8,128)(2,1)S(1)}, u32[]{:S(2)}, u32[]{:S(2)}) collective-permute-start(bf16[256,384]{1,0:T(8,128)(2,1)S(1)} %slice.54), channel_id=1, source_target_pairs={{0,3},{1,0},{2,1},{3,2},{4,7},{5,4},{6,5},{7,6},{8,11},{9,8},{10,9... | collective-permute-start | bytes 589832 | tf_op jit(solution)/shard_map/ppermute | solution.py:362
  234.5 10.8 %copy-start.14 = (bf16[512,384]{1,0:T(8,128)(2,1)}, bf16[512,384]{1,0:T(8,128)(2,1)S(1)}, u32[]{:S(2)}) copy-start(bf16[512,384]{1,0:T(8,128)(2,1)S(1)} %collective-permute-done.21.left) | copy-start | bytes 1179652
  234.6 10.8 %collective-permute-start.22 = (bf16[256,384]{1,0:T(8,128)(2,1)S(1)}, bf16[256,384]{1,0:T(8,128)(2,1)S(1)}, u32[]{:S(2)}, u32[]{:S(2)}) collective-permute-start(bf16[256,384]{1,0:T(8,128)(2,1)S(1)} %slice.51), channel_id=1, source_target_pairs={{0,1},{1,2},{2,3},{3,0},{4,5},{5,6},{6,7},{7,4},{8,9},{9,10},{10,1... | collective-permute-start | bytes 589832 | tf_op jit(solution)/shard_map/ppermute | solution.py:362
  234.7 10.7 %copy-start.15 = (bf16[512,384]{1,0:T(8,128)(2,1)}, bf16[512,384]{1,0:T(8,128)(2,1)S(1)}, u32[]{:S(2)}) copy-start(bf16[512,384]{1,0:T(8,128)(2,1)S(1)} %collective-permute-done.20.right) | copy-start | bytes 1179652
  234.7 10.7 %collective-permute-start.23 = (bf16[256,384]{1,0:T(8,128)(2,1)S(1)}, bf16[256,384]{1,0:T(8,128)(2,1)S(1)}, u32[]{:S(2)}, u32[]{:S(2)}) collective-permute-start(bf16[256,384]{1,0:T(8,128)(2,1)S(1)} %slice.52), channel_id=1, source_target_pairs={{0,3},{1,0},{2,1},{3,2},{4,7},{5,4},{6,5},{7,6},{8,11},{9,8},{10,9... | collective-permute-start | bytes 589832 | tf_op jit(solution)/shard_map/ppermute | solution.py:362
  251.9 37.5 %copy-start.20 = (bf16[128,1024]{1,0:T(8,128)(2,1)S(1)}, bf16[128,1024]{1,0:T(8,128)(2,1)}, u32[]{:S(2)}) copy-start(bf16[128,1024]{1,0:T(8,128)(2,1)} %get-tuple-element.39) | copy-start | bytes 786436
  (18 other events, 17.9 us)
Sparse Core Ops, SparseCore 0:
  9.7 34.6 all-gather.2
